TPU v7x, 512 devices: a whole 4x8x8 slice. The times are simulated.
512 devices in a mesh: blk: 128 (over y, z, core), dp: 4 (over x).
Axes of the slice: x: 4, y: 8, z: 8, core: 2. Of those that a mesh axis runs over, the one named last changes fastest.
Arguments:
- hidden: bfloat16 [512, 32768], P('dp', 'blk'), may hold values from -6 to 6
- weights: bfloat16 [256, 26, 128, 256], P('blk'), may hold values from -0.109375 to 0.109375
- pattern: int32 [256, 26], replicated, may hold values from 0 to 255, as said below
- row_of_slot: int32 [256], replicated, may hold values from 0 to 255, as said below
- cotangent: bfloat16 [512, 32768], P('dp', 'blk'), may hold values from -6 to 6
Outputs:
- output: bfloat16 [512, 32768], P('dp', 'blk')
- input_grad: bfloat16 [512, 32768], P('dp', 'blk')
- weight_grad: bfloat16 [256, 26, 128, 256], P('blk', None, 'dp')
Inputs may be any that keep to these rules, and one draw needn't show every extreme that they name: `row_of_slot`: A permutation of the block indices. `pattern`: the 26 entries of a row differ. The 52 slots source[p, k] read by the rows of one device lie on 52 different devices (slot q lies on device q // 2), so a device reads exactly one block from each device it reads from.
All inputs are finite; a program needn't handle non-finite values.
Results may differ from a plain program's by a relative error of at most 0.017.
Values may be sent and summed in bfloat16 or wider, within the bound.
No kernel may reach another device: no remote copies, remote signals or barrier semaphores. Data moves between devices by JAX's collectives and lax.ppermute only.
A program may use at most 64 MiB of HBM per device.

v0:
```python
import math

import jax
import jax.numpy as jnp
from jax import lax
from jax.sharding import PartitionSpec as P


def source_slots(pattern, row_of_slot):
    total = row_of_slot.shape[0]
    slots = jnp.arange(total, dtype=jnp.int32)
    equal = (row_of_slot[None, None, :] == pattern[:, :, None]).astype(jnp.int32)
    return jnp.sum(equal * slots[None, None, :], axis=2)


def local(hidden, weights, pattern, row_of_slot, cotangent):
    rows_here = hidden.shape[0]
    owned = weights.shape[0]
    per_row = weights.shape[1]
    width = weights.shape[2]
    reads = owned * per_row
    devices = lax.axis_size("blk")
    myself = lax.axis_index("blk")
    sources = source_slots(pattern, row_of_slot)
    producers = sources // owned
    my_sources = lax.dynamic_slice_in_dim(sources, myself * owned, owned, 0).reshape(reads)
    my_producers = my_sources // owned
    serving = jnp.where(producers == myself, sources % owned + 1, 0)
    wanted = jnp.sum(serving.reshape(devices, reads), axis=1)
    picked = (wanted[:, None] == jnp.arange(1, owned + 1, dtype=jnp.int32)[None, :]).astype(
        jnp.bfloat16
    )
    piece = lax.all_gather(hidden, "blk", axis=1, tiled=True)
    count = piece.shape[1] // width
    hits = (my_sources[:, None] == jnp.arange(count, dtype=jnp.int32)[None, :]).astype(jnp.bfloat16)
    added = jnp.einsum(
        "mc,tcb->mtb",
        hits,
        piece.reshape(rows_here, count, width),
        preferred_element_type=jnp.float32,
    )
    held_blocks = added.astype(jnp.bfloat16)
    held_four = held_blocks.reshape(owned, per_row, rows_here, width)
    both = jnp.einsum("jktb,jkbo->jto", held_four, weights, preferred_element_type=jnp.float32)
    gate = both[:, :, :width]
    upper = both[:, :, width:]
    sigma = jax.nn.sigmoid(gate)
    result = (gate * sigma * upper).astype(jnp.bfloat16)
    output = jnp.transpose(result, (1, 0, 2)).reshape(rows_here, owned * width)
    gradf = jnp.transpose(cotangent.reshape(rows_here, owned, width), (1, 0, 2)).astype(jnp.float32)
    dgate = gradf * upper * sigma * (1.0 + gate * (1.0 - sigma))
    dup = gradf * gate * sigma
    dboth = jnp.concatenate([dgate, dup], axis=2).astype(jnp.bfloat16)
    partial_value = jnp.einsum(
        "jto,jkbo->jktb", dboth, weights, preferred_element_type=jnp.float32
    ).astype(jnp.bfloat16)
    partial_value = partial_value.reshape(reads, rows_here, width)
    route = (jnp.arange(devices, dtype=jnp.int32)[:, None] == my_producers[None, :]).astype(
        jnp.bfloat16
    )
    outgoing_grads = jnp.einsum(
        "rm,mtb->rtb", route, partial_value, preferred_element_type=jnp.float32
    ).astype(jnp.bfloat16)
    wgrad = jnp.einsum("jktb,jto->jkbo", held_four, dboth, preferred_element_type=jnp.float32)
    scale = 1.0 / math.sqrt(rows_here * lax.axis_size("dp"))
    returned = lax.all_to_all(outgoing_grads, "blk", split_axis=0, concat_axis=0, tiled=True)
    summed = jnp.einsum("rj,rtb->tjb", picked, returned, preferred_element_type=jnp.float32)
    input_grad = summed.reshape(rows_here, owned * width).astype(jnp.bfloat16)
    summed = lax.psum_scatter(
        wgrad.astype(jnp.bfloat16), "dp", scatter_dimension=2, tiled=True
    ).astype(jnp.float32)
    weight_grad = (summed * scale).astype(jnp.bfloat16)
    return (output, input_grad, weight_grad)


def solution(mesh):
    placed = (P("dp", "blk"), P("blk", None, None, None), P(), P(), P("dp", "blk"))
    return jax.shard_map(
        local,
        mesh=mesh,
        in_specs=placed,
        out_specs=(P("dp", "blk"), P("dp", "blk"), P("blk", None, "dp", None)),
        check_vma=False,
    )
```

profile of v0, /device:TPU:103, one launch (start us, length us, event | category | flops | bytes accessed | tf_op | source)
XLA Modules:
  0.0 257.6 jit_solution(14925141314497352998)
XLA Ops:
  7.2 0.7 all-gather.2.cloned.1.call-update
  7.9 3.4 %select_reduce_fusion = s32[256,26]{0,1:T(8,128)S(1)} fusion(s32[256,26]{0,1:T(8,128)} %param.7, s32[256]{0:T(256)} %param.8), kind=kLoop, calls=%fused_computation | loop fusion | flops 5105152 | bytes 54272 | tf_op jit(solution)/shard_map/reduce_sum | solution.py:13
  11.3 0.6 copy-done.4
  12.2 0.9 copy.31
  13.1 0.8 copy.32
  13.9 91.9 %all-gather.2.cloned.1.call-done = bf16[128,32768]{1,0:T(8,128)(2,1)} async-done(((bf16[128,256]{1,0:T(8,128)(2,1)}), bf16[128,32768]{1,0:T(8,128)(2,1)}) %all-gather.2.cloned.1.call-update) | async-done | bytes 8388624 | tf_op jit(solution)/shard_map/all_gather | solution.py:33
  105.8 9.1 %copy.43 = bf16[16,8,256,128]{3,2,1,0:T(8,128)(2,1)} copy(bf16[16,8,256,128]{3,1,2,0:T(8,128)(2,1)} %bitcast.57) | data formatting | bytes 16777216
  114.9 5.0 %convolution_convert_fusion.2 = bf16[52,128,128]{2,0,1:T(8,128)(2,1)S(1)} fusion(bf16[128,256,128]{2,1,0:T(8,128)(2,1)} %bitcast.54, s32[52]{0:T(128)S(1)} %eq.67), kind=kOutput, calls=%fused_computation.6 | convolution fusion | flops 437072896 | bytes 10092752 | tf_op jit(solution)/shard_map/mc,tcb->mtb/dot_general | solution.py:36
  119.9 0.4 copy.29
  120.3 1.3 copy-done.1
  121.6 0.7 convolution_bitcast_fusion
  122.3 0.7 fusion.8
  123.0 1.2 convolution_convert_fusion.3
  124.2 1.8 convolution_convert_fusion
  126.1 4.7 %copy.34 = bf16[128,128,128]{2,1,0:T(8,128)(2,1)} copy(bf16[128,128,128]{2,0,1:T(8,128)(2,1)S(1)} %convolution_convert_fusion) | data formatting | bytes 8388608 | tf_op jit(solution)/shard_map/convert_element_type | solution.py:63
  130.8 12.0 %all-to-all-start = ((bf16[128,128,128]{2,1,0:T(8,128)(2,1)}), bf16[128,128,128]{2,1,0:T(8,128)(2,1)}, u32[]{:S(2)}, u32[]{:S(2)}) async-start(bf16[128,128,128]{2,1,0:T(8,128)(2,1)} %copy.34), calls=%async_computation | async-start | bytes 8388608 | tf_op jit(solution)/shard_map/all_to_all | solution.py:66
  143.0 4.3 %convolution_convert_fusion.1 = bf16[2,26,128,256]{3,2,1,0:T(8,128)(2,1)} fusion(bf16[2,26,128,128]{3,2,1,0:T(8,128)(2,1)} %bitcast.56, bf16[2,128,128]{2,1,0:T(8,128)(2,1)S(1)} %get-tuple-element.13, bf16[2,128,128]{2,1,0:T(8,128)(2,1)S(1)} %get-tuple-element.12), kind=kOutput, calls=%fused_computation.4 | convolution fusion | flops 438173696 | bytes 5242880 | tf_op jit(solution)/shard_map/jktb,jto->jkbo/dot_general | solution.py:64
  147.4 0.7 copy-done.5
  148.6 0.7 copy.37
  149.3 42.6 %reduce-scatter.2.cloned.1.call-done = bf16[2,26,32,256]{3,2,1,0:T(8,128)(2,1)} async-done(((bf16[2,26,128,256]{3,2,1,0:T(8,128)(2,1)}), bf16[2,26,32,256]{3,2,1,0:T(8,128)(2,1)}) %reduce-scatter.2.cloned.1.call-update) | async-done | bytes 851984 | tf_op jit(solution)/shard_map/reduce_scatter | solution.py:69
  192.0 2.3 multiply_convert_fusion
  194.2 51.4 %all-to-all-done = bf16[128,128,128]{2,1,0:T(8,128)(2,1)} async-done(((bf16[128,128,128]{2,1,0:T(8,128)(2,1)}), bf16[128,128,128]{2,1,0:T(8,128)(2,1)}, u32[]{:S(2)}, u32[]{:S(2)}) %all-to-all-start) | async-done | bytes 4194336 | tf_op jit(solution)/shard_map/all_to_all | solution.py:66
  245.6 4.5 %fusion.3 = bf16[128,128,2]{1,2,0:T(2,128)(2,1)S(1)} fusion(bf16[128,128,128]{2,1,0:T(8,128)(2,1)} %all-to-all-done, s32[128]{0:T(128)S(1)} %reduce_sum.28, s32[2]{0:T(128)S(1)} %iota_add_fusion), kind=kOutput, calls=%fused_computation.10 | convolution fusion | flops 8421632 | bytes 4260360 | tf_op jit(solution)/shard_map/rj,rtb->tjb/dot_general | solution.py:67
  250.1 0.6 copy.52
  (21 shorter events, 1.0 us)
Async XLA Ops:
  7.2 114.4 %copy-start = (bf16[2,26,128,256]{3,2,1,0:T(8,128)(2,1)S(1)}, bf16[2,26,128,256]{3,2,1,0:T(8,128)(2,1)}, u32[]{:S(2)}) copy-start(bf16[2,26,128,256]{3,2,1,0:T(8,128)(2,1)} %param.6) | copy-start | bytes 10223620
  7.2 98.6 %all-gather.2.cloned.1.call-start = ((), (), s32[]{:S(2)}) async-start(), calls=%async_computation.2 | async-start | bytes 8454144 | tf_op jit(solution)/shard_map/all_gather | solution.py:33
  11.3 0.6 copy-start.4
  120.3 1.3 copy-start.1
  120.3 2.0 copy-start.2
  130.8 114.8 %all-to-all-start = ((bf16[128,128,128]{2,1,0:T(8,128)(2,1)}), bf16[128,128,128]{2,1,0:T(8,128)(2,1)}, u32[]{:S(2)}, u32[]{:S(2)}) async-start(bf16[128,128,128]{2,1,0:T(8,128)(2,1)} %copy.34), calls=%async_computation | async-start | bytes 8388608 | tf_op jit(solution)/shard_map/all_to_all | solution.py:66
  142.8 49.2 %reduce-scatter.2.cloned.1.call-start = ((), (), s32[]{:S(2)}) async-start(), calls=%async_computation.3 | async-start | bytes 4259840 | tf_op jit(solution)/shard_map/reduce_scatter | solution.py:69
  147.4 0.8 copy-start.5
  147.4 1.1 copy-start.3
Sparse Core Ops, SparseCore 0:
  11.1 94.6 all-gather.1
  147.5 44.4 reduce-scatter.1
where the time goes:
time: 258 us
  waiting for transfers between devices  187 us (72%)
  local copies, waits for them, and re-layouts  20.4 us (8%)
  matrix products  17.6 us (7%)
  between operations  14.2 us (6%)
  starting transfers between devices  12.3 us (5%)
  other arithmetic  6.55 us (3%)
    all_gather x1, waiting for transfers between devices, local(): piece = lax.all_gather(hidden, 'blk', axis=1, tiled=True)  91.9 us
    all_to_all x1, waiting for transfers between devices, local(): lax.all_to_all(outgoing_grads, 'blk', split_axis=0, concat_axis=0, tiled=...  51.4 us
    reduce_scatter x1, waiting for transfers between devices, local(): lax.psum_scatter(wgrad.astype(jnp.bfloat16), 'dp', scatter_dimension=2, t...  42.6 us
    unnamed x16, local copies, waits for them, and re-layouts  14.1 us
    all_to_all x1, starting transfers between devices, local(): lax.all_to_all(outgoing_grads, 'blk', split_axis=0, concat_axis=0, tiled=...  12 us
  transfers between devices with their start and end apart: 3, of which 3 were waited for; matrix products, arithmetic and copies ran while one was open for 5% of the time, Pallas kernels for 0%

commit v1 on v0

v1 whole, which is shorter than its diff:
```python
import math

import jax
import jax.numpy as jnp
from jax import lax
from jax.experimental import pallas as pl
from jax.experimental.pallas import tpu as pltpu
from jax.sharding import PartitionSpec as P

BF = jnp.bfloat16
F32 = jnp.float32
SIDE = 8


def device_at(y, z, core):
    return (y * SIDE + z) * 2 + core


GROUPS_NEAR = [[device_at(y, z, 0) for y in range(SIDE)] for z in range(SIDE)] + [
    [device_at(y, z, 1) for z in range(SIDE)] for y in range(SIDE)
]
GROUPS_FAR = [[device_at(y, z, 0) for z in range(SIDE)] for y in range(SIDE)] + [
    [device_at(y, z, 1) for y in range(SIDE)] for z in range(SIDE)
]
SWAP = [(i, i ^ 1) for i in range(2 * SIDE * SIDE)]


def swap_cores(value):
    return lax.ppermute(value, "blk", SWAP)


def exchange(value, groups):
    return lax.all_to_all(value, "blk", 0, 0, axis_index_groups=groups, tiled=True)


def block_kernel(idx, gathered, weights, turned, grads, out, kept, dense):
    row = pl.program_id(0)
    blocks = weights.shape[1] // 128
    flat = blocks * 128

    @pl.when(row == 0)
    def _():
        dense[...] = jnp.zeros_like(dense)

    for k in range(blocks):
        kept[0, :, k * 128 : (k + 1) * 128] = gathered[idx[row * blocks + k]]
    both = jnp.dot(kept[0, :, :flat], weights[0], preferred_element_type=F32)
    gate = both[:, :128]
    upper = both[:, 128:]
    sigma = jax.nn.sigmoid(gate)
    out[0] = (gate * sigma * upper).astype(BF)
    gradf = grads[0].astype(F32)
    dgate = gradf * upper * sigma * (1.0 + gate * (1.0 - sigma))
    dup = gradf * gate * sigma
    dboth = jnp.concatenate([dgate, dup], axis=1).astype(BF)
    kept[0, :, flat:] = dboth
    partial = jnp.dot(dboth, turned[0], preferred_element_type=F32).astype(BF)
    for k in range(blocks):
        at = idx[row * blocks + k]
        total = dense[at].astype(F32) + partial[:, k * 128 : (k + 1) * 128].astype(F32)
        dense[at] = total.astype(BF)


def run_blocks(idx, gathered, weights, turned, grads):
    rows, flat = weights.shape[:2]
    tokens = grads.shape[1]
    return pl.pallas_call(
        block_kernel,
        grid_spec=pltpu.PrefetchScalarGridSpec(
            num_scalar_prefetch=1,
            grid=(rows,),
            in_specs=[
                pl.BlockSpec(gathered.shape, lambda r, i: (0, 0, 0)),
                pl.BlockSpec((1, flat, 256), lambda r, i: (r, 0, 0)),
                pl.BlockSpec((1, 256, flat), lambda r, i: (r, 0, 0)),
                pl.BlockSpec((1, tokens, 128), lambda r, i: (r, 0, 0)),
            ],
            out_specs=[
                pl.BlockSpec((1, tokens, 128), lambda r, i: (r, 0, 0)),
                pl.BlockSpec((1, tokens, flat + 256), lambda r, i: (r, 0, 0)),
                pl.BlockSpec(gathered.shape, lambda r, i: (0, 0, 0)),
            ],
        ),
        out_shape=[
            jax.ShapeDtypeStruct((rows, tokens, 128), BF),
            jax.ShapeDtypeStruct((rows, tokens, flat + 256), BF),
            jax.ShapeDtypeStruct(gathered.shape, BF),
        ],
        compiler_params=pltpu.CompilerParams(
            dimension_semantics=("arbitrary",), vmem_limit_bytes=44 * 1024 * 1024
        ),
        cost_estimate=pl.CostEstimate(
            flops=4 * rows * tokens * flat * 256,
            bytes_accessed=4 * rows * flat * 256 + 4 * gathered.size,
            transcendentals=rows * tokens * 128,
        ),
    )(idx, gathered, weights, turned, grads)


def local(hidden, weights, pattern, row_of_slot, cotangent):
    tokens = hidden.shape[0]
    half = tokens // 2
    owned, per_row, width = weights.shape[:3]
    flat = per_row * width
    me = lax.axis_index("blk")
    core = me % 2
    other = me + 1 - 2 * core
    first = core == 0

    def of_core(value, which):
        return lax.dynamic_slice_in_dim(value, which * half, half, 0)

    def split(value):
        return jnp.transpose(value.reshape(half, owned, width), (1, 0, 2))

    with jax.named_scope("swap_tokens"):
        sent = jnp.stack([of_core(hidden, 1 - core), of_core(cotangent, 1 - core)])
        came = swap_cores(sent)
        mine, theirs = split(of_core(hidden, core)), split(came[0])
        chip_blocks = jnp.where(
            first, jnp.concatenate([mine, theirs]), jnp.concatenate([theirs, mine])
        )
        grads = jnp.concatenate([split(of_core(cotangent, core)), split(came[1])])
    with jax.named_scope("gather_near"):
        near = exchange(
            jnp.broadcast_to(chip_blocks[None], (SIDE,) + chip_blocks.shape), GROUPS_NEAR
        )
    with jax.named_scope("gather_far"):
        gathered = lax.all_gather(near, "blk", axis_index_groups=GROUPS_FAR, tiled=True)
        gathered = gathered.reshape(SIDE * SIDE * 2 * owned, half, width)
    with jax.named_scope("swap_weights"):
        partner = swap_cores(weights)
        all_weights = jnp.concatenate([weights, partner]).reshape(2 * owned, flat, 2 * width)
        turned = jnp.transpose(all_weights, (0, 2, 1))
    with jax.named_scope("sources"):
        wanted = jnp.concatenate(
            [
                lax.dynamic_slice_in_dim(pattern, me * owned, owned, 0),
                lax.dynamic_slice_in_dim(pattern, other * owned, owned, 0),
            ]
        )
        slots = jnp.arange(row_of_slot.shape[0], dtype=jnp.int32)
        equal = row_of_slot[None, None, :] == wanted[:, :, None]
        source = jnp.sum(jnp.where(equal, slots[None, None, :], 0), axis=2)
        chip, inside = source // (2 * owned), source % (2 * owned)
        chip_y, chip_z = chip // SIDE, chip % SIDE
        place = jnp.where(first, chip_z * SIDE + chip_y, chip_y * SIDE + chip_z)
        idx = (place * (2 * owned) + inside).reshape(-1)

    with jax.named_scope("blocks"):
        result, kept, dense = run_blocks(idx, gathered, all_weights, turned, grads)

    def rejoin(keep, came):
        low = jnp.where(first, keep, came)
        high = jnp.where(first, came, keep)
        whole = jnp.stack([low, high])
        return jnp.transpose(whole, (0, 2, 1, 3)).reshape(tokens, owned * width)

    with jax.named_scope("weight_terms"):
        came = swap_cores(kept[owned:])
        both_halves = jnp.stack([kept[:owned], came])
        terms = jnp.einsum(
            "hjtb,hjto->jbo",
            both_halves[..., :flat],
            both_halves[..., flat:],
            preferred_element_type=F32,
        ).astype(BF)
        summed = lax.psum_scatter(
            terms.reshape(owned, per_row, width, 2 * width), "dp", scatter_dimension=2, tiled=True
        )
        scale = 1.0 / math.sqrt(tokens * lax.axis_size("dp"))
        weight_grad = (summed.astype(F32) * scale).astype(BF)

    with jax.named_scope("reduce_far"):
        pieces = exchange(dense.reshape(SIDE, SIDE * 2 * owned * half, width), GROUPS_FAR)
        column = jnp.sum(pieces.astype(F32), axis=0).astype(BF)
    with jax.named_scope("reduce_near"):
        pieces = exchange(column.reshape(SIDE, 2 * owned * half, width), GROUPS_NEAR)
        total = jnp.sum(pieces.astype(F32), axis=0).astype(BF)
        total = total.reshape(2, owned, half, width)
    with jax.named_scope("swap_back"):
        keep = jnp.where(first, total[0], total[1])
        came = swap_cores(jnp.where(first, total[1], total[0]))
        input_grad = rejoin(keep, came)
        output = rejoin(result[:owned], swap_cores(result[owned:]))
    return (output, input_grad, weight_grad)


def solution(mesh):
    placed = (P("dp", "blk"), P("blk", None, None, None), P(), P(), P("dp", "blk"))
    return jax.shard_map(
        local,
        mesh=mesh,
        in_specs=placed,
        out_specs=(P("dp", "blk"), P("dp", "blk"), P("blk", None, "dp", None)),
        check_vma=False,
    )
```

time: 258 us -> 187 us (0.72)
  the two profiles are of different devices: /device:TPU:103 before, /device:TPU:1 now
where the time goes in v1:
time: 187 us; the launch traced here: 186 us
  waiting for transfers between devices  64.9 us (35%)
  starting transfers between devices  45.7 us (24%)
  local copies, waits for them, and re-layouts  18.7 us (10%)
  blocking collectives  16.7 us (9%)
  between operations  14.3 us (8%)
  other arithmetic  14 us (7%)
  Pallas kernels  8.84 us (5%)
  matrix products  2.86 us (2%)
    all_to_all x2, waiting for transfers between devices, exchange(): lax.all_to_all(value, 'blk', 0, 0, axis_index_groups=groups, tiled=True)  44.3 us
    ppermute x5, starting transfers between devices, swap_cores(): return lax.ppermute(value, 'blk', SWAP)  34.1 us
    all_to_all x1, blocking collectives, exchange(): lax.all_to_all(value, 'blk', 0, 0, axis_index_groups=groups, tiled=True)  16.7 us
    all_gather x1, waiting for transfers between devices, local(): lax.all_gather(near, 'blk', axis_index_groups=GROUPS_FAR, tiled=True)  13.9 us
    all_to_all x2, starting transfers between devices, exchange(): lax.all_to_all(value, 'blk', 0, 0, axis_index_groups=groups, tiled=True)  11.5 us
    reshape x1, local copies, waits for them, and re-layouts, local(): jnp.concatenate([weights, partner]).reshape(2 * owned, flat, 2 * width)  9.91 us
    pallas_call x1, Pallas kernels, run_blocks(): pl.pallas_call(block_kernel, grid_spec=pltpu.PrefetchScalarGridSpec(num_s...  8.84 us
    ppermute x5, waiting for transfers between devices, swap_cores(): return lax.ppermute(value, 'blk', SWAP)  6.57 us
  transfers between devices with their start and end apart: 9, of which 6 were waited for; matrix products, arithmetic and copies ran while one was open for 15% of the time, Pallas kernels for 0%

profile of v1, /device:TPU:1, one launch (start us, length us, event | category | flops | bytes accessed | tf_op | source)
XLA Modules:
  0.0 185.9 jit_solution(13195550795927960892)
XLA Ops:
  8.8 8.8 %collective-permute-start = (bf16[2,64,256]{2,1,0:T(8,128)(2,1)S(1)}, bf16[2,64,256]{2,1,0:T(8,128)(2,1)S(1)}, u32[]{:S(2)}, u32[]{:S(2)}) collective-permute-start(bf16[2,64,256]{2,1,0:T(8,128)(2,1)S(1)} %pad_maximum_fusion.3), channel_id=1, source_target_pairs={{0,4},{4,0},{8,12},{12,8},{16,20},{20,16},{24,28},{28,24},{32,36},... | collective-permute-start | bytes 196616 | tf_op jit(solution)/shard_map/swap_tokens/ppermute | solution.py:29
  17.6 0.9 collective-permute-done
  18.8 16.7 %all_to_all.15 = bf16[8,4,64,128]{3,2,1,0:T(8,128)(2,1)} all-to-all(bf16[8,4,64,128]{3,2,1,0:T(8,128)(2,1)S(1)} %broadcast_in_dim.23), channel_id=1, replica_groups={{0,64,128,192,256,320,384,448},{8,72,136,200,264,328,392,456},{16,80,14..., dimensions={0} | all-to-all | bytes 1048576 | tf_op jit(solution)/shard_map/gather_near/all_to_all | solution.py:33
  35.5 1.9 %collective-permute-start.1 = (bf16[2,26,128,256]{3,2,1,0:T(8,128)(2,1)}, bf16[2,26,128,256]{3,2,1,0:T(8,128)(2,1)}, u32[]{:S(2)}, u32[]{:S(2)}) collective-permute-start(bf16[2,26,128,256]{3,2,1,0:T(8,128)(2,1)} %param.6), channel_id=1, source_target_pairs={{0,4},{4,0},{8,12},{12,8},{16,20},{20,16},{24,28},{28,24},{32,36},... | collective-permute-start | bytes 10223624 | tf_op jit(solution)/shard_map/swap_weights/ppermute | solution.py:29
  37.5 0.9 constant_dynamic-slice_fusion.2
  38.6 1.3 select_reduce_fusion
  40.1 3.6 %collective-permute-done.1 = bf16[2,26,128,256]{3,2,1,0:T(8,128)(2,1)} collective-permute-done((bf16[2,26,128,256]{3,2,1,0:T(8,128)(2,1)}, bf16[2,26,128,256]{3,2,1,0:T(8,128)(2,1)}, u32[]{:S(2)}, u32[]{:S(2)}) %collective-permute-start.1) | collective-permute-done | bytes 3407904 | tf_op jit(solution)/shard_map/swap_weights/ppermute | solution.py:29
  43.8 6.4 %pad_maximum_fusion = bf16[4,26,128,256]{3,2,1,0:T(8,128)(2,1)} fusion(bf16[2,26,128,256]{3,2,1,0:T(8,128)(2,1)} %collective-permute-done.1, bf16[2,26,128,256]{3,2,1,0:T(8,128)(2,1)} %param.6), kind=kLoop, calls=%fused_computation | loop fusion | flops 3407872 | bytes 13631488 | tf_op jit(solution)/shard_map/swap_weights/concatenate | solution.py:133
  50.2 9.9 %copy.35 = bf16[4,3328,256]{1,2,0:T(8,128)(2,1)} copy(bf16[4,3328,256]{2,1,0:T(8,128)(2,1)} %bitcast.54) | data formatting | bytes 13631488 | tf_op jit(solution)/shard_map/swap_weights/reshape | solution.py:133
  60.1 13.9 %all-gather.2.cloned.1.call-done = bf16[64,4,64,128]{3,2,1,0:T(8,128)(2,1)} async-done(((bf16[8,4,64,128]{3,2,1,0:T(8,128)(2,1)}), bf16[64,4,64,128]{3,2,1,0:T(8,128)(2,1)}) %all-gather.2.cloned.1.call-update) | async-done | bytes 4194320 | tf_op jit(solution)/shard_map/gather_far/all_gather | solution.py:129
  74.1 2.2 %copy-done.1 = bf16[64,4,64,128]{3,2,1,0:T(8,128)(2,1)S(1)} copy-done((bf16[64,4,64,128]{3,2,1,0:T(8,128)(2,1)S(1)}, bf16[64,4,64,128]{3,2,1,0:T(8,128)(2,1)}, u32[]{:S(2)}) %copy-start.1) | copy-done | bytes 4194328
  76.2 8.8 %blocks.1 = (bf16[4,64,128]{2,1,0:T(8,128)(2,1)S(1)}, bf16[4,64,3584]{2,1,0:T(8,128)(2,1)S(1)}, bf16[256,64,128]{2,1,0:T(8,128)(2,1)S(1)}) custom-call(s32[104]{0:T(128)S(1)} %fusion.3.idx, bf16[256,64,128]{2,1,0:T(8,128)(2,1)S(1)} %bitcast.53, bf16[4,3328,256]{2,1,0:T(8,128)(2,1)} %bitcast.55, bf16[4,256,3328]{2,1,0:T(8,128)(2,1)} %bitcast.56, ...), custom_call_target="tpu_custom_call" | custom-call | flops 872415232 | bytes 22020096 | tf_op jit(solution)/shard_map/blocks/pallas_call | solution.py:67
  85.1 2.0 %copy-done = bf16[256,64,128]{2,1,0:T(8,128)(2,1)} copy-done((bf16[256,64,128]{2,1,0:T(8,128)(2,1)}, bf16[256,64,128]{2,1,0:T(8,128)(2,1)S(1)}, u32[]{:S(2)}) %copy-start) | copy-done | bytes 4194328
  87.1 4.6 %all-to-all-start.1 = ((bf16[8,2048,128]{2,1,0:T(8,128)(2,1)}), bf16[8,2048,128]{2,1,0:T(8,128)(2,1)}, u32[]{:S(2)}, u32[]{:S(2)}) async-start(bf16[8,2048,128]{2,1,0:T(8,128)(2,1)} %bitcast.52), calls=%async_computation.1 | async-start | bytes 8388608 | tf_op jit(solution)/shard_map/reduce_far/all_to_all | solution.py:33
  91.8 6.9 %collective-permute-start.4 = (bf16[2,64,3584]{2,1,0:T(8,128)(2,1)S(1)}, bf16[2,64,3584]{2,1,0:T(8,128)(2,1)S(1)}, u32[]{:S(2)}, u32[]{:S(2)}) collective-permute-start(bf16[2,64,3584]{2,1,0:T(8,128)(2,1)S(1)} %get-tuple-element.9), channel_id=1, source_target_pairs={{0,4},{4,0},{8,12},{12,8},{16,20},{20,16},{24,28},{28,24},{32,36},... | collective-permute-start | bytes 2752520 | tf_op jit(solution)/shard_map/weight_terms/ppermute | solution.py:29
  98.7 2.1 %collective-permute-done.4 = bf16[2,64,3584]{2,1,0:T(8,128)(2,1)S(1)} collective-permute-done((bf16[2,64,3584]{2,1,0:T(8,128)(2,1)S(1)}, bf16[2,64,3584]{2,1,0:T(8,128)(2,1)S(1)}, u32[]{:S(2)}, u32[]{:S(2)}) %collective-permute-start.4) | collective-permute-done | bytes 917536 | tf_op jit(solution)/shard_map/weight_terms/ppermute | solution.py:29
  100.8 2.9 %bitcast_convert_fusion = bf16[2,3328,256]{2,1,0:T(8,128)(2,1)} fusion(bf16[1,2,64,3584]{3,2,1,0:T(8,128)(2,1)S(1)} %get-tuple-element.10, bf16[1,2,64,3584]{3,2,1,0:T(8,128)(2,1)S(1)} %bitcast.58), kind=kOutput, calls=%fused_computation.1 | convolution fusion | flops 439025664 | bytes 7077888 | tf_op jit(solution)/shard_map/weight_terms/hjtb,hjto->jbo/dot_general | solution.py:162
  103.7 39.8 %all-to-all-done.1 = bf16[8,2048,128]{2,1,0:T(8,128)(2,1)} async-done(((bf16[8,2048,128]{2,1,0:T(8,128)(2,1)}), bf16[8,2048,128]{2,1,0:T(8,128)(2,1)}, u32[]{:S(2)}, u32[]{:S(2)}) %all-to-all-start.1) | async-done | bytes 4194336 | tf_op jit(solution)/shard_map/reduce_far/all_to_all | solution.py:33
  143.5 3.7 %reduce_sum.37 = bf16[2048,128]{1,0:T(8,128)(2,1)} reduce(bf16[8,2048,128]{2,1,0:T(8,128)(2,1)} %all-to-all-done.1, bf16[]{:T(256)} %constant.77.clone.1), dimensions={0}, to_apply=%region_1.2 | reduce | flops 1835008 | bytes 4718594 | tf_op jit(solution)/shard_map/reduce_far/reduce_sum | solution.py:176
  147.2 7.0 %all-to-all-start.2 = ((bf16[8,256,128]{2,1,0:T(8,128)(2,1)}), bf16[8,256,128]{2,1,0:T(8,128)(2,1)S(1)}, u32[]{:S(2)}, u32[]{:S(2)}) async-start(bf16[8,256,128]{2,1,0:T(8,128)(2,1)} %bitcast.13), calls=%async_computation.2 | async-start | bytes 1048576 | tf_op jit(solution)/shard_map/reduce_near/all_to_all | solution.py:33
  154.2 7.7 %collective-permute-start.2 = (bf16[2,64,128]{2,1,0:T(8,128)(2,1)S(1)}, bf16[2,64,128]{2,1,0:T(8,128)(2,1)S(1)}, u32[]{:S(2)}, u32[]{:S(2)}) collective-permute-start(bf16[2,64,128]{2,1,0:T(8,128)(2,1)S(1)} %slice.37), channel_id=1, source_target_pairs={{0,4},{4,0},{8,12},{12,8},{16,20},{20,16},{24,28},{28,24},{32,36},... | collective-permute-start | bytes 98312 | tf_op jit(solution)/shard_map/swap_back/ppermute | solution.py:29
  161.9 4.5 %all-to-all-done.2 = bf16[8,256,128]{2,1,0:T(8,128)(2,1)S(1)} async-done(((bf16[8,256,128]{2,1,0:T(8,128)(2,1)}), bf16[8,256,128]{2,1,0:T(8,128)(2,1)S(1)}, u32[]{:S(2)}, u32[]{:S(2)}) %all-to-all-start.2) | async-done | bytes 524320 | tf_op jit(solution)/shard_map/reduce_near/all_to_all | solution.py:33
  166.5 8.8 %collective-permute-start.3 = (bf16[2,64,128]{2,1,0:T(8,128)(2,1)S(1)}, bf16[2,64,128]{2,1,0:T(8,128)(2,1)S(1)}, u32[]{:S(2)}, u32[]{:S(2)}) collective-permute-start(bf16[2,64,128]{2,1,0:T(8,128)(2,1)S(1)} %bitcast.68), channel_id=1, source_target_pairs={{0,4},{4,0},{8,12},{12,8},{16,20},{20,16},{24,28},{28,24},{32,36},... | collective-permute-start | bytes 98312 | tf_op jit(solution)/shard_map/swap_back/ppermute | solution.py:29
  175.3 2.3 %multiply_convert_fusion = bf16[2,26,32,256]{3,2,1,0:T(8,128)(2,1)} fusion(bf16[2,26,32,256]{3,2,1,0:T(8,128)(2,1)} %reduce-scatter.2.cloned.1.call-done), kind=kLoop, calls=%fused_computation.5 | loop fusion | flops 1277952 | bytes 1703936 | tf_op jit(solution)/shard_map/weight_terms/convert_element_type | solution.py:172
  (40 shorter events, 4.2 us)
Async XLA Ops:
  7.2 66.9 %all-gather.2.cloned.1.call-start = ((), (), s32[]{:S(2)}) async-start(), calls=%async_computation.4 | async-start | bytes 4718592 | tf_op jit(solution)/shard_map/gather_far/all_gather | solution.py:129
  8.8 9.7 %collective-permute-start = (bf16[2,64,256]{2,1,0:T(8,128)(2,1)S(1)}, bf16[2,64,256]{2,1,0:T(8,128)(2,1)S(1)}, u32[]{:S(2)}, u32[]{:S(2)}) collective-permute-start(bf16[2,64,256]{2,1,0:T(8,128)(2,1)S(1)} %pad_maximum_fusion.3), channel_id=1, source_target_pairs={{0,4},{4,0},{8,12},{12,8},{16,20},{20,16},{24,28},{28,24},{32,36},... | collective-permute-start | bytes 196616 | tf_op jit(solution)/shard_map/swap_tokens/ppermute | solution.py:29
  35.5 8.3 %collective-permute-start.1 = (bf16[2,26,128,256]{3,2,1,0:T(8,128)(2,1)}, bf16[2,26,128,256]{3,2,1,0:T(8,128)(2,1)}, u32[]{:S(2)}, u32[]{:S(2)}) collective-permute-start(bf16[2,26,128,256]{3,2,1,0:T(8,128)(2,1)} %param.6), channel_id=1, source_target_pairs={{0,4},{4,0},{8,12},{12,8},{16,20},{20,16},{24,28},{28,24},{32,36},... | collective-permute-start | bytes 10223624 | tf_op jit(solution)/shard_map/swap_weights/ppermute | solution.py:29
  74.1 2.2 %copy-start.1 = (bf16[64,4,64,128]{3,2,1,0:T(8,128)(2,1)S(1)}, bf16[64,4,64,128]{3,2,1,0:T(8,128)(2,1)}, u32[]{:S(2)}) copy-start(bf16[64,4,64,128]{3,2,1,0:T(8,128)(2,1)} %all-gather.2.cloned.1.call-done) | copy-start | bytes 12582916
  85.1 2.0 %copy-start = (bf16[256,64,128]{2,1,0:T(8,128)(2,1)}, bf16[256,64,128]{2,1,0:T(8,128)(2,1)S(1)}, u32[]{:S(2)}) copy-start(bf16[256,64,128]{2,1,0:T(8,128)(2,1)S(1)} %get-tuple-element.7) | copy-start | bytes 12582916
  87.1 56.5 %all-to-all-start.1 = ((bf16[8,2048,128]{2,1,0:T(8,128)(2,1)}), bf16[8,2048,128]{2,1,0:T(8,128)(2,1)}, u32[]{:S(2)}, u32[]{:S(2)}) async-start(bf16[8,2048,128]{2,1,0:T(8,128)(2,1)} %bitcast.52), calls=%async_computation.1 | async-start | bytes 8388608 | tf_op jit(solution)/shard_map/reduce_far/all_to_all | solution.py:33
  91.6 83.7 %reduce-scatter.2.cloned.1.call-start = ((), (), s32[]{:S(2)}) async-start(), calls=%async_computation.5 | async-start | bytes 4259840 | tf_op jit(solution)/shard_map/weight_terms/reduce_scatter | solution.py:168
  91.8 9.0 %collective-permute-start.4 = (bf16[2,64,3584]{2,1,0:T(8,128)(2,1)S(1)}, bf16[2,64,3584]{2,1,0:T(8,128)(2,1)S(1)}, u32[]{:S(2)}, u32[]{:S(2)}) collective-permute-start(bf16[2,64,3584]{2,1,0:T(8,128)(2,1)S(1)} %get-tuple-element.9), channel_id=1, source_target_pairs={{0,4},{4,0},{8,12},{12,8},{16,20},{20,16},{24,28},{28,24},{32,36},... | collective-permute-start | bytes 2752520 | tf_op jit(solution)/shard_map/weight_terms/ppermute | solution.py:29
  147.2 19.1 %all-to-all-start.2 = ((bf16[8,256,128]{2,1,0:T(8,128)(2,1)}), bf16[8,256,128]{2,1,0:T(8,128)(2,1)S(1)}, u32[]{:S(2)}, u32[]{:S(2)}) async-start(bf16[8,256,128]{2,1,0:T(8,128)(2,1)} %bitcast.13), calls=%async_computation.2 | async-start | bytes 1048576 | tf_op jit(solution)/shard_map/reduce_near/all_to_all | solution.py:33
  154.2 23.4 %collective-permute-start.2 = (bf16[2,64,128]{2,1,0:T(8,128)(2,1)S(1)}, bf16[2,64,128]{2,1,0:T(8,128)(2,1)S(1)}, u32[]{:S(2)}, u32[]{:S(2)}) collective-permute-start(bf16[2,64,128]{2,1,0:T(8,128)(2,1)S(1)} %slice.37), channel_id=1, source_target_pairs={{0,4},{4,0},{8,12},{12,8},{16,20},{20,16},{24,28},{28,24},{32,36},... | collective-permute-start | bytes 98312 | tf_op jit(solution)/shard_map/swap_back/ppermute | solution.py:29
  166.5 11.1 %collective-permute-start.3 = (bf16[2,64,128]{2,1,0:T(8,128)(2,1)S(1)}, bf16[2,64,128]{2,1,0:T(8,128)(2,1)S(1)}, u32[]{:S(2)}, u32[]{:S(2)}) collective-permute-start(bf16[2,64,128]{2,1,0:T(8,128)(2,1)S(1)} %bitcast.68), channel_id=1, source_target_pairs={{0,4},{4,0},{8,12},{12,8},{16,20},{20,16},{24,28},{28,24},{32,36},... | collective-permute-start | bytes 98312 | tf_op jit(solution)/shard_map/swap_back/ppermute | solution.py:29
Sparse Core Ops, SparseCore 0:
  35.6 38.3 all-gather.1
  103.8 46.4 reduce-scatter.1

commit v2 on v1

v2 whole, which is shorter than its diff:
```python
import math

import jax
import jax.numpy as jnp
from jax import lax
from jax.experimental import pallas as pl
from jax.experimental.pallas import tpu as pltpu
from jax.sharding import PartitionSpec as P

BF = jnp.bfloat16
F32 = jnp.float32
SIDE = 8
DEVICES = 2 * SIDE * SIDE
BOTH = ("blk", "dp")


def device_at(y, z, core):
    return (y % SIDE * SIDE + z % SIDE) * 2 + core


GROUPS_NEAR = [[device_at(y, z, 0) for y in range(SIDE)] for z in range(SIDE)] + [
    [device_at(y, z, 1) for z in range(SIDE)] for y in range(SIDE)
]
SWAP = [(i, i ^ 1) for i in range(DEVICES)]


def far_shift(value, by):
    pairs = []
    for y in range(SIDE):
        for z in range(SIDE):
            pairs.append((device_at(y, z, 0), device_at(y, z + by, 0)))
            pairs.append((device_at(y, z, 1), device_at(y + by, z, 1)))
    return lax.ppermute(value, "blk", pairs)


def swap_cores(value):
    return lax.ppermute(value, "blk", SWAP)


def near_exchange(value):
    return lax.all_to_all(value, "blk", 0, 0, axis_index_groups=GROUPS_NEAR, tiled=True)


def far_gather(own):
    middle = own.shape[0] // 2
    back2 = far_shift(own, 2)
    ahead2 = far_shift(own, -2)
    back1 = far_shift(own, 1)
    ahead1 = far_shift(own, -1)
    back3 = far_shift(back2, 1)
    ahead3 = far_shift(ahead2, -1)
    low = far_shift(back2[:middle], 2)
    high = far_shift(ahead2[middle:], -2)
    return own, ahead1, ahead2, ahead3, low, high, back3, back2, back1


def far_reduce(own, to31, to2, to4_low, to4_high, to57, to6):
    got31 = far_shift(to31, 1)
    got57 = far_shift(to57, -1)
    got4_low = far_shift(to4_low, 2)
    got4_high = far_shift(to4_high, -2)
    size = own.shape[0]
    middle = size // 2

    def add(*values):
        return sum(value.astype(F32) for value in values).astype(BF)

    sum2 = jnp.concatenate(
        [
            add(to2[:middle], got31[:middle], got4_low),
            add(to2[middle:], got31[middle:size]),
        ]
    )
    sum6 = jnp.concatenate(
        [
            add(to6[:middle], got57[:middle]),
            add(to6[middle:], got57[middle:size], got4_high),
        ]
    )
    got2 = far_shift(sum2, 2)
    got6 = far_shift(sum6, -2)
    return add(own, got31[size:], got57[size:], got2, got6)


def block_kernel(core, idx, *refs):
    chunks = refs[:9]
    weight_refs = refs[9:11]
    grads, out = refs[11:13]
    terms = refs[13:20]
    packed_out = refs[20]
    gathered, dense, kept, packed, in_sems, out_sems, pack_sems = refs[21:]
    rows, tokens, wide = kept.shape
    flat = wide - 256
    blocks = flat // 128
    side = chunks[0].shape[0]
    half = side // 2
    places = [(d * side, side) for d in range(4)]
    places += [(4 * side, half), (4 * side + half, half)]
    places += [(d * side, side) for d in range(5, 8)]

    loads = [
        pltpu.make_async_copy(ref, gathered.at[pl.ds(at, size)], in_sems.at[i])
        for i, (ref, (at, size)) in enumerate(zip(chunks, places))
    ]
    for copy in loads:
        copy.start()
    dense[...] = jnp.zeros_like(dense)
    for copy in loads:
        copy.wait()
    for row in range(rows):
        for k in range(blocks):
            kept[row, :, k * 128 : (k + 1) * 128] = gathered[idx[row * blocks + k]]
    for row in range(rows):
        weights = weight_refs[row // 2].at[row % 2]
        both = jnp.dot(kept[row, :, :flat], weights[...], preferred_element_type=F32)
        gate = both[:, :128]
        upper = both[:, 128:]
        sigma = jax.nn.sigmoid(gate)
        out[row] = (gate * sigma * upper).astype(BF)
        gradf = grads[row].astype(F32)
        dgate = gradf * upper * sigma * (1.0 + gate * (1.0 - sigma))
        dup = gradf * gate * sigma
        kept[row, :, flat:] = jnp.concatenate([dgate, dup], axis=1).astype(BF)
    for row in range(rows):
        weights = weight_refs[row // 2].at[row % 2]
        partial = lax.dot_general(
            kept[row, :, flat:],
            weights[...],
            (((1,), (1,)), ((), ())),
            preferred_element_type=F32,
        ).astype(BF)
        for start in range(0, blocks, 6):
            span = range(start, min(start + 6, blocks))
            values = [partial[:, k * 128 : (k + 1) * 128] for k in span]
            places_of = [idx[row * blocks + k] for k in span]
            if row >= rows // 2:
                values = [
                    (dense[at].astype(F32) + value.astype(F32)).astype(BF)
                    for at, value in zip(places_of, values)
                ]
            for at, value in zip(places_of, values):
                dense[at] = value
    own, to31, to2, to4_low, to4_high, to57, to6 = terms
    pieces = [
        (to31.at[pl.ds(0, side)], 3),
        (to57.at[pl.ds(0, side)], 6),
        (to4_low, 4),
        (to4_high, 5),
        (to31.at[pl.ds(side, side)], 1),
        (to57.at[pl.ds(side, side)], 8),
        (to2, 2),
        (to6, 7),
        (own, 0),
    ]
    stores = [
        pltpu.make_async_copy(
            dense.at[pl.ds(places[at][0], places[at][1])], ref, out_sems.at[i]
        )
        for i, (ref, at) in enumerate(pieces)
    ]
    for copy in stores:
        copy.start()
    shards = packed.shape[0] // 2
    part = 128 // shards
    for pair in range(2):
        base = lax.rem(core[0] + pair, 2) * shards
        for k in range(blocks):
            cut = slice(k * 128, (k + 1) * 128)
            turned = jnp.concatenate(
                [kept[2 * pair, :, cut], kept[2 * pair + 1, :, cut]], axis=0
            ).T
            for x in range(shards):
                packed[pair * shards + x, k * part : (k + 1) * part, :] = turned[
                    x * part : (x + 1) * part
                ]
        for row in range(2):
            for side in range(2):
                value = kept[2 * pair + row, :, flat + side * 128 : flat + (side + 1) * 128]
                at = blocks * part + (2 * row + side) * tokens
                for x in range(shards):
                    packed[pair * shards + x, at : at + tokens, :] = value
        copy = pltpu.make_async_copy(
            packed.at[pl.ds(pair * shards, shards)],
            packed_out.at[pl.ds(base, shards)],
            pack_sems.at[pair],
        )
        copy.start()
        stores.append(copy)
    for copy in stores:
        copy.wait()


def run_blocks(core, idx, chunks, weights, other_weights, grads, shards):
    rows, tokens = grads.shape[:2]
    flat = weights.shape[1]
    outside = pl.BlockSpec(memory_space=pl.ANY)
    whole = pl.BlockSpec(memory_space=pltpu.VMEM)
    scalars = pl.BlockSpec(memory_space=pltpu.SMEM)
    side = chunks[0].shape[0]
    total = SIDE * side
    lengths = (side, 2 * side, side, side // 2, side // 2, 2 * side, side)
    packed = (2 * shards, flat // shards + 4 * tokens, 128)
    return pl.pallas_call(
        block_kernel,
        in_specs=[scalars] * 2 + [outside] * 9 + [whole] * 3,
        out_specs=[whole] + [outside] * 8,
        out_shape=[jax.ShapeDtypeStruct((rows, tokens, 128), BF)]
        + [jax.ShapeDtypeStruct((n,) + chunks[0].shape[1:], BF) for n in lengths]
        + [jax.ShapeDtypeStruct(packed, BF)],
        scratch_shapes=[
            pltpu.VMEM((total, tokens, 128), BF),
            pltpu.VMEM((total, tokens, 128), BF),
            pltpu.VMEM((rows, tokens, flat + 256), BF),
            pltpu.VMEM(packed, BF),
            pltpu.SemaphoreType.DMA((9,)),
            pltpu.SemaphoreType.DMA((9,)),
            pltpu.SemaphoreType.DMA((2,)),
        ],
        compiler_params=pltpu.CompilerParams(vmem_limit_bytes=56 * 1024 * 1024),
        cost_estimate=pl.CostEstimate(
            flops=4 * rows * tokens * flat * 256,
            bytes_accessed=2 * rows * flat * 256 + 4 * total * tokens * 128,
            transcendentals=rows * tokens * 128,
        ),
    )(core, idx, *chunks, weights, other_weights, grads)


def weight_kernel(scale, packed, out, total, right):
    sources, height = packed.shape[:2]
    blocks, part = out.shape[1:3]
    flat = blocks * part
    tokens = (height - flat) // 4
    right[...] = jnp.zeros_like(right)
    for step in range(sources // 2):
        for i in range(2):
            for row in range(2):
                for side in range(2):
                    at = flat + (2 * row + side) * tokens
                    right[
                        (2 * i + row) * tokens : (2 * i + row + 1) * tokens,
                        row * 256 + side * 128 : row * 256 + (side + 1) * 128,
                    ] = packed[2 * step + i, at : at + tokens, :]
        left = jnp.concatenate([packed[2 * step, :flat, :], packed[2 * step + 1, :flat, :]], axis=1)
        product = jnp.dot(left, right[...], preferred_element_type=F32)
        if step == 0:
            total[...] = product
        else:
            total[...] += product
    for row in range(2):
        for k in range(blocks):
            value = total[k * part : (k + 1) * part, row * 256 : (row + 1) * 256]
            out[row, k] = (value * scale).astype(BF)


def run_weights(packed, blocks, part, scale):
    sources, height = packed.shape[:2]
    return pl.pallas_call(
        lambda *refs: weight_kernel(scale, *refs),
        in_specs=[pl.BlockSpec(memory_space=pltpu.VMEM)],
        out_specs=pl.BlockSpec(memory_space=pltpu.VMEM),
        out_shape=jax.ShapeDtypeStruct((2, blocks, part, 256), BF),
        scratch_shapes=[
            pltpu.VMEM((blocks * part, 512), F32),
            pltpu.VMEM((256, 512), BF),
        ],
        compiler_params=pltpu.CompilerParams(vmem_limit_bytes=16 * 1024 * 1024),
        cost_estimate=pl.CostEstimate(
            flops=2 * blocks * part * 512 * sources * 128,
            bytes_accessed=2 * sources * height * 128 + 4 * blocks * part * 256,
            transcendentals=0,
        ),
    )(packed)


def local(hidden, weights, pattern, row_of_slot, cotangent):
    tokens = hidden.shape[0]
    half = tokens // 2
    owned, per_row, width = weights.shape[:3]
    flat = per_row * width
    shards = lax.axis_size("dp")
    me = lax.axis_index("blk")
    core = me % 2
    other = me + 1 - 2 * core
    first = core == 0

    def choose(value, mine):
        low, high = value[:half], value[half:]
        return jnp.where(first == mine, low, high)

    def split(value):
        return jnp.transpose(value.reshape(half, owned, width), (1, 0, 2))

    with jax.named_scope("swap_tokens"):
        came = swap_cores(jnp.stack([choose(hidden, False), choose(cotangent, False)]))
        mine, theirs = split(choose(hidden, True)), split(came[0])
        chip_blocks = jnp.where(
            first, jnp.concatenate([mine, theirs]), jnp.concatenate([theirs, mine])
        )
        grads = jnp.concatenate([split(choose(cotangent, True)), split(came[1])])
    with jax.named_scope("gather_near"):
        near = near_exchange(jnp.broadcast_to(chip_blocks[None], (SIDE,) + chip_blocks.shape))
        near = near.reshape(SIDE * 2 * owned, half, width)
    with jax.named_scope("gather_far"):
        chunks = far_gather(near)
    with jax.named_scope("swap_weights"):
        ready, _ = lax.optimization_barrier((weights, near))
        other_weights = swap_cores(ready)
    with jax.named_scope("sources"):
        wanted = jnp.concatenate(
            [
                lax.dynamic_slice_in_dim(pattern, me * owned, owned, 0),
                lax.dynamic_slice_in_dim(pattern, other * owned, owned, 0),
            ]
        )
        slots = jnp.arange(row_of_slot.shape[0], dtype=jnp.int32)
        equal = row_of_slot[None, None, :] == wanted[:, :, None]
        source = jnp.sum(jnp.where(equal, slots[None, None, :], 0), axis=2)
        chip, inside = source // (2 * owned), source % (2 * owned)
        chip_y, chip_z = chip // SIDE, chip % SIDE
        my_y, my_z = me // (2 * SIDE), me // 2 % SIDE
        distance = jnp.where(first, chip_z - my_z, chip_y - my_y) % SIDE
        place = distance * SIDE + jnp.where(first, chip_y, chip_z)
        idx = (place * (2 * owned) + inside).reshape(-1)

    with jax.named_scope("blocks"):
        result, *terms, packed = run_blocks(
            core.reshape(1),
            idx,
            chunks,
            weights.reshape(owned, flat, 2 * width),
            other_weights.reshape(owned, flat, 2 * width),
            grads,
            shards,
        )

    def rejoin(keep, came):
        low = jnp.where(first, keep, came)
        high = jnp.where(first, came, keep)
        whole = jnp.stack([low, high])
        return jnp.transpose(whole, (0, 2, 1, 3)).reshape(tokens, owned * width)

    with jax.named_scope("reduce_far"):
        column = far_reduce(*terms)
    with jax.named_scope("weight_grad"):
        size = 2 * shards
        groups = [[i * size + j for j in range(size)] for i in range(DEVICES // 2)]
        packed = lax.all_to_all(packed, BOTH, 0, 0, axis_index_groups=groups, tiled=True)
        scale = 1.0 / math.sqrt(tokens * shards)
    with jax.named_scope("reduce_near"):
        column, packed = lax.optimization_barrier((column, packed))
        weight_grad = run_weights(packed, per_row, width // shards, scale)
        pieces = near_exchange(column.reshape(SIDE, 2 * owned * half, width))
        total = jnp.sum(pieces.astype(F32), axis=0).astype(BF)
        total = total.reshape(2, owned, half, width)
    with jax.named_scope("swap_back"):
        keep = jnp.where(first, total[0], total[1])
        came = swap_cores(jnp.where(first, total[1], total[0]))
        input_grad = rejoin(keep, came)
        output = rejoin(result[:owned], swap_cores(result[owned:]))
    return (output, input_grad, weight_grad)


def solution(mesh):
    placed = (P("dp", "blk"), P("blk", None, None, None), P(), P(), P("dp", "blk"))
    return jax.shard_map(
        local,
        mesh=mesh,
        in_specs=placed,
        out_specs=(P("dp", "blk"), P("dp", "blk"), P("blk", None, "dp", None)),
        check_vma=False,
    )
```

time: 187 us -> 168 us (0.90)
  starting transfers between devices: 45.7 us -> 85.7 us
  waiting for transfers between devices: 64.9 us -> 33.1 us
  between operations: 14.3 us -> 1.06 us
  local copies, waits for them, and re-layouts: 18.7 us -> 7.38 us
  Pallas kernels: 8.84 us -> 13.8 us
  other arithmetic: 14 us -> 9.44 us
  matrix products: 2.86 us -> 0 us
    ppermute x0 -> x14, starting transfers between devices: none -> 50.4 us  [far_shift(): return lax.ppermute(value, 'blk', pairs)]
    all_to_all x2, waiting for transfers between devices: 44.3 us -> 6.29 us  [the longest x1 6.29 us: near_exchange(): lax.all_to_all(value, 'blk', 0, 0, axis_index_groups=GROUPS_NEAR, tiled=T...]
    ppermute x0 -> x14, waiting for transfers between devices: none -> 25.1 us  [far_shift(): return lax.ppermute(value, 'blk', pairs)]
    all_gather x1 -> x0, waiting for transfers between devices: 13.9 us -> none  [local(): lax.all_gather(near, 'blk', axis_index_groups=GROUPS_FAR, tiled=True)]
    ppermute x5 -> x4, starting transfers between devices: 34.1 us -> 21.5 us  [swap_cores(): return lax.ppermute(value, 'blk', SWAP)]
    reshape x1, local copies, waits for them, and re-layouts: 9.91 us -> 0.67 us  [rejoin(): return jnp.transpose(whole, (0, 2, 1, 3)).reshape(tokens, owned * width)]
    concatenate x2 -> x3, other arithmetic: 6.43 us -> 0.74 us  [the longest x1 0.64 us: local(): grads = jnp.concatenate([split(choose(cotangent, True)), split(came[1])])]
    pallas_call x1 -> x2, Pallas kernels: 8.84 us -> 13.8 us  [the longest x1 11.8 us: run_blocks(): pl.pallas_call(block_kernel, in_specs=[scalars] * 2 + [outside] * 9 + [wh...]
  transfers between devices with their start and end apart: 9 -> 20, of which waited for: 6 -> 10; matrix products, arithmetic and copies ran while one was open for 15% -> 7% of each run, Pallas kernels for 0% -> 1%
where the time goes in v2:
time: 168 us; the launch traced here: 167 us
  starting transfers between devices  85.7 us (51%)
  waiting for transfers between devices  33.1 us (20%)
  blocking collectives  16.7 us (10%)
  Pallas kernels  13.8 us (8%)
  other arithmetic  9.44 us (6%)
  local copies, waits for them, and re-layouts  7.38 us (4%)
    ppermute x14, starting transfers between devices, far_shift(): return lax.ppermute(value, 'blk', pairs)  50.4 us
    ppermute x14, waiting for transfers between devices, far_shift(): return lax.ppermute(value, 'blk', pairs)  25.1 us
    ppermute x4, starting transfers between devices, swap_cores(): return lax.ppermute(value, 'blk', SWAP)  21.5 us
    all_to_all x1, blocking collectives, near_exchange(): lax.all_to_all(value, 'blk', 0, 0, axis_index_groups=GROUPS_NEAR, tiled=T...  16.7 us
    pallas_call x1, Pallas kernels, run_blocks(): pl.pallas_call(block_kernel, in_specs=[scalars] * 2 + [outside] * 9 + [wh...  11.8 us
    all_to_all x1, starting transfers between devices, local(): lax.all_to_all(packed, BOTH, 0, 0, axis_index_groups=groups, tiled=True)  9.28 us
    all_to_all x1, waiting for transfers between devices, near_exchange(): lax.all_to_all(value, 'blk', 0, 0, axis_index_groups=GROUPS_NEAR, tiled=T...  6.29 us
    convert_element_type x3, other arithmetic, add(): return sum((value.astype(F32) for value in values)).astype(BF)  4.99 us
  transfers between devices with their start and end apart: 20, of which 10 were waited for; matrix products, arithmetic and copies ran while one was open for 7% of the time, Pallas kernels for 1%

profile of v2, /device:TPU:1, one launch (start us, length us, event | category | flops | bytes accessed | tf_op | source)
XLA Modules:
  0.0 167.2 jit_solution(4289991250224674966)
XLA Ops:
  2.2 8.8 %collective-permute-start = (bf16[2,64,256]{2,1,0:T(8,128)(2,1)S(1)}, bf16[2,64,256]{2,1,0:T(8,128)(2,1)S(1)}, u32[]{:S(2)}, u32[]{:S(2)}) collective-permute-start(bf16[2,64,256]{2,1,0:T(8,128)(2,1)S(1)} %pad_maximum_fusion.2), channel_id=1, source_target_pairs={{0,4},{4,0},{8,12},{12,8},{16,20},{20,16},{24,28},{28,24},{32,36},... | collective-permute-start | bytes 196616 | tf_op jit(solution)/shard_map/swap_tokens/ppermute | solution.py:37
  12.2 16.7 %all_to_all.15 = bf16[8,4,64,128]{3,2,1,0:T(8,128)(2,1)} all-to-all(bf16[8,4,64,128]{3,2,1,0:T(8,128)(2,1)S(1)} %broadcast_in_dim.23), channel_id=1, replica_groups={{0,64,128,192,256,320,384,448},{8,72,136,200,264,328,392,456},{16,80,14..., dimensions={0} | all-to-all | bytes 1048576 | tf_op jit(solution)/shard_map/gather_near/all_to_all | solution.py:41
  30.8 4.2 %collective-permute-start.4 = (bf16[32,64,128]{2,1,0:T(8,128)(2,1)}, bf16[32,64,128]{2,1,0:T(8,128)(2,1)}, u32[]{:S(2)}, u32[]{:S(2)}) collective-permute-start(bf16[32,64,128]{2,1,0:T(8,128)(2,1)} %bitcast.5.refs_0_), channel_id=1, source_target_pairs={{0,16},{4,132},{8,24},{12,140},{16,32},{20,148},{24,40},{28,156},{... | collective-permute-start | bytes 1572872 | tf_op jit(solution)/shard_map/gather_far/ppermute | solution.py:33
  35.0 3.6 %collective-permute-start.2 = (bf16[32,64,128]{2,1,0:T(8,128)(2,1)}, bf16[32,64,128]{2,1,0:T(8,128)(2,1)}, u32[]{:S(2)}, u32[]{:S(2)}) collective-permute-start(bf16[32,64,128]{2,1,0:T(8,128)(2,1)} %bitcast.5.refs_0_), channel_id=1, source_target_pairs={{0,48},{4,388},{8,56},{12,396},{16,0},{20,404},{24,8},{28,412},{32... | collective-permute-start | bytes 1572872 | tf_op jit(solution)/shard_map/gather_far/ppermute | solution.py:33
  38.6 2.8 %collective-permute-start.8 = (bf16[32,64,128]{2,1,0:T(8,128)(2,1)}, bf16[32,64,128]{2,1,0:T(8,128)(2,1)}, u32[]{:S(2)}, u32[]{:S(2)}) collective-permute-start(bf16[32,64,128]{2,1,0:T(8,128)(2,1)} %bitcast.5.refs_0_), channel_id=1, source_target_pairs={{0,8},{4,68},{8,16},{12,76},{16,24},{20,84},{24,32},{28,92},{32,40... | collective-permute-start | bytes 1572872 | tf_op jit(solution)/shard_map/gather_far/ppermute | solution.py:33
  41.4 3.7 %collective-permute-start.1 = (bf16[32,64,128]{2,1,0:T(8,128)(2,1)}, bf16[32,64,128]{2,1,0:T(8,128)(2,1)}, u32[]{:S(2)}, u32[]{:S(2)}) collective-permute-start(bf16[32,64,128]{2,1,0:T(8,128)(2,1)} %bitcast.5.refs_0_), channel_id=1, source_target_pairs={{0,56},{4,452},{8,0},{12,460},{16,8},{20,468},{24,16},{28,476},{32... | collective-permute-start | bytes 1572872 | tf_op jit(solution)/shard_map/gather_far/ppermute | solution.py:33
  46.8 5.2 %collective-permute-start.7 = (bf16[32,64,128]{2,1,0:T(8,128)(2,1)}, bf16[32,64,128]{2,1,0:T(8,128)(2,1)}, u32[]{:S(2)}, u32[]{:S(2)}) collective-permute-start(bf16[32,64,128]{2,1,0:T(8,128)(2,1)} %collective-permute-done.4.refs_7_), channel_id=1, source_target_pairs={{0,8},{4,68},{8,16},{12,76},{16,24},{20,84},{24,32},{28,92},{32,40... | collective-permute-start | bytes 1572872 | tf_op jit(solution)/shard_map/gather_far/ppermute | solution.py:33
  60.1 4.4 %collective-permute-start.5 = (bf16[16,64,128]{2,1,0:T(8,128)(2,1)}, bf16[16,64,128]{2,1,0:T(8,128)(2,1)}, u32[]{:S(2)}, u32[]{:S(2)}) collective-permute-start(bf16[16,64,128]{2,1,0:T(8,128)(2,1)} %slice.97), channel_id=1, source_target_pairs={{0,16},{4,132},{8,24},{12,140},{16,32},{20,148},{24,40},{28,156},{... | collective-permute-start | bytes 786440 | tf_op jit(solution)/shard_map/gather_far/ppermute | solution.py:33
  64.6 3.0 %collective-permute-start.6 = (bf16[16,64,128]{2,1,0:T(8,128)(2,1)}, bf16[16,64,128]{2,1,0:T(8,128)(2,1)}, u32[]{:S(2)}, u32[]{:S(2)}) collective-permute-start(bf16[16,64,128]{2,1,0:T(8,128)(2,1)} %slice.98), channel_id=1, source_target_pairs={{0,48},{4,388},{8,56},{12,396},{16,0},{20,404},{24,8},{28,412},{32... | collective-permute-start | bytes 786440 | tf_op jit(solution)/shard_map/gather_far/ppermute | solution.py:33
  68.8 3.6 %collective-permute-done.5.refs_4_ = bf16[16,64,128]{2,1,0:T(8,128)(2,1)} collective-permute-done((bf16[16,64,128]{2,1,0:T(8,128)(2,1)}, bf16[16,64,128]{2,1,0:T(8,128)(2,1)}, u32[]{:S(2)}, u32[]{:S(2)}) %collective-permute-start.5) | collective-permute-done | bytes 262176 | tf_op jit(solution)/shard_map/gather_far/ppermute | solution.py:33
  72.5 4.6 %collective-permute-done.6.refs_5_ = bf16[16,64,128]{2,1,0:T(8,128)(2,1)} collective-permute-done((bf16[16,64,128]{2,1,0:T(8,128)(2,1)}, bf16[16,64,128]{2,1,0:T(8,128)(2,1)}, u32[]{:S(2)}, u32[]{:S(2)}) %collective-permute-start.6) | collective-permute-done | bytes 262176 | tf_op jit(solution)/shard_map/gather_far/ppermute | solution.py:33
  78.8 11.8 %blocks.1 = (bf16[4,64,128]{2,1,0:T(8,128)(2,1)}, bf16[32,64,128]{2,1,0:T(8,128)(2,1)}, bf16[64,64,128]{2,1,0:T(8,128)(2,1)}, bf16[32,64,128]{2,1,0:T(8,128)(2,1...) custom-call(s32[1]{0:T(128)} %bitcast.core, ...), custom_call_target="tpu_custom_call" | custom-call | flops 872415232 | bytes 15204352 | tf_op jit(solution)/shard_map/blocks/pallas_call | solution.py:203
  92.6 4.6 %collective-permute-start.12 = (bf16[64,64,128]{2,1,0:T(8,128)(2,1)}, bf16[64,64,128]{2,1,0:T(8,128)(2,1)}, u32[]{:S(2)}, u32[]{:S(2)}) collective-permute-start(bf16[64,64,128]{2,1,0:T(8,128)(2,1)} %get-tuple-element.19), channel_id=1, source_target_pairs={{0,56},{4,452},{8,0},{12,460},{16,8},{20,468},{24,16},{28,476},{32... | collective-permute-start | bytes 3145736 | tf_op jit(solution)/shard_map/reduce_far/ppermute | solution.py:33
  97.2 9.3 %all-to-all-start.1 = ((bf16[8,1088,128]{2,1,0:T(8,128)(2,1)}), bf16[8,1088,128]{2,1,0:T(8,128)(2,1)S(1)}, u32[]{:S(2)}, u32[]{:S(2)}) async-start(bf16[8,1088,128]{2,1,0:T(8,128)(2,1)} %get-tuple-element.24), calls=%async_computation.1 | async-start | bytes 4456448 | tf_op jit(solution)/shard_map/weight_grad/all_to_all | solution.py:347
  108.6 5.5 %collective-permute-start.15 = (bf16[16,64,128]{2,1,0:T(8,128)(2,1)S(1)}, bf16[16,64,128]{2,1,0:T(8,128)(2,1)S(1)}, u32[]{:S(2)}, u32[]{:S(2)}) collective-permute-start(bf16[16,64,128]{2,1,0:T(8,128)(2,1)S(1)} %copy-done.3), channel_id=1, source_target_pairs={{0,48},{4,388},{8,56},{12,396},{16,0},{20,404},{24,8},{28,412},{32... | collective-permute-start | bytes 786440 | tf_op jit(solution)/shard_map/reduce_far/ppermute | solution.py:33
  114.0 3.3 %collective-permute-done.13 = bf16[16,64,128]{2,1,0:T(8,128)(2,1)S(1)} collective-permute-done((bf16[16,64,128]{2,1,0:T(8,128)(2,1)}, bf16[16,64,128]{2,1,0:T(8,128)(2,1)S(1)}, u32[]{:S(2)}, u32[]{:S(2)}) %collective-permute-start.13) | collective-permute-done | bytes 262176 | tf_op jit(solution)/shard_map/reduce_far/ppermute | solution.py:33
  122.2 5.5 %collective-permute-start.16 = (bf16[32,64,128]{2,1,0:T(8,128)(2,1)S(1)}, bf16[32,64,128]{2,1,0:T(8,128)(2,1)S(1)}, u32[]{:S(2)}, u32[]{:S(2)}) collective-permute-start(bf16[32,64,128]{2,1,0:T(8,128)(2,1)S(1)} %pad_maximum_fusion.1), channel_id=1, source_target_pairs={{0,48},{4,388},{8,56},{12,396},{16,0},{20,404},{24,8},{28,412},{32... | collective-permute-start | bytes 1572872 | tf_op jit(solution)/shard_map/reduce_far/ppermute | solution.py:33
  127.7 8.9 %collective-permute-done.14 = bf16[32,64,128]{2,1,0:T(8,128)(2,1)S(1)} collective-permute-done((bf16[32,64,128]{2,1,0:T(8,128)(2,1)S(1)}, bf16[32,64,128]{2,1,0:T(8,128)(2,1)S(1)}, u32[]{:S(2)}, u32[]{:S(2)}) %collective-permute-start.14) | collective-permute-done | bytes 524320 | tf_op jit(solution)/shard_map/reduce_far/ppermute | solution.py:33
  136.6 2.8 %collective-permute-done.16 = bf16[32,64,128]{2,1,0:T(8,128)(2,1)S(1)} collective-permute-done((bf16[32,64,128]{2,1,0:T(8,128)(2,1)S(1)}, bf16[32,64,128]{2,1,0:T(8,128)(2,1)S(1)}, u32[]{:S(2)}, u32[]{:S(2)}) %collective-permute-start.16) | collective-permute-done | bytes 524320 | tf_op jit(solution)/shard_map/reduce_far/ppermute | solution.py:33
  139.4 2.3 %add_convert_fusion = bf16[32,64,128]{2,1,0:T(8,128)(2,1)} fusion(bf16[32,64,128]{2,1,0:T(8,128)(2,1)S(1)} %collective-permute-done.16, bf16[32,64,128]{2,1,0:T(8,128)(2,1)S(1)} %collective-permute-done.14, bf16[32,64,128]{2,1,0:T(8,128)(2,1)S(1)} %copy-done.1, bf16[64,64,128]{2,1,0:T(8,128)(2,1)} %collective-permute-done.12, ...), kind=kLoop, calls=%fused_computation | loop fusion | flops 2621440 | bytes 3145728 | tf_op jit(solution)/shard_map/reduce_far/convert_element_type | solution.py:66
  141.7 4.6 %all-to-all-start.2 = ((bf16[8,256,128]{2,1,0:T(8,128)(2,1)}), bf16[8,256,128]{2,1,0:T(8,128)(2,1)S(1)}, u32[]{:S(2)}, u32[]{:S(2)}) async-start(bf16[8,256,128]{2,1,0:T(8,128)(2,1)} %bitcast.13), calls=%async_computation.2 | async-start | bytes 1048576 | tf_op jit(solution)/shard_map/reduce_near/all_to_all | solution.py:41
  146.3 4.9 %collective-permute-start.10 = (bf16[2,64,128]{2,1,0:T(8,128)(2,1)S(1)}, bf16[2,64,128]{2,1,0:T(8,128)(2,1)S(1)}, u32[]{:S(2)}, u32[]{:S(2)}) collective-permute-start(bf16[2,64,128]{2,1,0:T(8,128)(2,1)S(1)} %slice.83), channel_id=1, source_target_pairs={{0,4},{4,0},{8,12},{12,8},{16,20},{20,16},{24,28},{28,24},{32,36},... | collective-permute-start | bytes 98312 | tf_op jit(solution)/shard_map/swap_back/ppermute | solution.py:37
  152.1 6.3 %all-to-all-done.2 = bf16[8,256,128]{2,1,0:T(8,128)(2,1)S(1)} async-done(((bf16[8,256,128]{2,1,0:T(8,128)(2,1)}), bf16[8,256,128]{2,1,0:T(8,128)(2,1)S(1)}, u32[]{:S(2)}, u32[]{:S(2)}) %all-to-all-start.2) | async-done | bytes 524320 | tf_op jit(solution)/shard_map/reduce_near/all_to_all | solution.py:41
  158.5 5.9 %collective-permute-start.17 = (bf16[2,64,128]{2,1,0:T(8,128)(2,1)S(1)}, bf16[2,64,128]{2,1,0:T(8,128)(2,1)S(1)}, u32[]{:S(2)}, u32[]{:S(2)}) collective-permute-start(bf16[2,64,128]{2,1,0:T(8,128)(2,1)S(1)} %bitcast.53), channel_id=1, source_target_pairs={{0,4},{4,0},{8,12},{12,8},{16,20},{20,16},{24,28},{28,24},{32,36},... | collective-permute-start | bytes 98312 | tf_op jit(solution)/shard_map/swap_back/ppermute | solution.py:37
  (66 shorter events, 29.9 us)
Async XLA Ops:
  2.2 9.7 %collective-permute-start = (bf16[2,64,256]{2,1,0:T(8,128)(2,1)S(1)}, bf16[2,64,256]{2,1,0:T(8,128)(2,1)S(1)}, u32[]{:S(2)}, u32[]{:S(2)}) collective-permute-start(bf16[2,64,256]{2,1,0:T(8,128)(2,1)S(1)} %pad_maximum_fusion.2), channel_id=1, source_target_pairs={{0,4},{4,0},{8,12},{12,8},{16,20},{20,16},{24,28},{28,24},{32,36},... | collective-permute-start | bytes 196616 | tf_op jit(solution)/shard_map/swap_tokens/ppermute | solution.py:37
  28.9 48.1 %collective-permute-start.9 = (bf16[2,26,128,256]{3,2,1,0:T(8,128)(2,1)}, bf16[2,26,128,256]{3,2,1,0:T(8,128)(2,1)S(1)}, u32[]{:S(2)}, u32[]{:S(2)}) collective-permute-start(bf16[2,26,128,256]{3,2,1,0:T(8,128)(2,1)} %param.6), channel_id=1, source_target_pairs={{0,4},{4,0},{8,12},{12,8},{16,20},{20,16},{24,28},{28,24},{32,36},... | collective-permute-start | bytes 10223624 | tf_op jit(solution)/shard_map/swap_weights/ppermute | solution.py:37
  30.8 16.0 %collective-permute-start.4 = (bf16[32,64,128]{2,1,0:T(8,128)(2,1)}, bf16[32,64,128]{2,1,0:T(8,128)(2,1)}, u32[]{:S(2)}, u32[]{:S(2)}) collective-permute-start(bf16[32,64,128]{2,1,0:T(8,128)(2,1)} %bitcast.5.refs_0_), channel_id=1, source_target_pairs={{0,16},{4,132},{8,24},{12,140},{16,32},{20,148},{24,40},{28,156},{... | collective-permute-start | bytes 1572872 | tf_op jit(solution)/shard_map/gather_far/ppermute | solution.py:33
  35.0 18.3 %collective-permute-start.2 = (bf16[32,64,128]{2,1,0:T(8,128)(2,1)}, bf16[32,64,128]{2,1,0:T(8,128)(2,1)}, u32[]{:S(2)}, u32[]{:S(2)}) collective-permute-start(bf16[32,64,128]{2,1,0:T(8,128)(2,1)} %bitcast.5.refs_0_), channel_id=1, source_target_pairs={{0,48},{4,388},{8,56},{12,396},{16,0},{20,404},{24,8},{28,412},{32... | collective-permute-start | bytes 1572872 | tf_op jit(solution)/shard_map/gather_far/ppermute | solution.py:33
  38.6 21.5 %collective-permute-start.8 = (bf16[32,64,128]{2,1,0:T(8,128)(2,1)}, bf16[32,64,128]{2,1,0:T(8,128)(2,1)}, u32[]{:S(2)}, u32[]{:S(2)}) collective-permute-start(bf16[32,64,128]{2,1,0:T(8,128)(2,1)} %bitcast.5.refs_0_), channel_id=1, source_target_pairs={{0,8},{4,68},{8,16},{12,76},{16,24},{20,84},{24,32},{28,92},{32,40... | collective-permute-start | bytes 1572872 | tf_op jit(solution)/shard_map/gather_far/ppermute | solution.py:33
  41.4 23.1 %collective-permute-start.1 = (bf16[32,64,128]{2,1,0:T(8,128)(2,1)}, bf16[32,64,128]{2,1,0:T(8,128)(2,1)}, u32[]{:S(2)}, u32[]{:S(2)}) collective-permute-start(bf16[32,64,128]{2,1,0:T(8,128)(2,1)} %bitcast.5.refs_0_), channel_id=1, source_target_pairs={{0,56},{4,452},{8,0},{12,460},{16,8},{20,468},{24,16},{28,476},{32... | collective-permute-start | bytes 1572872 | tf_op jit(solution)/shard_map/gather_far/ppermute | solution.py:33
  46.8 30.2 %collective-permute-start.7 = (bf16[32,64,128]{2,1,0:T(8,128)(2,1)}, bf16[32,64,128]{2,1,0:T(8,128)(2,1)}, u32[]{:S(2)}, u32[]{:S(2)}) collective-permute-start(bf16[32,64,128]{2,1,0:T(8,128)(2,1)} %collective-permute-done.4.refs_7_), channel_id=1, source_target_pairs={{0,8},{4,68},{8,16},{12,76},{16,24},{20,84},{24,32},{28,92},{32,40... | collective-permute-start | bytes 1572872 | tf_op jit(solution)/shard_map/gather_far/ppermute | solution.py:33
  53.3 23.7 %collective-permute-start.3 = (bf16[32,64,128]{2,1,0:T(8,128)(2,1)}, bf16[32,64,128]{2,1,0:T(8,128)(2,1)}, u32[]{:S(2)}, u32[]{:S(2)}) collective-permute-start(bf16[32,64,128]{2,1,0:T(8,128)(2,1)} %collective-permute-done.2.refs_2_), channel_id=1, source_target_pairs={{0,56},{4,452},{8,0},{12,460},{16,8},{20,468},{24,16},{28,476},{32... | collective-permute-start | bytes 1572872 | tf_op jit(solution)/shard_map/gather_far/ppermute | solution.py:33
  60.1 12.3 %collective-permute-start.5 = (bf16[16,64,128]{2,1,0:T(8,128)(2,1)}, bf16[16,64,128]{2,1,0:T(8,128)(2,1)}, u32[]{:S(2)}, u32[]{:S(2)}) collective-permute-start(bf16[16,64,128]{2,1,0:T(8,128)(2,1)} %slice.97), channel_id=1, source_target_pairs={{0,16},{4,132},{8,24},{12,140},{16,32},{20,148},{24,40},{28,156},{... | collective-permute-start | bytes 786440 | tf_op jit(solution)/shard_map/gather_far/ppermute | solution.py:33
  64.6 12.5 %collective-permute-start.6 = (bf16[16,64,128]{2,1,0:T(8,128)(2,1)}, bf16[16,64,128]{2,1,0:T(8,128)(2,1)}, u32[]{:S(2)}, u32[]{:S(2)}) collective-permute-start(bf16[16,64,128]{2,1,0:T(8,128)(2,1)} %slice.98), channel_id=1, source_target_pairs={{0,48},{4,388},{8,56},{12,396},{16,0},{20,404},{24,8},{28,412},{32... | collective-permute-start | bytes 786440 | tf_op jit(solution)/shard_map/gather_far/ppermute | solution.py:33
  77.0 1.7 %copy-start = (bf16[2,26,128,256]{3,2,1,0:T(8,128)(2,1)}, bf16[2,26,128,256]{3,2,1,0:T(8,128)(2,1)S(1)}, u32[]{:S(2)}) copy-start(bf16[2,26,128,256]{3,2,1,0:T(8,128)(2,1)S(1)} %collective-permute-done.9) | copy-start | bytes 10223620
  90.6 18.0 %copy-start.3 = (bf16[16,64,128]{2,1,0:T(8,128)(2,1)S(1)}, bf16[16,64,128]{2,1,0:T(8,128)(2,1)}, u32[]{:S(2)}) copy-start(bf16[16,64,128]{2,1,0:T(8,128)(2,1)} %get-tuple-element.23) | copy-start | bytes 786436
  90.6 26.8 %collective-permute-start.11 = (bf16[64,64,128]{2,1,0:T(8,128)(2,1)}, bf16[64,64,128]{2,1,0:T(8,128)(2,1)S(1)}, u32[]{:S(2)}, u32[]{:S(2)}) collective-permute-start(bf16[64,64,128]{2,1,0:T(8,128)(2,1)} %get-tuple-element.18), channel_id=1, source_target_pairs={{0,8},{4,68},{8,16},{12,76},{16,24},{20,84},{24,32},{28,92},{32,40... | collective-permute-start | bytes 3145736 | tf_op jit(solution)/shard_map/reduce_far/ppermute | solution.py:33
  92.6 28.0 %collective-permute-start.12 = (bf16[64,64,128]{2,1,0:T(8,128)(2,1)}, bf16[64,64,128]{2,1,0:T(8,128)(2,1)}, u32[]{:S(2)}, u32[]{:S(2)}) collective-permute-start(bf16[64,64,128]{2,1,0:T(8,128)(2,1)} %get-tuple-element.19), channel_id=1, source_target_pairs={{0,56},{4,452},{8,0},{12,460},{16,8},{20,468},{24,16},{28,476},{32... | collective-permute-start | bytes 3145736 | tf_op jit(solution)/shard_map/reduce_far/ppermute | solution.py:33
  97.2 44.5 %all-to-all-start.1 = ((bf16[8,1088,128]{2,1,0:T(8,128)(2,1)}), bf16[8,1088,128]{2,1,0:T(8,128)(2,1)S(1)}, u32[]{:S(2)}, u32[]{:S(2)}) async-start(bf16[8,1088,128]{2,1,0:T(8,128)(2,1)} %get-tuple-element.24), calls=%async_computation.1 | async-start | bytes 4456448 | tf_op jit(solution)/shard_map/weight_grad/all_to_all | solution.py:347
  106.5 32.9 %copy-start.1 = (bf16[32,64,128]{2,1,0:T(8,128)(2,1)S(1)}, bf16[32,64,128]{2,1,0:T(8,128)(2,1)}, u32[]{:S(2)}) copy-start(bf16[32,64,128]{2,1,0:T(8,128)(2,1)} %get-tuple-element.17) | copy-start | bytes 1572868
  106.5 10.9 %collective-permute-start.13 = (bf16[16,64,128]{2,1,0:T(8,128)(2,1)}, bf16[16,64,128]{2,1,0:T(8,128)(2,1)S(1)}, u32[]{:S(2)}, u32[]{:S(2)}) collective-permute-start(bf16[16,64,128]{2,1,0:T(8,128)(2,1)} %get-tuple-element.21), channel_id=1, source_target_pairs={{0,16},{4,132},{8,24},{12,140},{16,32},{20,148},{24,40},{28,156},{... | collective-permute-start | bytes 786440 | tf_op jit(solution)/shard_map/reduce_far/ppermute | solution.py:33
  108.6 12.1 %collective-permute-start.15 = (bf16[16,64,128]{2,1,0:T(8,128)(2,1)S(1)}, bf16[16,64,128]{2,1,0:T(8,128)(2,1)S(1)}, u32[]{:S(2)}, u32[]{:S(2)}) collective-permute-start(bf16[16,64,128]{2,1,0:T(8,128)(2,1)S(1)} %copy-done.3), channel_id=1, source_target_pairs={{0,48},{4,388},{8,56},{12,396},{16,0},{20,404},{24,8},{28,412},{32... | collective-permute-start | bytes 786440 | tf_op jit(solution)/shard_map/reduce_far/ppermute | solution.py:33
  118.7 17.9 %collective-permute-start.14 = (bf16[32,64,128]{2,1,0:T(8,128)(2,1)S(1)}, bf16[32,64,128]{2,1,0:T(8,128)(2,1)S(1)}, u32[]{:S(2)}, u32[]{:S(2)}) collective-permute-start(bf16[32,64,128]{2,1,0:T(8,128)(2,1)S(1)} %pad_maximum_fusion), channel_id=1, source_target_pairs={{0,16},{4,132},{8,24},{12,140},{16,32},{20,148},{24,40},{28,156},{... | collective-permute-start | bytes 1572872 | tf_op jit(solution)/shard_map/reduce_far/ppermute | solution.py:33
  120.6 25.6 %copy-start.2 = (bf16[4,64,128]{2,1,0:T(8,128)(2,1)S(1)}, bf16[4,64,128]{2,1,0:T(8,128)(2,1)}, u32[]{:S(2)}) copy-start(bf16[4,64,128]{2,1,0:T(8,128)(2,1)} %get-tuple-element.16) | copy-start | bytes 196612
  122.2 17.2 %collective-permute-start.16 = (bf16[32,64,128]{2,1,0:T(8,128)(2,1)S(1)}, bf16[32,64,128]{2,1,0:T(8,128)(2,1)S(1)}, u32[]{:S(2)}, u32[]{:S(2)}) collective-permute-start(bf16[32,64,128]{2,1,0:T(8,128)(2,1)S(1)} %pad_maximum_fusion.1), channel_id=1, source_target_pairs={{0,48},{4,388},{8,56},{12,396},{16,0},{20,404},{24,8},{28,412},{32... | collective-permute-start | bytes 1572872 | tf_op jit(solution)/shard_map/reduce_far/ppermute | solution.py:33
  141.7 16.7 %all-to-all-start.2 = ((bf16[8,256,128]{2,1,0:T(8,128)(2,1)}), bf16[8,256,128]{2,1,0:T(8,128)(2,1)S(1)}, u32[]{:S(2)}, u32[]{:S(2)}) async-start(bf16[8,256,128]{2,1,0:T(8,128)(2,1)} %bitcast.13), calls=%async_computation.2 | async-start | bytes 1048576 | tf_op jit(solution)/shard_map/reduce_near/all_to_all | solution.py:41
  146.3 5.7 %collective-permute-start.10 = (bf16[2,64,128]{2,1,0:T(8,128)(2,1)S(1)}, bf16[2,64,128]{2,1,0:T(8,128)(2,1)S(1)}, u32[]{:S(2)}, u32[]{:S(2)}) collective-permute-start(bf16[2,64,128]{2,1,0:T(8,128)(2,1)S(1)} %slice.83), channel_id=1, source_target_pairs={{0,4},{4,0},{8,12},{12,8},{16,20},{20,16},{24,28},{28,24},{32,36},... | collective-permute-start | bytes 98312 | tf_op jit(solution)/shard_map/swap_back/ppermute | solution.py:37
  158.5 7.9 %collective-permute-start.17 = (bf16[2,64,128]{2,1,0:T(8,128)(2,1)S(1)}, bf16[2,64,128]{2,1,0:T(8,128)(2,1)S(1)}, u32[]{:S(2)}, u32[]{:S(2)}) collective-permute-start(bf16[2,64,128]{2,1,0:T(8,128)(2,1)S(1)} %bitcast.53), channel_id=1, source_target_pairs={{0,4},{4,0},{8,12},{12,8},{16,20},{20,16},{24,28},{28,24},{32,36},... | collective-permute-start | bytes 98312 | tf_op jit(solution)/shard_map/swap_back/ppermute | solution.py:37

commit v3 on v2

--- a/solution.py
+++ b/solution.py
@@ -28,8 +28,10 @@
     pairs = []
     for y in range(SIDE):
         for z in range(SIDE):
-            pairs.append((device_at(y, z, 0), device_at(y, z + by, 0)))
-            pairs.append((device_at(y, z, 1), device_at(y + by, z, 1)))
+            here = z + by * (1 - 2 * (z % 2))
+            pairs.append((device_at(y, z, 0), device_at(y, here, 0)))
+            here = y + by * (1 - 2 * (y % 2))
+            pairs.append((device_at(y, z, 1), device_at(here, z, 1)))
     return lax.ppermute(value, "blk", pairs)
 
 
@@ -42,67 +44,56 @@
 
 
 def far_gather(own):
-    middle = own.shape[0] // 2
-    back2 = far_shift(own, 2)
-    ahead2 = far_shift(own, -2)
-    back1 = far_shift(own, 1)
-    ahead1 = far_shift(own, -1)
-    back3 = far_shift(back2, 1)
-    ahead3 = far_shift(ahead2, -1)
-    low = far_shift(back2[:middle], 2)
-    high = far_shift(ahead2[middle:], -2)
-    return own, ahead1, ahead2, ahead3, low, high, back3, back2, back1
-
-
-def far_reduce(own, to31, to2, to4_low, to4_high, to57, to6):
+    at6 = far_shift(own, 2)
+    at2 = far_shift(own, -2)
+    at1 = far_shift(own, 1)
+    at7 = far_shift(own, -1)
+    at4 = far_shift(at6, 2)
+    at3 = far_shift(at6, 1)
+    at5 = far_shift(at2, -1)
+    return own, at1, at2, at3, at4, at5, at6, at7
+
+
+def far_reduce(own, to31, to57, to4, to2, to6):
+    size = own.shape[0]
     got31 = far_shift(to31, 1)
     got57 = far_shift(to57, -1)
-    got4_low = far_shift(to4_low, 2)
-    got4_high = far_shift(to4_high, -2)
-    size = own.shape[0]
-    middle = size // 2
+    got4 = far_shift(to4, 2)
 
     def add(*values):
         return sum(value.astype(F32) for value in values).astype(BF)
 
-    sum2 = jnp.concatenate(
-        [
-            add(to2[:middle], got31[:middle], got4_low),
-            add(to2[middle:], got31[middle:size]),
-        ]
+    got6 = far_shift(add(to6, got31[:size]), -2)
+    got2 = far_shift(add(to2, got57[:size], got4), 2)
+    early = lax.optimization_barrier(
+        own.astype(F32) + got31[size:].astype(F32) + got57[size:].astype(F32)
     )
-    sum6 = jnp.concatenate(
-        [
-            add(to6[:middle], got57[:middle]),
-            add(to6[middle:], got57[middle:size], got4_high),
-        ]
-    )
-    got2 = far_shift(sum2, 2)
-    got6 = far_shift(sum6, -2)
-    return add(own, got31[size:], got57[size:], got2, got6)
+    return add(early, got2, got6)
 
 
 def block_kernel(core, idx, *refs):
-    chunks = refs[:9]
-    weight_refs = refs[9:11]
-    grads, out = refs[11:13]
-    terms = refs[13:20]
-    packed_out = refs[20]
-    gathered, dense, kept, packed, in_sems, out_sems, pack_sems = refs[21:]
+    chunks = refs[:8]
+    weights_here, weights_there, grads, out = refs[8:12]
+    terms = refs[12:18]
+    packed_out = refs[18]
+    gathered, dense, kept, packed, weights, in_sems, out_sems, pack_sems, weight_sems = refs[19:]
     rows, tokens, wide = kept.shape
     flat = wide - 256
     blocks = flat // 128
     side = chunks[0].shape[0]
-    half = side // 2
-    places = [(d * side, side) for d in range(4)]
-    places += [(4 * side, half), (4 * side + half, half)]
-    places += [(d * side, side) for d in range(5, 8)]
+
+    def place(distance):
+        return pl.ds(distance * side, side)
 
     loads = [
-        pltpu.make_async_copy(ref, gathered.at[pl.ds(at, size)], in_sems.at[i])
-        for i, (ref, (at, size)) in enumerate(zip(chunks, places))
+        pltpu.make_async_copy(ref, gathered.at[place(i)], in_sems.at[i])
+        for i, ref in enumerate(chunks)
     ]
-    for copy in loads:
+    weight_loads = [
+        pltpu.make_async_copy(weights_here.at[i], weights.at[i], weight_sems.at[i])
+        for i in range(rows // 2)
+    ]
+    for copy in loads + weight_loads:
         copy.start()
     dense[...] = jnp.zeros_like(dense)
     for copy in loads:
@@ -110,9 +101,12 @@
     for row in range(rows):
         for k in range(blocks):
             kept[row, :, k * 128 : (k + 1) * 128] = gathered[idx[row * blocks + k]]
-    for row in range(rows):
-        weights = weight_refs[row // 2].at[row % 2]
-        both = jnp.dot(kept[row, :, :flat], weights[...], preferred_element_type=F32)
+    order = [2, 3, 0, 1]
+    for row in order:
+        if row < 2:
+            weight_loads[row].wait()
+        matrix = weights[row] if row < 2 else weights_there[row - 2]
+        both = jnp.dot(kept[row, :, :flat], matrix, preferred_element_type=F32)
         gate = both[:, :128]
         upper = both[:, 128:]
         sigma = jax.nn.sigmoid(gate)
@@ -121,11 +115,11 @@
         dgate = gradf * upper * sigma * (1.0 + gate * (1.0 - sigma))
         dup = gradf * gate * sigma
         kept[row, :, flat:] = jnp.concatenate([dgate, dup], axis=1).astype(BF)
-    for row in range(rows):
-        weights = weight_refs[row // 2].at[row % 2]
+    for row in order:
+        matrix = weights[row] if row < 2 else weights_there[row - 2]
         partial = lax.dot_general(
             kept[row, :, flat:],
-            weights[...],
+            matrix,
             (((1,), (1,)), ((), ())),
             preferred_element_type=F32,
         ).astype(BF)
@@ -133,29 +127,26 @@
             span = range(start, min(start + 6, blocks))
             values = [partial[:, k * 128 : (k + 1) * 128] for k in span]
             places_of = [idx[row * blocks + k] for k in span]
-            if row >= rows // 2:
+            if row < 2:
                 values = [
                     (dense[at].astype(F32) + value.astype(F32)).astype(BF)
                     for at, value in zip(places_of, values)
                 ]
             for at, value in zip(places_of, values):
                 dense[at] = value
-    own, to31, to2, to4_low, to4_high, to57, to6 = terms
+    own, to31, to57, to4, to2, to6 = terms
     pieces = [
-        (to31.at[pl.ds(0, side)], 3),
-        (to57.at[pl.ds(0, side)], 6),
-        (to4_low, 4),
-        (to4_high, 5),
-        (to31.at[pl.ds(side, side)], 1),
-        (to57.at[pl.ds(side, side)], 8),
-        (to2, 2),
-        (to6, 7),
-        (own, 0),
+        (to31.at[place(0)], place(3)),
+        (to57.at[place(0)], place(5)),
+        (to4, place(4)),
+        (to31.at[place(1)], place(1)),
+        (to57.at[place(1)], place(7)),
+        (to2, place(2)),
+        (to6, place(6)),
+        (own, place(0)),
     ]
     stores = [
-        pltpu.make_async_copy(
-            dense.at[pl.ds(places[at][0], places[at][1])], ref, out_sems.at[i]
-        )
+        pltpu.make_async_copy(dense.at[at], ref, out_sems.at[i])
         for i, (ref, at) in enumerate(pieces)
     ]
     for copy in stores:
@@ -174,9 +165,9 @@
                     x * part : (x + 1) * part
                 ]
         for row in range(2):
-            for side in range(2):
-                value = kept[2 * pair + row, :, flat + side * 128 : flat + (side + 1) * 128]
-                at = blocks * part + (2 * row + side) * tokens
+            for wing in range(2):
+                value = kept[2 * pair + row, :, flat + wing * 128 : flat + (wing + 1) * 128]
+                at = blocks * part + (2 * row + wing) * tokens
                 for x in range(shards):
                     packed[pair * shards + x, at : at + tokens, :] = value
         copy = pltpu.make_async_copy(
@@ -198,31 +189,40 @@
     scalars = pl.BlockSpec(memory_space=pltpu.SMEM)
     side = chunks[0].shape[0]
     total = SIDE * side
-    lengths = (side, 2 * side, side, side // 2, side // 2, 2 * side, side)
+    lengths = (side, 2 * side, 2 * side, side, side, side)
     packed = (2 * shards, flat // shards + 4 * tokens, 128)
     return pl.pallas_call(
         block_kernel,
-        in_specs=[scalars] * 2 + [outside] * 9 + [whole] * 3,
-        out_specs=[whole] + [outside] * 8,
+        in_specs=[scalars] * 2 + [outside] * 9 + [whole] * 2,
+        out_specs=[whole] + [outside] * 7,
         out_shape=[jax.ShapeDtypeStruct((rows, tokens, 128), BF)]
-        + [jax.ShapeDtypeStruct((n,) + chunks[0].shape[1:], BF) for n in lengths]
-        + [jax.ShapeDtypeStruct(packed, BF)],
+        + [pltpu.HBM((n,) + chunks[0].shape[1:], BF) for n in lengths]
+        + [pltpu.HBM(packed, BF)],
         scratch_shapes=[
             pltpu.VMEM((total, tokens, 128), BF),
             pltpu.VMEM((total, tokens, 128), BF),
             pltpu.VMEM((rows, tokens, flat + 256), BF),
             pltpu.VMEM(packed, BF),
-            pltpu.SemaphoreType.DMA((9,)),
-            pltpu.SemaphoreType.DMA((9,)),
+            pltpu.VMEM(weights.shape, BF),
+            pltpu.SemaphoreType.DMA((8,)),
+            pltpu.SemaphoreType.DMA((8,)),
+            pltpu.SemaphoreType.DMA((2,)),
             pltpu.SemaphoreType.DMA((2,)),
         ],
-        compiler_params=pltpu.CompilerParams(vmem_limit_bytes=56 * 1024 * 1024),
+        compiler_params=pltpu.CompilerParams(vmem_limit_bytes=40 * 1024 * 1024),
         cost_estimate=pl.CostEstimate(
             flops=4 * rows * tokens * flat * 256,
             bytes_accessed=2 * rows * flat * 256 + 4 * total * tokens * 128,
             transcendentals=rows * tokens * 128,
         ),
-    )(core, idx, *chunks, weights, other_weights, grads)
+    )(
+        core,
+        idx,
+        *chunks,
+        pltpu.with_memory_space_constraint(weights, pltpu.HBM),
+        other_weights,
+        grads,
+    )
 
 
 def weight_kernel(scale, packed, out, total, right):
@@ -283,20 +283,19 @@
     other = me + 1 - 2 * core
     first = core == 0
 
-    def choose(value, mine):
-        low, high = value[:half], value[half:]
-        return jnp.where(first == mine, low, high)
-
     def split(value):
         return jnp.transpose(value.reshape(half, owned, width), (1, 0, 2))
 
     with jax.named_scope("swap_tokens"):
-        came = swap_cores(jnp.stack([choose(hidden, False), choose(cotangent, False)]))
-        mine, theirs = split(choose(hidden, True)), split(came[0])
+        both = jnp.stack([hidden, cotangent])
+        low, high = both[:, :half], both[:, half:]
+        came = swap_cores(jnp.where(first, high, low))
+        stays = jnp.where(first, low, high)
+        mine, theirs = split(stays[0]), split(came[0])
         chip_blocks = jnp.where(
             first, jnp.concatenate([mine, theirs]), jnp.concatenate([theirs, mine])
         )
-        grads = jnp.concatenate([split(choose(cotangent, True)), split(came[1])])
+        grads = jnp.concatenate([split(stays[1]), split(came[1])])
     with jax.named_scope("gather_near"):
         near = near_exchange(jnp.broadcast_to(chip_blocks[None], (SIDE,) + chip_blocks.shape))
         near = near.reshape(SIDE * 2 * owned, half, width)
@@ -318,7 +317,8 @@
         chip, inside = source // (2 * owned), source % (2 * owned)
         chip_y, chip_z = chip // SIDE, chip % SIDE
         my_y, my_z = me // (2 * SIDE), me // 2 % SIDE
-        distance = jnp.where(first, chip_z - my_z, chip_y - my_y) % SIDE
+        far = jnp.where(first, my_z, my_y)
+        distance = (jnp.where(first, chip_z, chip_y) - far) * (1 - 2 * (far % 2)) % SIDE
         place = distance * SIDE + jnp.where(first, chip_y, chip_z)
         idx = (place * (2 * owned) + inside).reshape(-1)
 
@@ -351,6 +351,7 @@
         weight_grad = run_weights(packed, per_row, width // shards, scale)
         pieces = near_exchange(column.reshape(SIDE, 2 * owned * half, width))
         total = jnp.sum(pieces.astype(F32), axis=0).astype(BF)
+        total, weight_grad = lax.optimization_barrier((total, weight_grad))
         total = total.reshape(2, owned, half, width)
     with jax.named_scope("swap_back"):
         keep = jnp.where(first, total[0], total[1])

time: 168 us -> 157 us (0.935)
  starting transfers between devices: 85.7 us -> 75.2 us
  waiting for transfers between devices: 33.1 us -> 40.7 us
  local copies, waits for them, and re-layouts: 7.38 us -> 3.92 us
  other arithmetic: 9.44 us -> 6.36 us
  Pallas kernels: 13.8 us -> 11.9 us
    ppermute x14 -> x12, waiting for transfers between devices: 25.1 us -> 33.9 us  [far_shift(): return lax.ppermute(value, 'blk', pairs)]
    ppermute x14 -> x12, starting transfers between devices: 50.4 us -> 41.9 us  [far_shift(): return lax.ppermute(value, 'blk', pairs)]
    slice x3 -> x2, local copies, waits for them, and re-layouts: 3.34 us -> 0.01 us  [local(): grads = jnp.concatenate([split(stays[1]), split(came[1])])]
    pallas_call x1, Pallas kernels: 11.8 us -> 9.95 us  [run_blocks(): pl.pallas_call(block_kernel, in_specs=[scalars] * 2 + [outside] * 9 + [wh...]
    convert_element_type x3 -> x2, other arithmetic: 4.99 us -> 3.89 us  [add(): return sum((value.astype(F32) for value in values)).astype(BF)]
  transfers between devices with their start and end apart: 20 -> 18, of which waited for: 10 -> 10; matrix products, arithmetic and copies ran while one was open for 7% -> 5% of each run, Pallas kernels for 1% -> 1%
where the time goes in v3:
time: 157 us; the launch traced here: 156 us
  starting transfers between devices  75.2 us (48%)
  waiting for transfers between devices  40.7 us (26%)
  blocking collectives  16.7 us (11%)
  Pallas kernels  11.9 us (8%)
  other arithmetic  6.36 us (4%)
  local copies, waits for them, and re-layouts  3.92 us (2%)
    ppermute x12, starting transfers between devices, far_shift(): return lax.ppermute(value, 'blk', pairs)  41.9 us
    ppermute x12, waiting for transfers between devices, far_shift(): return lax.ppermute(value, 'blk', pairs)  33.9 us
    ppermute x4, starting transfers between devices, swap_cores(): return lax.ppermute(value, 'blk', SWAP)  20.2 us
    all_to_all x1, blocking collectives, near_exchange(): lax.all_to_all(value, 'blk', 0, 0, axis_index_groups=GROUPS_NEAR, tiled=T...  16.7 us
    pallas_call x1, Pallas kernels, run_blocks(): pl.pallas_call(block_kernel, in_specs=[scalars] * 2 + [outside] * 9 + [wh...  9.95 us
    all_to_all x1, starting transfers between devices, local(): lax.all_to_all(packed, BOTH, 0, 0, axis_index_groups=groups, tiled=True)  9.64 us
    all_to_all x1, waiting for transfers between devices, near_exchange(): lax.all_to_all(value, 'blk', 0, 0, axis_index_groups=GROUPS_NEAR, tiled=T...  5.04 us
    convert_element_type x2, other arithmetic, add(): return sum((value.astype(F32) for value in values)).astype(BF)  3.89 us
  transfers between devices with their start and end apart: 18, of which 10 were waited for; matrix products, arithmetic and copies ran while one was open for 5% of the time, Pallas kernels for 1%

profile of v3, /device:TPU:1, one launch (start us, length us, event | category | flops | bytes accessed | tf_op | source)
XLA Modules:
  0.0 155.9 jit_solution(15853843083172446701)
XLA Ops:
  1.5 8.8 %collective-permute-start = (bf16[2,64,256]{2,1,0:T(8,128)(2,1)S(1)}, bf16[2,64,256]{2,1,0:T(8,128)(2,1)S(1)}, u32[]{:S(2)}, u32[]{:S(2)}) collective-permute-start(bf16[2,64,256]{2,1,0:T(8,128)(2,1)S(1)} %get-tuple-element.33), channel_id=1, source_target_pairs={{0,4},{4,0},{8,12},{12,8},{16,20},{20,16},{24,28},{28,24},{32,36},... | collective-permute-start | bytes 196616 | tf_op jit(solution)/shard_map/swap_tokens/ppermute | solution.py:39
  11.5 16.7 %all_to_all.15 = bf16[8,4,64,128]{3,2,1,0:T(8,128)(2,1)} all-to-all(bf16[8,4,64,128]{3,2,1,0:T(8,128)(2,1)S(1)} %broadcast_in_dim.23), channel_id=1, replica_groups={{0,64,128,192,256,320,384,448},{8,72,136,200,264,328,392,456},{16,80,14..., dimensions={0} | all-to-all | bytes 1048576 | tf_op jit(solution)/shard_map/gather_near/all_to_all | solution.py:43
  30.1 4.2 %collective-permute-start.3 = (bf16[32,64,128]{2,1,0:T(8,128)(2,1)}, bf16[32,64,128]{2,1,0:T(8,128)(2,1)}, u32[]{:S(2)}, u32[]{:S(2)}) collective-permute-start(bf16[32,64,128]{2,1,0:T(8,128)(2,1)} %bitcast.5.refs_0_), channel_id=1, source_target_pairs={{0,16},{4,132},{8,56},{12,140},{16,32},{20,148},{24,8},{28,156},{3... | collective-permute-start | bytes 1572872 | tf_op jit(solution)/shard_map/gather_far/ppermute | solution.py:35
  34.4 4.6 %collective-permute-start.7 = (bf16[32,64,128]{2,1,0:T(8,128)(2,1)}, bf16[32,64,128]{2,1,0:T(8,128)(2,1)}, u32[]{:S(2)}, u32[]{:S(2)}) collective-permute-start(bf16[32,64,128]{2,1,0:T(8,128)(2,1)} %bitcast.5.refs_0_), channel_id=1, source_target_pairs={{0,56},{4,452},{8,16},{12,460},{16,8},{20,468},{24,32},{28,476},{3... | collective-permute-start | bytes 1572872 | tf_op jit(solution)/shard_map/gather_far/ppermute | solution.py:35
  39.0 2.9 %collective-permute-start.2 = (bf16[32,64,128]{2,1,0:T(8,128)(2,1)}, bf16[32,64,128]{2,1,0:T(8,128)(2,1)}, u32[]{:S(2)}, u32[]{:S(2)}) collective-permute-start(bf16[32,64,128]{2,1,0:T(8,128)(2,1)} %bitcast.5.refs_0_), channel_id=1, source_target_pairs={{0,48},{4,388},{8,24},{12,396},{16,0},{20,404},{24,40},{28,412},{3... | collective-permute-start | bytes 1572872 | tf_op jit(solution)/shard_map/gather_far/ppermute | solution.py:35
  44.6 2.5 %collective-permute-start.1 = (bf16[32,64,128]{2,1,0:T(8,128)(2,1)}, bf16[32,64,128]{2,1,0:T(8,128)(2,1)}, u32[]{:S(2)}, u32[]{:S(2)}) collective-permute-start(bf16[32,64,128]{2,1,0:T(8,128)(2,1)} %bitcast.5.refs_0_), channel_id=1, source_target_pairs={{0,8},{4,68},{8,0},{12,76},{16,24},{20,84},{24,16},{28,92},{32,40}... | collective-permute-start | bytes 1572872 | tf_op jit(solution)/shard_map/gather_far/ppermute | solution.py:35
  47.1 2.7 %collective-permute-start.5 = (bf16[32,64,128]{2,1,0:T(8,128)(2,1)}, bf16[32,64,128]{2,1,0:T(8,128)(2,1)}, u32[]{:S(2)}, u32[]{:S(2)}) collective-permute-start(bf16[32,64,128]{2,1,0:T(8,128)(2,1)} %collective-permute-done.3.refs_6_), channel_id=1, source_target_pairs={{0,16},{4,132},{8,56},{12,140},{16,32},{20,148},{24,8},{28,156},{3... | collective-permute-start | bytes 1572872 | tf_op jit(solution)/shard_map/gather_far/ppermute | solution.py:35
  49.9 4.2 %collective-permute-start.4 = (bf16[32,64,128]{2,1,0:T(8,128)(2,1)}, bf16[32,64,128]{2,1,0:T(8,128)(2,1)}, u32[]{:S(2)}, u32[]{:S(2)}) collective-permute-start(bf16[32,64,128]{2,1,0:T(8,128)(2,1)} %collective-permute-done.3.refs_6_), channel_id=1, source_target_pairs={{0,8},{4,68},{8,0},{12,76},{16,24},{20,84},{24,16},{28,92},{32,40}... | collective-permute-start | bytes 1572872 | tf_op jit(solution)/shard_map/gather_far/ppermute | solution.py:35
  54.1 4.7 %collective-permute-start.6 = (bf16[32,64,128]{2,1,0:T(8,128)(2,1)}, bf16[32,64,128]{2,1,0:T(8,128)(2,1)}, u32[]{:S(2)}, u32[]{:S(2)}) collective-permute-start(bf16[32,64,128]{2,1,0:T(8,128)(2,1)} %collective-permute-done.2.refs_2_), channel_id=1, source_target_pairs={{0,56},{4,452},{8,16},{12,460},{16,8},{20,468},{24,32},{28,476},{3... | collective-permute-start | bytes 1572872 | tf_op jit(solution)/shard_map/gather_far/ppermute | solution.py:35
  59.4 8.3 %collective-permute-done.5.refs_4_ = bf16[32,64,128]{2,1,0:T(8,128)(2,1)} collective-permute-done((bf16[32,64,128]{2,1,0:T(8,128)(2,1)}, bf16[32,64,128]{2,1,0:T(8,128)(2,1)}, u32[]{:S(2)}, u32[]{:S(2)}) %collective-permute-start.5) | collective-permute-done | bytes 524320 | tf_op jit(solution)/shard_map/gather_far/ppermute | solution.py:35
  67.8 2.9 %collective-permute-done.4.refs_3_ = bf16[32,64,128]{2,1,0:T(8,128)(2,1)} collective-permute-done((bf16[32,64,128]{2,1,0:T(8,128)(2,1)}, bf16[32,64,128]{2,1,0:T(8,128)(2,1)}, u32[]{:S(2)}, u32[]{:S(2)}) %collective-permute-start.4) | collective-permute-done | bytes 524320 | tf_op jit(solution)/shard_map/gather_far/ppermute | solution.py:35
  71.5 10.0 %blocks.1 = (bf16[4,64,128]{2,1,0:T(8,128)(2,1)S(1)}, bf16[32,64,128]{2,1,0:T(8,128)(2,1)}, bf16[64,64,128]{2,1,0:T(8,128)(2,1)}, bf16[64,64,128]{2,1,0:T(8,128)...) custom-call(s32[1]{0:T(128)} %bitcast.core, ...), custom_call_target="tpu_custom_call" | custom-call | flops 872415232 | bytes 15204352 | tf_op jit(solution)/shard_map/blocks/pallas_call | solution.py:194
  81.5 2.9 %collective-permute-start.10 = (bf16[64,64,128]{2,1,0:T(8,128)(2,1)}, bf16[64,64,128]{2,1,0:T(8,128)(2,1)S(1)}, u32[]{:S(2)}, u32[]{:S(2)}) collective-permute-start(bf16[64,64,128]{2,1,0:T(8,128)(2,1)} %get-tuple-element.19), channel_id=1, source_target_pairs={{0,8},{4,68},{8,0},{12,76},{16,24},{20,84},{24,16},{28,92},{32,40}... | collective-permute-start | bytes 3145736 | tf_op jit(solution)/shard_map/reduce_far/ppermute | solution.py:35
  84.4 3.9 %collective-permute-start.11 = (bf16[64,64,128]{2,1,0:T(8,128)(2,1)}, bf16[64,64,128]{2,1,0:T(8,128)(2,1)}, u32[]{:S(2)}, u32[]{:S(2)}) collective-permute-start(bf16[64,64,128]{2,1,0:T(8,128)(2,1)} %get-tuple-element.20), channel_id=1, source_target_pairs={{0,56},{4,452},{8,16},{12,460},{16,8},{20,468},{24,32},{28,476},{3... | collective-permute-start | bytes 3145736 | tf_op jit(solution)/shard_map/reduce_far/ppermute | solution.py:35
  88.3 9.6 %all-to-all-start.1 = ((bf16[8,1088,128]{2,1,0:T(8,128)(2,1)}), bf16[8,1088,128]{2,1,0:T(8,128)(2,1)S(1)}, u32[]{:S(2)}, u32[]{:S(2)}) async-start(bf16[8,1088,128]{2,1,0:T(8,128)(2,1)} %get-tuple-element.24), calls=%async_computation.1 | async-start | bytes 4456448 | tf_op jit(solution)/shard_map/weight_grad/all_to_all | solution.py:347
  99.9 10.6 %collective-permute-done.12 = bf16[32,64,128]{2,1,0:T(8,128)(2,1)S(1)} collective-permute-done((bf16[32,64,128]{2,1,0:T(8,128)(2,1)}, bf16[32,64,128]{2,1,0:T(8,128)(2,1)S(1)}, u32[]{:S(2)}, u32[]{:S(2)}) %collective-permute-start.12) | collective-permute-done | bytes 524320 | tf_op jit(solution)/shard_map/reduce_far/ppermute | solution.py:35
  111.5 2.9 %add_convert_fusion.2 = (bf16[32,64,128]{2,1,0:T(8,128)(2,1)S(1)}, f32[32,64,128]{2,1,0:T(8,128)S(1)}, bf16[32,64,128]{2,1,0:T(8,128)(2,1)S(1)}) fusion(bf16[32,64,128]{2,1,0:T(8,128)(2,1)S(1)} %collective-permute-done.12, bf16[32,64,128]{2,1,0:T(8,128)(2,1)} %get-tuple-element.21, bf16[64,64,128]{2,1,0:T(8,128)(2,1)} %collective-permute-done.11, ...), kind=kLoop, calls=%fused_computation.2 | loop fusion | flops 3932160 | bytes 6291456 | tf_op jit(solution)/shard_map/reduce_far/convert_element_type | solution.py:64
  116.3 5.5 %collective-permute-start.14 = (bf16[32,64,128]{2,1,0:T(8,128)(2,1)S(1)}, bf16[32,64,128]{2,1,0:T(8,128)(2,1)S(1)}, u32[]{:S(2)}, u32[]{:S(2)}) collective-permute-start(bf16[32,64,128]{2,1,0:T(8,128)(2,1)S(1)} %get-tuple-element.31), channel_id=1, source_target_pairs={{0,48},{4,388},{8,24},{12,396},{16,0},{20,404},{24,40},{28,412},{3... | collective-permute-start | bytes 1572872 | tf_op jit(solution)/shard_map/reduce_far/ppermute | solution.py:35
  121.8 10.5 %collective-permute-done.13 = bf16[32,64,128]{2,1,0:T(8,128)(2,1)S(1)} collective-permute-done((bf16[32,64,128]{2,1,0:T(8,128)(2,1)S(1)}, bf16[32,64,128]{2,1,0:T(8,128)(2,1)S(1)}, u32[]{:S(2)}, u32[]{:S(2)}) %collective-permute-start.13) | collective-permute-done | bytes 524320 | tf_op jit(solution)/shard_map/reduce_far/ppermute | solution.py:35
  133.3 3.5 %all-to-all-start.2 = ((bf16[8,256,128]{2,1,0:T(8,128)(2,1)}), bf16[8,256,128]{2,1,0:T(8,128)(2,1)S(1)}, u32[]{:S(2)}, u32[]{:S(2)}) async-start(bf16[8,256,128]{2,1,0:T(8,128)(2,1)} %bitcast.39), calls=%async_computation.2 | async-start | bytes 1048576 | tf_op jit(solution)/shard_map/reduce_near/all_to_all | solution.py:43
  136.8 4.2 %collective-permute-start.9 = (bf16[2,64,128]{2,1,0:T(8,128)(2,1)S(1)}, bf16[2,64,128]{2,1,0:T(8,128)(2,1)S(1)}, u32[]{:S(2)}, u32[]{:S(2)}) collective-permute-start(bf16[2,64,128]{2,1,0:T(8,128)(2,1)S(1)} %slice.53), channel_id=1, source_target_pairs={{0,4},{4,0},{8,12},{12,8},{16,20},{20,16},{24,28},{28,24},{32,36},... | collective-permute-start | bytes 98312 | tf_op jit(solution)/shard_map/swap_back/ppermute | solution.py:39
  141.9 2.0 %reduce_near.1 = bf16[2,26,32,256]{3,2,1,0:T(8,128)(2,1)} custom-call(bf16[8,1088,128]{2,1,0:T(8,128)(2,1)S(1)} %all-to-all-done.1.refs_0_), custom_call_target="tpu_custom_call" | custom-call | flops 872415232 | bytes 3080192 | tf_op jit(solution)/shard_map/reduce_near/pallas_call | solution.py:257
  143.9 5.0 %all-to-all-done.2 = bf16[8,256,128]{2,1,0:T(8,128)(2,1)S(1)} async-done(((bf16[8,256,128]{2,1,0:T(8,128)(2,1)}), bf16[8,256,128]{2,1,0:T(8,128)(2,1)S(1)}, u32[]{:S(2)}, u32[]{:S(2)}) %all-to-all-start.2) | async-done | bytes 524320 | tf_op jit(solution)/shard_map/reduce_near/all_to_all | solution.py:43
  149.0 5.3 %collective-permute-start.15 = (bf16[2,64,128]{2,1,0:T(8,128)(2,1)S(1)}, bf16[2,64,128]{2,1,0:T(8,128)(2,1)S(1)}, u32[]{:S(2)}, u32[]{:S(2)}) collective-permute-start(bf16[2,64,128]{2,1,0:T(8,128)(2,1)S(1)} %bitcast.49), channel_id=1, source_target_pairs={{0,4},{4,0},{8,12},{12,8},{16,20},{20,16},{24,28},{28,24},{32,36},... | collective-permute-start | bytes 98312 | tf_op jit(solution)/shard_map/swap_back/ppermute | solution.py:39
  (51 shorter events, 16.4 us)
Async XLA Ops:
  1.5 9.7 %collective-permute-start = (bf16[2,64,256]{2,1,0:T(8,128)(2,1)S(1)}, bf16[2,64,256]{2,1,0:T(8,128)(2,1)S(1)}, u32[]{:S(2)}, u32[]{:S(2)}) collective-permute-start(bf16[2,64,256]{2,1,0:T(8,128)(2,1)S(1)} %get-tuple-element.33), channel_id=1, source_target_pairs={{0,4},{4,0},{8,12},{12,8},{16,20},{20,16},{24,28},{28,24},{32,36},... | collective-permute-start | bytes 196616 | tf_op jit(solution)/shard_map/swap_tokens/ppermute | solution.py:39
  28.2 43.3 %collective-permute-start.8 = (bf16[2,26,128,256]{3,2,1,0:T(8,128)(2,1)}, bf16[2,26,128,256]{3,2,1,0:T(8,128)(2,1)S(1)}, u32[]{:S(2)}, u32[]{:S(2)}) collective-permute-start(bf16[2,26,128,256]{3,2,1,0:T(8,128)(2,1)} %param.6), channel_id=1, source_target_pairs={{0,4},{4,0},{8,12},{12,8},{16,20},{20,16},{24,28},{28,24},{32,36},... | collective-permute-start | bytes 10223624 | tf_op jit(solution)/shard_map/swap_weights/ppermute | solution.py:39
  30.1 17.0 %collective-permute-start.3 = (bf16[32,64,128]{2,1,0:T(8,128)(2,1)}, bf16[32,64,128]{2,1,0:T(8,128)(2,1)}, u32[]{:S(2)}, u32[]{:S(2)}) collective-permute-start(bf16[32,64,128]{2,1,0:T(8,128)(2,1)} %bitcast.5.refs_0_), channel_id=1, source_target_pairs={{0,16},{4,132},{8,56},{12,140},{16,32},{20,148},{24,8},{28,156},{3... | collective-permute-start | bytes 1572872 | tf_op jit(solution)/shard_map/gather_far/ppermute | solution.py:35
  34.4 15.5 %collective-permute-start.7 = (bf16[32,64,128]{2,1,0:T(8,128)(2,1)}, bf16[32,64,128]{2,1,0:T(8,128)(2,1)}, u32[]{:S(2)}, u32[]{:S(2)}) collective-permute-start(bf16[32,64,128]{2,1,0:T(8,128)(2,1)} %bitcast.5.refs_0_), channel_id=1, source_target_pairs={{0,56},{4,452},{8,16},{12,460},{16,8},{20,468},{24,32},{28,476},{3... | collective-permute-start | bytes 1572872 | tf_op jit(solution)/shard_map/gather_far/ppermute | solution.py:35
  39.0 15.0 %collective-permute-start.2 = (bf16[32,64,128]{2,1,0:T(8,128)(2,1)}, bf16[32,64,128]{2,1,0:T(8,128)(2,1)}, u32[]{:S(2)}, u32[]{:S(2)}) collective-permute-start(bf16[32,64,128]{2,1,0:T(8,128)(2,1)} %bitcast.5.refs_0_), channel_id=1, source_target_pairs={{0,48},{4,388},{8,24},{12,396},{16,0},{20,404},{24,40},{28,412},{3... | collective-permute-start | bytes 1572872 | tf_op jit(solution)/shard_map/gather_far/ppermute | solution.py:35
  44.6 14.9 %collective-permute-start.1 = (bf16[32,64,128]{2,1,0:T(8,128)(2,1)}, bf16[32,64,128]{2,1,0:T(8,128)(2,1)}, u32[]{:S(2)}, u32[]{:S(2)}) collective-permute-start(bf16[32,64,128]{2,1,0:T(8,128)(2,1)} %bitcast.5.refs_0_), channel_id=1, source_target_pairs={{0,8},{4,68},{8,0},{12,76},{16,24},{20,84},{24,16},{28,92},{32,40}... | collective-permute-start | bytes 1572872 | tf_op jit(solution)/shard_map/gather_far/ppermute | solution.py:35
  47.1 20.6 %collective-permute-start.5 = (bf16[32,64,128]{2,1,0:T(8,128)(2,1)}, bf16[32,64,128]{2,1,0:T(8,128)(2,1)}, u32[]{:S(2)}, u32[]{:S(2)}) collective-permute-start(bf16[32,64,128]{2,1,0:T(8,128)(2,1)} %collective-permute-done.3.refs_6_), channel_id=1, source_target_pairs={{0,16},{4,132},{8,56},{12,140},{16,32},{20,148},{24,8},{28,156},{3... | collective-permute-start | bytes 1572872 | tf_op jit(solution)/shard_map/gather_far/ppermute | solution.py:35
  49.9 20.9 %collective-permute-start.4 = (bf16[32,64,128]{2,1,0:T(8,128)(2,1)}, bf16[32,64,128]{2,1,0:T(8,128)(2,1)}, u32[]{:S(2)}, u32[]{:S(2)}) collective-permute-start(bf16[32,64,128]{2,1,0:T(8,128)(2,1)} %collective-permute-done.3.refs_6_), channel_id=1, source_target_pairs={{0,8},{4,68},{8,0},{12,76},{16,24},{20,84},{24,16},{28,92},{32,40}... | collective-permute-start | bytes 1572872 | tf_op jit(solution)/shard_map/gather_far/ppermute | solution.py:35
  54.1 17.4 %collective-permute-start.6 = (bf16[32,64,128]{2,1,0:T(8,128)(2,1)}, bf16[32,64,128]{2,1,0:T(8,128)(2,1)}, u32[]{:S(2)}, u32[]{:S(2)}) collective-permute-start(bf16[32,64,128]{2,1,0:T(8,128)(2,1)} %collective-permute-done.2.refs_2_), channel_id=1, source_target_pairs={{0,56},{4,452},{8,16},{12,460},{16,8},{20,468},{24,32},{28,476},{3... | collective-permute-start | bytes 1572872 | tf_op jit(solution)/shard_map/gather_far/ppermute | solution.py:35
  81.5 29.0 %collective-permute-start.10 = (bf16[64,64,128]{2,1,0:T(8,128)(2,1)}, bf16[64,64,128]{2,1,0:T(8,128)(2,1)S(1)}, u32[]{:S(2)}, u32[]{:S(2)}) collective-permute-start(bf16[64,64,128]{2,1,0:T(8,128)(2,1)} %get-tuple-element.19), channel_id=1, source_target_pairs={{0,8},{4,68},{8,0},{12,76},{16,24},{20,84},{24,16},{28,92},{32,40}... | collective-permute-start | bytes 3145736 | tf_op jit(solution)/shard_map/reduce_far/ppermute | solution.py:35
  84.4 26.1 %collective-permute-start.11 = (bf16[64,64,128]{2,1,0:T(8,128)(2,1)}, bf16[64,64,128]{2,1,0:T(8,128)(2,1)}, u32[]{:S(2)}, u32[]{:S(2)}) collective-permute-start(bf16[64,64,128]{2,1,0:T(8,128)(2,1)} %get-tuple-element.20), channel_id=1, source_target_pairs={{0,56},{4,452},{8,16},{12,460},{16,8},{20,468},{24,32},{28,476},{3... | collective-permute-start | bytes 3145736 | tf_op jit(solution)/shard_map/reduce_far/ppermute | solution.py:35
  88.3 45.0 %all-to-all-start.1 = ((bf16[8,1088,128]{2,1,0:T(8,128)(2,1)}), bf16[8,1088,128]{2,1,0:T(8,128)(2,1)S(1)}, u32[]{:S(2)}, u32[]{:S(2)}) async-start(bf16[8,1088,128]{2,1,0:T(8,128)(2,1)} %get-tuple-element.24), calls=%async_computation.1 | async-start | bytes 4456448 | tf_op jit(solution)/shard_map/weight_grad/all_to_all | solution.py:347
  98.0 12.5 %collective-permute-start.12 = (bf16[32,64,128]{2,1,0:T(8,128)(2,1)}, bf16[32,64,128]{2,1,0:T(8,128)(2,1)S(1)}, u32[]{:S(2)}, u32[]{:S(2)}) collective-permute-start(bf16[32,64,128]{2,1,0:T(8,128)(2,1)} %get-tuple-element.22), channel_id=1, source_target_pairs={{0,16},{4,132},{8,56},{12,140},{16,32},{20,148},{24,8},{28,156},{3... | collective-permute-start | bytes 1572872 | tf_op jit(solution)/shard_map/reduce_far/ppermute | solution.py:35
  110.5 1.0 copy-start
  114.3 17.9 %collective-permute-start.13 = (bf16[32,64,128]{2,1,0:T(8,128)(2,1)S(1)}, bf16[32,64,128]{2,1,0:T(8,128)(2,1)S(1)}, u32[]{:S(2)}, u32[]{:S(2)}) collective-permute-start(bf16[32,64,128]{2,1,0:T(8,128)(2,1)S(1)} %get-tuple-element.29), channel_id=1, source_target_pairs={{0,16},{4,132},{8,56},{12,140},{16,32},{20,148},{24,8},{28,156},{3... | collective-permute-start | bytes 1572872 | tf_op jit(solution)/shard_map/reduce_far/ppermute | solution.py:35
  116.3 16.0 %collective-permute-start.14 = (bf16[32,64,128]{2,1,0:T(8,128)(2,1)S(1)}, bf16[32,64,128]{2,1,0:T(8,128)(2,1)S(1)}, u32[]{:S(2)}, u32[]{:S(2)}) collective-permute-start(bf16[32,64,128]{2,1,0:T(8,128)(2,1)S(1)} %get-tuple-element.31), channel_id=1, source_target_pairs={{0,48},{4,388},{8,24},{12,396},{16,0},{20,404},{24,40},{28,412},{3... | collective-permute-start | bytes 1572872 | tf_op jit(solution)/shard_map/reduce_far/ppermute | solution.py:35
  133.3 15.6 %all-to-all-start.2 = ((bf16[8,256,128]{2,1,0:T(8,128)(2,1)}), bf16[8,256,128]{2,1,0:T(8,128)(2,1)S(1)}, u32[]{:S(2)}, u32[]{:S(2)}) async-start(bf16[8,256,128]{2,1,0:T(8,128)(2,1)} %bitcast.39), calls=%async_computation.2 | async-start | bytes 1048576 | tf_op jit(solution)/shard_map/reduce_near/all_to_all | solution.py:43
  136.8 5.0 %collective-permute-start.9 = (bf16[2,64,128]{2,1,0:T(8,128)(2,1)S(1)}, bf16[2,64,128]{2,1,0:T(8,128)(2,1)S(1)}, u32[]{:S(2)}, u32[]{:S(2)}) collective-permute-start(bf16[2,64,128]{2,1,0:T(8,128)(2,1)S(1)} %slice.53), channel_id=1, source_target_pairs={{0,4},{4,0},{8,12},{12,8},{16,20},{20,16},{24,28},{28,24},{32,36},... | collective-permute-start | bytes 98312 | tf_op jit(solution)/shard_map/swap_back/ppermute | solution.py:39
  149.0 6.2 %collective-permute-start.15 = (bf16[2,64,128]{2,1,0:T(8,128)(2,1)S(1)}, bf16[2,64,128]{2,1,0:T(8,128)(2,1)S(1)}, u32[]{:S(2)}, u32[]{:S(2)}) collective-permute-start(bf16[2,64,128]{2,1,0:T(8,128)(2,1)S(1)} %bitcast.49), channel_id=1, source_target_pairs={{0,4},{4,0},{8,12},{12,8},{16,20},{20,16},{24,28},{28,24},{32,36},... | collective-permute-start | bytes 98312 | tf_op jit(solution)/shard_map/swap_back/ppermute | solution.py:39

commit v4 on v3

--- a/solution.py
+++ b/solution.py
@@ -63,8 +63,12 @@
     def add(*values):
         return sum(value.astype(F32) for value in values).astype(BF)
 
-    got6 = far_shift(add(to6, got31[:size]), -2)
-    got2 = far_shift(add(to2, got57[:size], got4), 2)
+    sum6 = add(to6, got31[:size])
+    to2, _ = lax.optimization_barrier((to2, sum6))
+    sum2 = add(to2, got57[:size], got4)
+    own, _ = lax.optimization_barrier((own, sum2))
+    got6 = far_shift(sum6, -2)
+    got2 = far_shift(sum2, 2)
     early = lax.optimization_barrier(
         own.astype(F32) + got31[size:].astype(F32) + got57[size:].astype(F32)
     )

time: 157 us -> 151 us (0.962)
  starting transfers between devices: 75.2 us -> 69.8 us
  other arithmetic: 6.36 us -> 8 us
    ppermute x4, starting transfers between devices: 20.2 us -> 14.5 us  [swap_cores(): return lax.ppermute(value, 'blk', SWAP)]
    ppermute x12, waiting for transfers between devices: 33.9 us -> 30.1 us  [far_shift(): return lax.ppermute(value, 'blk', pairs)]
    all_to_all x1, waiting for transfers between devices: 5.04 us -> 6.94 us  [near_exchange(): lax.all_to_all(value, 'blk', 0, 0, axis_index_groups=GROUPS_NEAR, tiled=T...]
    convert_element_type x2 -> x3, other arithmetic: 3.89 us -> 4.08 us  [add(): return sum((value.astype(F32) for value in values)).astype(BF)]
  transfers between devices with their start and end apart: 18 -> 18, of which waited for: 10 -> 10; matrix products, arithmetic and copies ran while one was open for 5% -> 6% of each run, Pallas kernels for 1% -> 1%
where the time goes in v4:
time: 151 us; the launch traced here: 150 us
  starting transfers between devices  69.8 us (46%)
  waiting for transfers between devices  39.5 us (26%)
  blocking collectives  16.7 us (11%)
  Pallas kernels  11.9 us (8%)
  other arithmetic  8 us (5%)
  local copies, waits for them, and re-layouts  2.96 us (2%)
    ppermute x12, starting transfers between devices, far_shift(): return lax.ppermute(value, 'blk', pairs)  42.1 us
    ppermute x12, waiting for transfers between devices, far_shift(): return lax.ppermute(value, 'blk', pairs)  30.1 us
    all_to_all x1, blocking collectives, near_exchange(): lax.all_to_all(value, 'blk', 0, 0, axis_index_groups=GROUPS_NEAR, tiled=T...  16.7 us
    ppermute x4, starting transfers between devices, swap_cores(): return lax.ppermute(value, 'blk', SWAP)  14.5 us
    pallas_call x1, Pallas kernels, run_blocks(): pl.pallas_call(block_kernel, in_specs=[scalars] * 2 + [outside] * 9 + [wh...  9.95 us
    all_to_all x1, starting transfers between devices, local(): lax.all_to_all(packed, BOTH, 0, 0, axis_index_groups=groups, tiled=True)  9.64 us
    all_to_all x1, waiting for transfers between devices, near_exchange(): lax.all_to_all(value, 'blk', 0, 0, axis_index_groups=GROUPS_NEAR, tiled=T...  6.94 us
    convert_element_type x3, other arithmetic, add(): return sum((value.astype(F32) for value in values)).astype(BF)  4.08 us
  transfers between devices with their start and end apart: 18, of which 10 were waited for; matrix products, arithmetic and copies ran while one was open for 6% of the time, Pallas kernels for 1%

profile of v4, /device:TPU:1, one launch (start us, length us, event | category | flops | bytes accessed | tf_op | source)
XLA Modules:
  0.0 150.0 jit_solution(4277170158853681308)
XLA Ops:
  1.5 8.8 %collective-permute-start = (bf16[2,64,256]{2,1,0:T(8,128)(2,1)S(1)}, bf16[2,64,256]{2,1,0:T(8,128)(2,1)S(1)}, u32[]{:S(2)}, u32[]{:S(2)}) collective-permute-start(bf16[2,64,256]{2,1,0:T(8,128)(2,1)S(1)} %get-tuple-element.34), channel_id=1, source_target_pairs={{0,4},{4,0},{8,12},{12,8},{16,20},{20,16},{24,28},{28,24},{32,36},... | collective-permute-start | bytes 196616 | tf_op jit(solution)/shard_map/swap_tokens/ppermute | solution.py:39
  11.5 16.7 %all_to_all.15 = bf16[8,4,64,128]{3,2,1,0:T(8,128)(2,1)} all-to-all(bf16[8,4,64,128]{3,2,1,0:T(8,128)(2,1)S(1)} %broadcast_in_dim.23), channel_id=1, replica_groups={{0,64,128,192,256,320,384,448},{8,72,136,200,264,328,392,456},{16,80,14..., dimensions={0} | all-to-all | bytes 1048576 | tf_op jit(solution)/shard_map/gather_near/all_to_all | solution.py:43
  30.1 4.2 %collective-permute-start.3 = (bf16[32,64,128]{2,1,0:T(8,128)(2,1)}, bf16[32,64,128]{2,1,0:T(8,128)(2,1)}, u32[]{:S(2)}, u32[]{:S(2)}) collective-permute-start(bf16[32,64,128]{2,1,0:T(8,128)(2,1)} %bitcast.5.refs_0_), channel_id=1, source_target_pairs={{0,16},{4,132},{8,56},{12,140},{16,32},{20,148},{24,8},{28,156},{3... | collective-permute-start | bytes 1572872 | tf_op jit(solution)/shard_map/gather_far/ppermute | solution.py:35
  34.4 4.6 %collective-permute-start.7 = (bf16[32,64,128]{2,1,0:T(8,128)(2,1)}, bf16[32,64,128]{2,1,0:T(8,128)(2,1)}, u32[]{:S(2)}, u32[]{:S(2)}) collective-permute-start(bf16[32,64,128]{2,1,0:T(8,128)(2,1)} %bitcast.5.refs_0_), channel_id=1, source_target_pairs={{0,56},{4,452},{8,16},{12,460},{16,8},{20,468},{24,32},{28,476},{3... | collective-permute-start | bytes 1572872 | tf_op jit(solution)/shard_map/gather_far/ppermute | solution.py:35
  39.0 2.9 %collective-permute-start.2 = (bf16[32,64,128]{2,1,0:T(8,128)(2,1)}, bf16[32,64,128]{2,1,0:T(8,128)(2,1)}, u32[]{:S(2)}, u32[]{:S(2)}) collective-permute-start(bf16[32,64,128]{2,1,0:T(8,128)(2,1)} %bitcast.5.refs_0_), channel_id=1, source_target_pairs={{0,48},{4,388},{8,24},{12,396},{16,0},{20,404},{24,40},{28,412},{3... | collective-permute-start | bytes 1572872 | tf_op jit(solution)/shard_map/gather_far/ppermute | solution.py:35
  44.6 2.5 %collective-permute-start.1 = (bf16[32,64,128]{2,1,0:T(8,128)(2,1)}, bf16[32,64,128]{2,1,0:T(8,128)(2,1)}, u32[]{:S(2)}, u32[]{:S(2)}) collective-permute-start(bf16[32,64,128]{2,1,0:T(8,128)(2,1)} %bitcast.5.refs_0_), channel_id=1, source_target_pairs={{0,8},{4,68},{8,0},{12,76},{16,24},{20,84},{24,16},{28,92},{32,40}... | collective-permute-start | bytes 1572872 | tf_op jit(solution)/shard_map/gather_far/ppermute | solution.py:35
  47.1 2.7 %collective-permute-start.5 = (bf16[32,64,128]{2,1,0:T(8,128)(2,1)}, bf16[32,64,128]{2,1,0:T(8,128)(2,1)}, u32[]{:S(2)}, u32[]{:S(2)}) collective-permute-start(bf16[32,64,128]{2,1,0:T(8,128)(2,1)} %collective-permute-done.3.refs_6_), channel_id=1, source_target_pairs={{0,16},{4,132},{8,56},{12,140},{16,32},{20,148},{24,8},{28,156},{3... | collective-permute-start | bytes 1572872 | tf_op jit(solution)/shard_map/gather_far/ppermute | solution.py:35
  49.9 4.2 %collective-permute-start.4 = (bf16[32,64,128]{2,1,0:T(8,128)(2,1)}, bf16[32,64,128]{2,1,0:T(8,128)(2,1)}, u32[]{:S(2)}, u32[]{:S(2)}) collective-permute-start(bf16[32,64,128]{2,1,0:T(8,128)(2,1)} %collective-permute-done.3.refs_6_), channel_id=1, source_target_pairs={{0,8},{4,68},{8,0},{12,76},{16,24},{20,84},{24,16},{28,92},{32,40}... | collective-permute-start | bytes 1572872 | tf_op jit(solution)/shard_map/gather_far/ppermute | solution.py:35
  54.1 4.7 %collective-permute-start.6 = (bf16[32,64,128]{2,1,0:T(8,128)(2,1)}, bf16[32,64,128]{2,1,0:T(8,128)(2,1)}, u32[]{:S(2)}, u32[]{:S(2)}) collective-permute-start(bf16[32,64,128]{2,1,0:T(8,128)(2,1)} %collective-permute-done.2.refs_2_), channel_id=1, source_target_pairs={{0,56},{4,452},{8,16},{12,460},{16,8},{20,468},{24,32},{28,476},{3... | collective-permute-start | bytes 1572872 | tf_op jit(solution)/shard_map/gather_far/ppermute | solution.py:35
  59.4 8.3 %collective-permute-done.5.refs_4_ = bf16[32,64,128]{2,1,0:T(8,128)(2,1)} collective-permute-done((bf16[32,64,128]{2,1,0:T(8,128)(2,1)}, bf16[32,64,128]{2,1,0:T(8,128)(2,1)}, u32[]{:S(2)}, u32[]{:S(2)}) %collective-permute-start.5) | collective-permute-done | bytes 524320 | tf_op jit(solution)/shard_map/gather_far/ppermute | solution.py:35
  67.8 2.9 %collective-permute-done.4.refs_3_ = bf16[32,64,128]{2,1,0:T(8,128)(2,1)} collective-permute-done((bf16[32,64,128]{2,1,0:T(8,128)(2,1)}, bf16[32,64,128]{2,1,0:T(8,128)(2,1)}, u32[]{:S(2)}, u32[]{:S(2)}) %collective-permute-start.4) | collective-permute-done | bytes 524320 | tf_op jit(solution)/shard_map/gather_far/ppermute | solution.py:35
  71.5 10.0 %blocks.1 = (bf16[4,64,128]{2,1,0:T(8,128)(2,1)S(1)}, bf16[32,64,128]{2,1,0:T(8,128)(2,1)}, bf16[64,64,128]{2,1,0:T(8,128)(2,1)}, bf16[64,64,128]{2,1,0:T(8,128)...) custom-call(s32[1]{0:T(128)} %bitcast.core, ...), custom_call_target="tpu_custom_call" | custom-call | flops 872415232 | bytes 15204352 | tf_op jit(solution)/shard_map/blocks/pallas_call | solution.py:198
  81.5 2.9 %collective-permute-start.10 = (bf16[64,64,128]{2,1,0:T(8,128)(2,1)}, bf16[64,64,128]{2,1,0:T(8,128)(2,1)S(1)}, u32[]{:S(2)}, u32[]{:S(2)}) collective-permute-start(bf16[64,64,128]{2,1,0:T(8,128)(2,1)} %get-tuple-element.23), channel_id=1, source_target_pairs={{0,8},{4,68},{8,0},{12,76},{16,24},{20,84},{24,16},{28,92},{32,40}... | collective-permute-start | bytes 3145736 | tf_op jit(solution)/shard_map/reduce_far/ppermute | solution.py:35
  84.4 3.9 %collective-permute-start.11 = (bf16[64,64,128]{2,1,0:T(8,128)(2,1)}, bf16[64,64,128]{2,1,0:T(8,128)(2,1)}, u32[]{:S(2)}, u32[]{:S(2)}) collective-permute-start(bf16[64,64,128]{2,1,0:T(8,128)(2,1)} %get-tuple-element.25), channel_id=1, source_target_pairs={{0,56},{4,452},{8,16},{12,460},{16,8},{20,468},{24,32},{28,476},{3... | collective-permute-start | bytes 3145736 | tf_op jit(solution)/shard_map/reduce_far/ppermute | solution.py:35
  88.3 9.6 %all-to-all-start.1 = ((bf16[8,1088,128]{2,1,0:T(8,128)(2,1)}), bf16[8,1088,128]{2,1,0:T(8,128)(2,1)S(1)}, u32[]{:S(2)}, u32[]{:S(2)}) async-start(bf16[8,1088,128]{2,1,0:T(8,128)(2,1)} %get-tuple-element.28), calls=%async_computation.1 | async-start | bytes 4456448 | tf_op jit(solution)/shard_map/weight_grad/all_to_all | solution.py:351
  98.0 2.0 %collective-permute-start.12 = (bf16[32,64,128]{2,1,0:T(8,128)(2,1)}, bf16[32,64,128]{2,1,0:T(8,128)(2,1)S(1)}, u32[]{:S(2)}, u32[]{:S(2)}) collective-permute-start(bf16[32,64,128]{2,1,0:T(8,128)(2,1)} %get-tuple-element.26), channel_id=1, source_target_pairs={{0,16},{4,132},{8,56},{12,140},{16,32},{20,148},{24,8},{28,156},{3... | collective-permute-start | bytes 1572872 | tf_op jit(solution)/shard_map/reduce_far/ppermute | solution.py:35
  101.7 5.5 %collective-permute-start.14 = (bf16[32,64,128]{2,1,0:T(8,128)(2,1)S(1)}, bf16[32,64,128]{2,1,0:T(8,128)(2,1)S(1)}, u32[]{:S(2)}, u32[]{:S(2)}) collective-permute-start(bf16[32,64,128]{2,1,0:T(8,128)(2,1)S(1)} %add_convert_fusion.2), channel_id=1, source_target_pairs={{0,48},{4,388},{8,24},{12,396},{16,0},{20,404},{24,40},{28,412},{3... | collective-permute-start | bytes 1572872 | tf_op jit(solution)/shard_map/reduce_far/ppermute | solution.py:35
  107.1 8.8 %collective-permute-done.12 = bf16[32,64,128]{2,1,0:T(8,128)(2,1)S(1)} collective-permute-done((bf16[32,64,128]{2,1,0:T(8,128)(2,1)}, bf16[32,64,128]{2,1,0:T(8,128)(2,1)S(1)}, u32[]{:S(2)}, u32[]{:S(2)}) %collective-permute-start.12) | collective-permute-done | bytes 524320 | tf_op jit(solution)/shard_map/reduce_far/ppermute | solution.py:35
  117.4 1.9 %collective-permute-start.13 = (bf16[32,64,128]{2,1,0:T(8,128)(2,1)S(1)}, bf16[32,64,128]{2,1,0:T(8,128)(2,1)S(1)}, u32[]{:S(2)}, u32[]{:S(2)}) collective-permute-start(bf16[32,64,128]{2,1,0:T(8,128)(2,1)S(1)} %add_convert_fusion.1), channel_id=1, source_target_pairs={{0,16},{4,132},{8,56},{12,140},{16,32},{20,148},{24,8},{28,156},{3... | collective-permute-start | bytes 1572872 | tf_op jit(solution)/shard_map/reduce_far/ppermute | solution.py:35
  120.8 8.6 %collective-permute-done.13 = bf16[32,64,128]{2,1,0:T(8,128)(2,1)S(1)} collective-permute-done((bf16[32,64,128]{2,1,0:T(8,128)(2,1)S(1)}, bf16[32,64,128]{2,1,0:T(8,128)(2,1)S(1)}, u32[]{:S(2)}, u32[]{:S(2)}) %collective-permute-start.13) | collective-permute-done | bytes 524320 | tf_op jit(solution)/shard_map/reduce_far/ppermute | solution.py:35
  130.5 3.5 %all-to-all-start.2 = ((bf16[8,256,128]{2,1,0:T(8,128)(2,1)}), bf16[8,256,128]{2,1,0:T(8,128)(2,1)S(1)}, u32[]{:S(2)}, u32[]{:S(2)}) async-start(bf16[8,256,128]{2,1,0:T(8,128)(2,1)} %bitcast.39), calls=%async_computation.2 | async-start | bytes 1048576 | tf_op jit(solution)/shard_map/reduce_near/all_to_all | solution.py:43
  134.0 1.9 %collective-permute-start.9 = (bf16[2,64,128]{2,1,0:T(8,128)(2,1)S(1)}, bf16[2,64,128]{2,1,0:T(8,128)(2,1)S(1)}, u32[]{:S(2)}, u32[]{:S(2)}) collective-permute-start(bf16[2,64,128]{2,1,0:T(8,128)(2,1)S(1)} %slice.53), channel_id=1, source_target_pairs={{0,4},{4,0},{8,12},{12,8},{16,20},{20,16},{24,28},{28,24},{32,36},... | collective-permute-start | bytes 98312 | tf_op jit(solution)/shard_map/swap_back/ppermute | solution.py:39
  137.1 2.0 %reduce_near.1 = bf16[2,26,32,256]{3,2,1,0:T(8,128)(2,1)} custom-call(bf16[8,1088,128]{2,1,0:T(8,128)(2,1)S(1)} %all-to-all-done.1.refs_0_), custom_call_target="tpu_custom_call" | custom-call | flops 872415232 | bytes 3080192 | tf_op jit(solution)/shard_map/reduce_near/pallas_call | solution.py:261
  139.1 6.9 %all-to-all-done.2 = bf16[8,256,128]{2,1,0:T(8,128)(2,1)S(1)} async-done(((bf16[8,256,128]{2,1,0:T(8,128)(2,1)}), bf16[8,256,128]{2,1,0:T(8,128)(2,1)S(1)}, u32[]{:S(2)}, u32[]{:S(2)}) %all-to-all-start.2) | async-done | bytes 524320 | tf_op jit(solution)/shard_map/reduce_near/all_to_all | solution.py:43
  (55 shorter events, 18.7 us)
Async XLA Ops:
  1.5 9.7 %collective-permute-start = (bf16[2,64,256]{2,1,0:T(8,128)(2,1)S(1)}, bf16[2,64,256]{2,1,0:T(8,128)(2,1)S(1)}, u32[]{:S(2)}, u32[]{:S(2)}) collective-permute-start(bf16[2,64,256]{2,1,0:T(8,128)(2,1)S(1)} %get-tuple-element.34), channel_id=1, source_target_pairs={{0,4},{4,0},{8,12},{12,8},{16,20},{20,16},{24,28},{28,24},{32,36},... | collective-permute-start | bytes 196616 | tf_op jit(solution)/shard_map/swap_tokens/ppermute | solution.py:39
  28.2 43.3 %collective-permute-start.8 = (bf16[2,26,128,256]{3,2,1,0:T(8,128)(2,1)}, bf16[2,26,128,256]{3,2,1,0:T(8,128)(2,1)S(1)}, u32[]{:S(2)}, u32[]{:S(2)}) collective-permute-start(bf16[2,26,128,256]{3,2,1,0:T(8,128)(2,1)} %param.6), channel_id=1, source_target_pairs={{0,4},{4,0},{8,12},{12,8},{16,20},{20,16},{24,28},{28,24},{32,36},... | collective-permute-start | bytes 10223624 | tf_op jit(solution)/shard_map/swap_weights/ppermute | solution.py:39
  30.1 17.0 %collective-permute-start.3 = (bf16[32,64,128]{2,1,0:T(8,128)(2,1)}, bf16[32,64,128]{2,1,0:T(8,128)(2,1)}, u32[]{:S(2)}, u32[]{:S(2)}) collective-permute-start(bf16[32,64,128]{2,1,0:T(8,128)(2,1)} %bitcast.5.refs_0_), channel_id=1, source_target_pairs={{0,16},{4,132},{8,56},{12,140},{16,32},{20,148},{24,8},{28,156},{3... | collective-permute-start | bytes 1572872 | tf_op jit(solution)/shard_map/gather_far/ppermute | solution.py:35
  34.4 15.5 %collective-permute-start.7 = (bf16[32,64,128]{2,1,0:T(8,128)(2,1)}, bf16[32,64,128]{2,1,0:T(8,128)(2,1)}, u32[]{:S(2)}, u32[]{:S(2)}) collective-permute-start(bf16[32,64,128]{2,1,0:T(8,128)(2,1)} %bitcast.5.refs_0_), channel_id=1, source_target_pairs={{0,56},{4,452},{8,16},{12,460},{16,8},{20,468},{24,32},{28,476},{3... | collective-permute-start | bytes 1572872 | tf_op jit(solution)/shard_map/gather_far/ppermute | solution.py:35
  39.0 15.0 %collective-permute-start.2 = (bf16[32,64,128]{2,1,0:T(8,128)(2,1)}, bf16[32,64,128]{2,1,0:T(8,128)(2,1)}, u32[]{:S(2)}, u32[]{:S(2)}) collective-permute-start(bf16[32,64,128]{2,1,0:T(8,128)(2,1)} %bitcast.5.refs_0_), channel_id=1, source_target_pairs={{0,48},{4,388},{8,24},{12,396},{16,0},{20,404},{24,40},{28,412},{3... | collective-permute-start | bytes 1572872 | tf_op jit(solution)/shard_map/gather_far/ppermute | solution.py:35
  44.6 14.9 %collective-permute-start.1 = (bf16[32,64,128]{2,1,0:T(8,128)(2,1)}, bf16[32,64,128]{2,1,0:T(8,128)(2,1)}, u32[]{:S(2)}, u32[]{:S(2)}) collective-permute-start(bf16[32,64,128]{2,1,0:T(8,128)(2,1)} %bitcast.5.refs_0_), channel_id=1, source_target_pairs={{0,8},{4,68},{8,0},{12,76},{16,24},{20,84},{24,16},{28,92},{32,40}... | collective-permute-start | bytes 1572872 | tf_op jit(solution)/shard_map/gather_far/ppermute | solution.py:35
  47.1 20.6 %collective-permute-start.5 = (bf16[32,64,128]{2,1,0:T(8,128)(2,1)}, bf16[32,64,128]{2,1,0:T(8,128)(2,1)}, u32[]{:S(2)}, u32[]{:S(2)}) collective-permute-start(bf16[32,64,128]{2,1,0:T(8,128)(2,1)} %collective-permute-done.3.refs_6_), channel_id=1, source_target_pairs={{0,16},{4,132},{8,56},{12,140},{16,32},{20,148},{24,8},{28,156},{3... | collective-permute-start | bytes 1572872 | tf_op jit(solution)/shard_map/gather_far/ppermute | solution.py:35
  49.9 20.9 %collective-permute-start.4 = (bf16[32,64,128]{2,1,0:T(8,128)(2,1)}, bf16[32,64,128]{2,1,0:T(8,128)(2,1)}, u32[]{:S(2)}, u32[]{:S(2)}) collective-permute-start(bf16[32,64,128]{2,1,0:T(8,128)(2,1)} %collective-permute-done.3.refs_6_), channel_id=1, source_target_pairs={{0,8},{4,68},{8,0},{12,76},{16,24},{20,84},{24,16},{28,92},{32,40}... | collective-permute-start | bytes 1572872 | tf_op jit(solution)/shard_map/gather_far/ppermute | solution.py:35
  54.1 17.4 %collective-permute-start.6 = (bf16[32,64,128]{2,1,0:T(8,128)(2,1)}, bf16[32,64,128]{2,1,0:T(8,128)(2,1)}, u32[]{:S(2)}, u32[]{:S(2)}) collective-permute-start(bf16[32,64,128]{2,1,0:T(8,128)(2,1)} %collective-permute-done.2.refs_2_), channel_id=1, source_target_pairs={{0,56},{4,452},{8,16},{12,460},{16,8},{20,468},{24,32},{28,476},{3... | collective-permute-start | bytes 1572872 | tf_op jit(solution)/shard_map/gather_far/ppermute | solution.py:35
  81.5 18.5 %collective-permute-start.10 = (bf16[64,64,128]{2,1,0:T(8,128)(2,1)}, bf16[64,64,128]{2,1,0:T(8,128)(2,1)S(1)}, u32[]{:S(2)}, u32[]{:S(2)}) collective-permute-start(bf16[64,64,128]{2,1,0:T(8,128)(2,1)} %get-tuple-element.23), channel_id=1, source_target_pairs={{0,8},{4,68},{8,0},{12,76},{16,24},{20,84},{24,16},{28,92},{32,40}... | collective-permute-start | bytes 3145736 | tf_op jit(solution)/shard_map/reduce_far/ppermute | solution.py:35
  84.4 31.6 %collective-permute-start.11 = (bf16[64,64,128]{2,1,0:T(8,128)(2,1)}, bf16[64,64,128]{2,1,0:T(8,128)(2,1)}, u32[]{:S(2)}, u32[]{:S(2)}) collective-permute-start(bf16[64,64,128]{2,1,0:T(8,128)(2,1)} %get-tuple-element.25), channel_id=1, source_target_pairs={{0,56},{4,452},{8,16},{12,460},{16,8},{20,468},{24,32},{28,476},{3... | collective-permute-start | bytes 3145736 | tf_op jit(solution)/shard_map/reduce_far/ppermute | solution.py:35
  88.3 42.2 %all-to-all-start.1 = ((bf16[8,1088,128]{2,1,0:T(8,128)(2,1)}), bf16[8,1088,128]{2,1,0:T(8,128)(2,1)S(1)}, u32[]{:S(2)}, u32[]{:S(2)}) async-start(bf16[8,1088,128]{2,1,0:T(8,128)(2,1)} %get-tuple-element.28), calls=%async_computation.1 | async-start | bytes 4456448 | tf_op jit(solution)/shard_map/weight_grad/all_to_all | solution.py:351
  98.0 21.4 %copy-start.1 = (bf16[32,64,128]{2,1,0:T(8,128)(2,1)S(1)}, bf16[32,64,128]{2,1,0:T(8,128)(2,1)}, u32[]{:S(2)}) copy-start(bf16[32,64,128]{2,1,0:T(8,128)(2,1)} %get-tuple-element.27) | copy-start | bytes 1572868
  98.0 18.0 %collective-permute-start.12 = (bf16[32,64,128]{2,1,0:T(8,128)(2,1)}, bf16[32,64,128]{2,1,0:T(8,128)(2,1)S(1)}, u32[]{:S(2)}, u32[]{:S(2)}) collective-permute-start(bf16[32,64,128]{2,1,0:T(8,128)(2,1)} %get-tuple-element.26), channel_id=1, source_target_pairs={{0,16},{4,132},{8,56},{12,140},{16,32},{20,148},{24,8},{28,156},{3... | collective-permute-start | bytes 1572872 | tf_op jit(solution)/shard_map/reduce_far/ppermute | solution.py:35
  100.0 19.3 %copy-start = (bf16[64,64,128]{2,1,0:T(8,128)(2,1)}, bf16[64,64,128]{2,1,0:T(8,128)(2,1)S(1)}, u32[]{:S(2)}) copy-start(bf16[64,64,128]{2,1,0:T(8,128)(2,1)S(1)} %collective-permute-done.10) | copy-start | bytes 3145732
  101.7 19.2 %collective-permute-start.14 = (bf16[32,64,128]{2,1,0:T(8,128)(2,1)S(1)}, bf16[32,64,128]{2,1,0:T(8,128)(2,1)S(1)}, u32[]{:S(2)}, u32[]{:S(2)}) collective-permute-start(bf16[32,64,128]{2,1,0:T(8,128)(2,1)S(1)} %add_convert_fusion.2), channel_id=1, source_target_pairs={{0,48},{4,388},{8,24},{12,396},{16,0},{20,404},{24,40},{28,412},{3... | collective-permute-start | bytes 1572872 | tf_op jit(solution)/shard_map/reduce_far/ppermute | solution.py:35
  117.4 12.0 %collective-permute-start.13 = (bf16[32,64,128]{2,1,0:T(8,128)(2,1)S(1)}, bf16[32,64,128]{2,1,0:T(8,128)(2,1)S(1)}, u32[]{:S(2)}, u32[]{:S(2)}) collective-permute-start(bf16[32,64,128]{2,1,0:T(8,128)(2,1)S(1)} %add_convert_fusion.1), channel_id=1, source_target_pairs={{0,16},{4,132},{8,56},{12,140},{16,32},{20,148},{24,8},{28,156},{3... | collective-permute-start | bytes 1572872 | tf_op jit(solution)/shard_map/reduce_far/ppermute | solution.py:35
  130.5 15.6 %all-to-all-start.2 = ((bf16[8,256,128]{2,1,0:T(8,128)(2,1)}), bf16[8,256,128]{2,1,0:T(8,128)(2,1)S(1)}, u32[]{:S(2)}, u32[]{:S(2)}) async-start(bf16[8,256,128]{2,1,0:T(8,128)(2,1)} %bitcast.39), calls=%async_computation.2 | async-start | bytes 1048576 | tf_op jit(solution)/shard_map/reduce_near/all_to_all | solution.py:43
  134.0 3.1 %collective-permute-start.9 = (bf16[2,64,128]{2,1,0:T(8,128)(2,1)S(1)}, bf16[2,64,128]{2,1,0:T(8,128)(2,1)S(1)}, u32[]{:S(2)}, u32[]{:S(2)}) collective-permute-start(bf16[2,64,128]{2,1,0:T(8,128)(2,1)S(1)} %slice.53), channel_id=1, source_target_pairs={{0,4},{4,0},{8,12},{12,8},{16,20},{20,16},{24,28},{28,24},{32,36},... | collective-permute-start | bytes 98312 | tf_op jit(solution)/shard_map/swap_back/ppermute | solution.py:39
  146.1 3.1 %collective-permute-start.15 = (bf16[2,64,128]{2,1,0:T(8,128)(2,1)S(1)}, bf16[2,64,128]{2,1,0:T(8,128)(2,1)S(1)}, u32[]{:S(2)}, u32[]{:S(2)}) collective-permute-start(bf16[2,64,128]{2,1,0:T(8,128)(2,1)S(1)} %bitcast.49), channel_id=1, source_target_pairs={{0,4},{4,0},{8,12},{12,8},{16,20},{20,16},{24,28},{28,24},{32,36},... | collective-permute-start | bytes 98312 | tf_op jit(solution)/shard_map/swap_back/ppermute | solution.py:39

commit v5 on v4

--- a/solution.py
+++ b/solution.py
@@ -43,15 +43,17 @@
     return lax.all_to_all(value, "blk", 0, 0, axis_index_groups=GROUPS_NEAR, tiled=True)
 
 
-def far_gather(own):
+def far_gather(own, beside):
     at6 = far_shift(own, 2)
     at2 = far_shift(own, -2)
     at1 = far_shift(own, 1)
-    at7 = far_shift(own, -1)
+    at6, beside = lax.optimization_barrier((at6, beside))
     at4 = far_shift(at6, 2)
     at3 = far_shift(at6, 1)
     at5 = far_shift(at2, -1)
-    return own, at1, at2, at3, at4, at5, at6, at7
+    late, _, _ = lax.optimization_barrier((own, at2, at6))
+    at7 = far_shift(late, -1)
+    return (own, at1, at2, at3, at4, at5, at6, at7), beside
 
 
 def far_reduce(own, to31, to57, to4, to2, to6):
@@ -304,10 +306,8 @@
         near = near_exchange(jnp.broadcast_to(chip_blocks[None], (SIDE,) + chip_blocks.shape))
         near = near.reshape(SIDE * 2 * owned, half, width)
     with jax.named_scope("gather_far"):
-        chunks = far_gather(near)
-    with jax.named_scope("swap_weights"):
         ready, _ = lax.optimization_barrier((weights, near))
-        other_weights = swap_cores(ready)
+        chunks, other_weights = far_gather(near, swap_cores(ready))
     with jax.named_scope("sources"):
         wanted = jnp.concatenate(
             [

time: 151 us -> 152 us (level)
  waiting for transfers between devices: 39.5 us -> 41.1 us
    ppermute x12, starting transfers between devices: 42.1 us -> 40.5 us  [far_shift(): return lax.ppermute(value, 'blk', pairs)]
where the time goes in v5:
time: 152 us; the launch traced here: 151 us
  starting transfers between devices  68.8 us (45%)
  waiting for transfers between devices  41.1 us (27%)
  blocking collectives  16.7 us (11%)
  Pallas kernels  11.9 us (8%)
  other arithmetic  8 us (5%)
  local copies, waits for them, and re-layouts  2.96 us (2%)
    ppermute x12, starting transfers between devices, far_shift(): return lax.ppermute(value, 'blk', pairs)  40.5 us
    ppermute x12, waiting for transfers between devices, far_shift(): return lax.ppermute(value, 'blk', pairs)  31.6 us
    all_to_all x1, blocking collectives, near_exchange(): lax.all_to_all(value, 'blk', 0, 0, axis_index_groups=GROUPS_NEAR, tiled=T...  16.7 us
    ppermute x4, starting transfers between devices, swap_cores(): return lax.ppermute(value, 'blk', SWAP)  14.5 us
    all_to_all x1, starting transfers between devices, local(): lax.all_to_all(packed, BOTH, 0, 0, axis_index_groups=groups, tiled=True)  10 us
    pallas_call x1, Pallas kernels, run_blocks(): pl.pallas_call(block_kernel, in_specs=[scalars] * 2 + [outside] * 9 + [wh...  9.96 us
    all_to_all x1, waiting for transfers between devices, near_exchange(): lax.all_to_all(value, 'blk', 0, 0, axis_index_groups=GROUPS_NEAR, tiled=T...  7.03 us
    convert_element_type x3, other arithmetic, add(): return sum((value.astype(F32) for value in values)).astype(BF)  4.08 us
  transfers between devices with their start and end apart: 18, of which 10 were waited for; matrix products, arithmetic and copies ran while one was open for 6% of the time, Pallas kernels for 1%

profile of v5, /device:TPU:1, one launch (start us, length us, event | category | flops | bytes accessed | tf_op | source)
XLA Modules:
  0.0 150.6 jit_solution(7948507241955089138)
XLA Ops:
  1.5 8.8 %collective-permute-start = (bf16[2,64,256]{2,1,0:T(8,128)(2,1)S(1)}, bf16[2,64,256]{2,1,0:T(8,128)(2,1)S(1)}, u32[]{:S(2)}, u32[]{:S(2)}) collective-permute-start(bf16[2,64,256]{2,1,0:T(8,128)(2,1)S(1)} %get-tuple-element.40), channel_id=1, source_target_pairs={{0,4},{4,0},{8,12},{12,8},{16,20},{20,16},{24,28},{28,24},{32,36},... | collective-permute-start | bytes 196616 | tf_op jit(solution)/shard_map/swap_tokens/ppermute | solution.py:39
  11.5 16.7 %all_to_all.15 = bf16[8,4,64,128]{3,2,1,0:T(8,128)(2,1)} all-to-all(bf16[8,4,64,128]{3,2,1,0:T(8,128)(2,1)S(1)} %broadcast_in_dim.23), channel_id=1, replica_groups={{0,64,128,192,256,320,384,448},{8,72,136,200,264,328,392,456},{16,80,14..., dimensions={0} | all-to-all | bytes 1048576 | tf_op jit(solution)/shard_map/gather_near/all_to_all | solution.py:43
  30.1 5.9 %collective-permute-start.2 = (bf16[32,64,128]{2,1,0:T(8,128)(2,1)}, bf16[32,64,128]{2,1,0:T(8,128)(2,1)}, u32[]{:S(2)}, u32[]{:S(2)}) collective-permute-start(bf16[32,64,128]{2,1,0:T(8,128)(2,1)} %bitcast.5.refs_0_), channel_id=1, source_target_pairs={{0,48},{4,388},{8,24},{12,396},{16,0},{20,404},{24,40},{28,412},{3... | collective-permute-start | bytes 1572872 | tf_op jit(solution)/shard_map/gather_far/ppermute | solution.py:35
  36.0 1.9 %collective-permute-start.3 = (bf16[32,64,128]{2,1,0:T(8,128)(2,1)}, bf16[32,64,128]{2,1,0:T(8,128)(2,1)}, u32[]{:S(2)}, u32[]{:S(2)}) collective-permute-start(bf16[32,64,128]{2,1,0:T(8,128)(2,1)} %bitcast.5.refs_0_), channel_id=1, source_target_pairs={{0,16},{4,132},{8,56},{12,140},{16,32},{20,148},{24,8},{28,156},{3... | collective-permute-start | bytes 1572872 | tf_op jit(solution)/shard_map/gather_far/ppermute | solution.py:35
  40.7 2.8 %collective-permute-start.1 = (bf16[32,64,128]{2,1,0:T(8,128)(2,1)}, bf16[32,64,128]{2,1,0:T(8,128)(2,1)}, u32[]{:S(2)}, u32[]{:S(2)}) collective-permute-start(bf16[32,64,128]{2,1,0:T(8,128)(2,1)} %bitcast.5.refs_0_), channel_id=1, source_target_pairs={{0,8},{4,68},{8,0},{12,76},{16,24},{20,84},{24,16},{28,92},{32,40}... | collective-permute-start | bytes 1572872 | tf_op jit(solution)/shard_map/gather_far/ppermute | solution.py:35
  43.5 4.6 %collective-permute-done.2.refs_2_ = bf16[32,64,128]{2,1,0:T(8,128)(2,1)} collective-permute-done((bf16[32,64,128]{2,1,0:T(8,128)(2,1)}, bf16[32,64,128]{2,1,0:T(8,128)(2,1)}, u32[]{:S(2)}, u32[]{:S(2)}) %collective-permute-start.2) | collective-permute-done | bytes 524320 | tf_op jit(solution)/shard_map/gather_far/ppermute | solution.py:35
  50.1 2.4 %collective-permute-start.6 = (bf16[32,64,128]{2,1,0:T(8,128)(2,1)}, bf16[32,64,128]{2,1,0:T(8,128)(2,1)}, u32[]{:S(2)}, u32[]{:S(2)}) collective-permute-start(bf16[32,64,128]{2,1,0:T(8,128)(2,1)} %collective-permute-done.3.refs_6_), channel_id=1, source_target_pairs={{0,16},{4,132},{8,56},{12,140},{16,32},{20,148},{24,8},{28,156},{3... | collective-permute-start | bytes 1572872 | tf_op jit(solution)/shard_map/gather_far/ppermute | solution.py:35
  52.5 5.2 %collective-permute-start.5 = (bf16[32,64,128]{2,1,0:T(8,128)(2,1)}, bf16[32,64,128]{2,1,0:T(8,128)(2,1)}, u32[]{:S(2)}, u32[]{:S(2)}) collective-permute-start(bf16[32,64,128]{2,1,0:T(8,128)(2,1)} %collective-permute-done.3.refs_6_), channel_id=1, source_target_pairs={{0,8},{4,68},{8,0},{12,76},{16,24},{20,84},{24,16},{28,92},{32,40}... | collective-permute-start | bytes 1572872 | tf_op jit(solution)/shard_map/gather_far/ppermute | solution.py:35
  57.7 3.8 %collective-permute-start.8 = (bf16[32,64,128]{2,1,0:T(8,128)(2,1)}, bf16[32,64,128]{2,1,0:T(8,128)(2,1)}, u32[]{:S(2)}, u32[]{:S(2)}) collective-permute-start(bf16[32,64,128]{2,1,0:T(8,128)(2,1)} %bitcast.5.refs_0_), channel_id=1, source_target_pairs={{0,56},{4,452},{8,16},{12,460},{16,8},{20,468},{24,32},{28,476},{3... | collective-permute-start | bytes 1572872 | tf_op jit(solution)/shard_map/gather_far/ppermute | solution.py:35
  61.6 3.8 %collective-permute-done.7.refs_5_ = bf16[32,64,128]{2,1,0:T(8,128)(2,1)} collective-permute-done((bf16[32,64,128]{2,1,0:T(8,128)(2,1)}, bf16[32,64,128]{2,1,0:T(8,128)(2,1)}, u32[]{:S(2)}, u32[]{:S(2)}) %collective-permute-start.7) | collective-permute-done | bytes 524320 | tf_op jit(solution)/shard_map/gather_far/ppermute | solution.py:35
  65.4 5.6 %collective-permute-done.8.refs_7_ = bf16[32,64,128]{2,1,0:T(8,128)(2,1)} collective-permute-done((bf16[32,64,128]{2,1,0:T(8,128)(2,1)}, bf16[32,64,128]{2,1,0:T(8,128)(2,1)}, u32[]{:S(2)}, u32[]{:S(2)}) %collective-permute-start.8) | collective-permute-done | bytes 524320 | tf_op jit(solution)/shard_map/gather_far/ppermute | solution.py:35
  71.0 10.0 %blocks.1 = (bf16[4,64,128]{2,1,0:T(8,128)(2,1)S(1)}, bf16[32,64,128]{2,1,0:T(8,128)(2,1)}, bf16[64,64,128]{2,1,0:T(8,128)(2,1)}, bf16[64,64,128]{2,1,0:T(8,128)...) custom-call(s32[1]{0:T(128)} %bitcast.core, ...), custom_call_target="tpu_custom_call" | custom-call | flops 872415232 | bytes 15204352 | tf_op jit(solution)/shard_map/blocks/pallas_call | solution.py:200
  82.9 5.3 %collective-permute-start.11 = (bf16[64,64,128]{2,1,0:T(8,128)(2,1)}, bf16[64,64,128]{2,1,0:T(8,128)(2,1)}, u32[]{:S(2)}, u32[]{:S(2)}) collective-permute-start(bf16[64,64,128]{2,1,0:T(8,128)(2,1)} %get-tuple-element.31), channel_id=1, source_target_pairs={{0,56},{4,452},{8,16},{12,460},{16,8},{20,468},{24,32},{28,476},{3... | collective-permute-start | bytes 3145736 | tf_op jit(solution)/shard_map/reduce_far/ppermute | solution.py:35
  88.2 10.0 %all-to-all-start.1 = ((bf16[8,1088,128]{2,1,0:T(8,128)(2,1)}), bf16[8,1088,128]{2,1,0:T(8,128)(2,1)S(1)}, u32[]{:S(2)}, u32[]{:S(2)}) async-start(bf16[8,1088,128]{2,1,0:T(8,128)(2,1)} %get-tuple-element.34), calls=%async_computation.1 | async-start | bytes 4456448 | tf_op jit(solution)/shard_map/weight_grad/all_to_all | solution.py:351
  98.2 2.0 %collective-permute-start.12 = (bf16[32,64,128]{2,1,0:T(8,128)(2,1)}, bf16[32,64,128]{2,1,0:T(8,128)(2,1)S(1)}, u32[]{:S(2)}, u32[]{:S(2)}) collective-permute-start(bf16[32,64,128]{2,1,0:T(8,128)(2,1)} %get-tuple-element.32), channel_id=1, source_target_pairs={{0,16},{4,132},{8,56},{12,140},{16,32},{20,148},{24,8},{28,156},{3... | collective-permute-start | bytes 1572872 | tf_op jit(solution)/shard_map/reduce_far/ppermute | solution.py:35
  101.9 5.5 %collective-permute-start.14 = (bf16[32,64,128]{2,1,0:T(8,128)(2,1)S(1)}, bf16[32,64,128]{2,1,0:T(8,128)(2,1)S(1)}, u32[]{:S(2)}, u32[]{:S(2)}) collective-permute-start(bf16[32,64,128]{2,1,0:T(8,128)(2,1)S(1)} %add_convert_fusion.2), channel_id=1, source_target_pairs={{0,48},{4,388},{8,24},{12,396},{16,0},{20,404},{24,40},{28,412},{3... | collective-permute-start | bytes 1572872 | tf_op jit(solution)/shard_map/reduce_far/ppermute | solution.py:35
  107.4 8.8 %collective-permute-done.12 = bf16[32,64,128]{2,1,0:T(8,128)(2,1)S(1)} collective-permute-done((bf16[32,64,128]{2,1,0:T(8,128)(2,1)}, bf16[32,64,128]{2,1,0:T(8,128)(2,1)S(1)}, u32[]{:S(2)}, u32[]{:S(2)}) %collective-permute-start.12) | collective-permute-done | bytes 524320 | tf_op jit(solution)/shard_map/reduce_far/ppermute | solution.py:35
  117.7 1.9 %collective-permute-start.13 = (bf16[32,64,128]{2,1,0:T(8,128)(2,1)S(1)}, bf16[32,64,128]{2,1,0:T(8,128)(2,1)S(1)}, u32[]{:S(2)}, u32[]{:S(2)}) collective-permute-start(bf16[32,64,128]{2,1,0:T(8,128)(2,1)S(1)} %add_convert_fusion.1), channel_id=1, source_target_pairs={{0,16},{4,132},{8,56},{12,140},{16,32},{20,148},{24,8},{28,156},{3... | collective-permute-start | bytes 1572872 | tf_op jit(solution)/shard_map/reduce_far/ppermute | solution.py:35
  121.1 8.6 %collective-permute-done.13 = bf16[32,64,128]{2,1,0:T(8,128)(2,1)S(1)} collective-permute-done((bf16[32,64,128]{2,1,0:T(8,128)(2,1)S(1)}, bf16[32,64,128]{2,1,0:T(8,128)(2,1)S(1)}, u32[]{:S(2)}, u32[]{:S(2)}) %collective-permute-start.13) | collective-permute-done | bytes 524320 | tf_op jit(solution)/shard_map/reduce_far/ppermute | solution.py:35
  130.8 3.7 %all-to-all-start.2 = ((bf16[8,256,128]{2,1,0:T(8,128)(2,1)}), bf16[8,256,128]{2,1,0:T(8,128)(2,1)S(1)}, u32[]{:S(2)}, u32[]{:S(2)}) async-start(bf16[8,256,128]{2,1,0:T(8,128)(2,1)} %bitcast.39), calls=%async_computation.2 | async-start | bytes 1048576 | tf_op jit(solution)/shard_map/reduce_near/all_to_all | solution.py:43
  134.5 1.9 %collective-permute-start.9 = (bf16[2,64,128]{2,1,0:T(8,128)(2,1)S(1)}, bf16[2,64,128]{2,1,0:T(8,128)(2,1)S(1)}, u32[]{:S(2)}, u32[]{:S(2)}) collective-permute-start(bf16[2,64,128]{2,1,0:T(8,128)(2,1)S(1)} %slice.53), channel_id=1, source_target_pairs={{0,4},{4,0},{8,12},{12,8},{16,20},{20,16},{24,28},{28,24},{32,36},... | collective-permute-start | bytes 98312 | tf_op jit(solution)/shard_map/swap_back/ppermute | solution.py:39
  137.6 2.0 %reduce_near.1 = bf16[2,26,32,256]{3,2,1,0:T(8,128)(2,1)} custom-call(bf16[8,1088,128]{2,1,0:T(8,128)(2,1)S(1)} %all-to-all-done.1.refs_0_), custom_call_target="tpu_custom_call" | custom-call | flops 872415232 | bytes 3080192 | tf_op jit(solution)/shard_map/reduce_near/pallas_call | solution.py:263
  139.6 7.0 %all-to-all-done.2 = bf16[8,256,128]{2,1,0:T(8,128)(2,1)S(1)} async-done(((bf16[8,256,128]{2,1,0:T(8,128)(2,1)}), bf16[8,256,128]{2,1,0:T(8,128)(2,1)S(1)}, u32[]{:S(2)}, u32[]{:S(2)}) %all-to-all-start.2) | async-done | bytes 524320 | tf_op jit(solution)/shard_map/reduce_near/all_to_all | solution.py:43
  146.7 1.9 %collective-permute-start.15 = (bf16[2,64,128]{2,1,0:T(8,128)(2,1)S(1)}, bf16[2,64,128]{2,1,0:T(8,128)(2,1)S(1)}, u32[]{:S(2)}, u32[]{:S(2)}) collective-permute-start(bf16[2,64,128]{2,1,0:T(8,128)(2,1)S(1)} %bitcast.49), channel_id=1, source_target_pairs={{0,4},{4,0},{8,12},{12,8},{16,20},{20,16},{24,28},{28,24},{32,36},... | collective-permute-start | bytes 98312 | tf_op jit(solution)/shard_map/swap_back/ppermute | solution.py:39
  (55 shorter events, 19.3 us)
Async XLA Ops:
  1.5 9.7 %collective-permute-start = (bf16[2,64,256]{2,1,0:T(8,128)(2,1)S(1)}, bf16[2,64,256]{2,1,0:T(8,128)(2,1)S(1)}, u32[]{:S(2)}, u32[]{:S(2)}) collective-permute-start(bf16[2,64,256]{2,1,0:T(8,128)(2,1)S(1)} %get-tuple-element.40), channel_id=1, source_target_pairs={{0,4},{4,0},{8,12},{12,8},{16,20},{20,16},{24,28},{28,24},{32,36},... | collective-permute-start | bytes 196616 | tf_op jit(solution)/shard_map/swap_tokens/ppermute | solution.py:39
  28.2 21.9 %collective-permute-start.4 = (bf16[2,26,128,256]{3,2,1,0:T(8,128)(2,1)}, bf16[2,26,128,256]{3,2,1,0:T(8,128)(2,1)S(1)}, u32[]{:S(2)}, u32[]{:S(2)}) collective-permute-start(bf16[2,26,128,256]{3,2,1,0:T(8,128)(2,1)} %param.6), channel_id=1, source_target_pairs={{0,4},{4,0},{8,12},{12,8},{16,20},{20,16},{24,28},{28,24},{32,36},... | collective-permute-start | bytes 10223624 | tf_op jit(solution)/shard_map/gather_far/ppermute | solution.py:39
  30.1 17.9 %collective-permute-start.2 = (bf16[32,64,128]{2,1,0:T(8,128)(2,1)}, bf16[32,64,128]{2,1,0:T(8,128)(2,1)}, u32[]{:S(2)}, u32[]{:S(2)}) collective-permute-start(bf16[32,64,128]{2,1,0:T(8,128)(2,1)} %bitcast.5.refs_0_), channel_id=1, source_target_pairs={{0,48},{4,388},{8,24},{12,396},{16,0},{20,404},{24,40},{28,412},{3... | collective-permute-start | bytes 1572872 | tf_op jit(solution)/shard_map/gather_far/ppermute | solution.py:35
  36.0 14.1 %collective-permute-start.3 = (bf16[32,64,128]{2,1,0:T(8,128)(2,1)}, bf16[32,64,128]{2,1,0:T(8,128)(2,1)}, u32[]{:S(2)}, u32[]{:S(2)}) collective-permute-start(bf16[32,64,128]{2,1,0:T(8,128)(2,1)} %bitcast.5.refs_0_), channel_id=1, source_target_pairs={{0,16},{4,132},{8,56},{12,140},{16,32},{20,148},{24,8},{28,156},{3... | collective-permute-start | bytes 1572872 | tf_op jit(solution)/shard_map/gather_far/ppermute | solution.py:35
  40.7 21.0 %collective-permute-start.1 = (bf16[32,64,128]{2,1,0:T(8,128)(2,1)}, bf16[32,64,128]{2,1,0:T(8,128)(2,1)}, u32[]{:S(2)}, u32[]{:S(2)}) collective-permute-start(bf16[32,64,128]{2,1,0:T(8,128)(2,1)} %bitcast.5.refs_0_), channel_id=1, source_target_pairs={{0,8},{4,68},{8,0},{12,76},{16,24},{20,84},{24,16},{28,92},{32,40}... | collective-permute-start | bytes 1572872 | tf_op jit(solution)/shard_map/gather_far/ppermute | solution.py:35
  48.1 17.4 %collective-permute-start.7 = (bf16[32,64,128]{2,1,0:T(8,128)(2,1)}, bf16[32,64,128]{2,1,0:T(8,128)(2,1)}, u32[]{:S(2)}, u32[]{:S(2)}) collective-permute-start(bf16[32,64,128]{2,1,0:T(8,128)(2,1)} %collective-permute-done.2.refs_2_), channel_id=1, source_target_pairs={{0,56},{4,452},{8,16},{12,460},{16,8},{20,468},{24,32},{28,476},{3... | collective-permute-start | bytes 1572872 | tf_op jit(solution)/shard_map/gather_far/ppermute | solution.py:35
  50.1 20.9 %collective-permute-start.6 = (bf16[32,64,128]{2,1,0:T(8,128)(2,1)}, bf16[32,64,128]{2,1,0:T(8,128)(2,1)}, u32[]{:S(2)}, u32[]{:S(2)}) collective-permute-start(bf16[32,64,128]{2,1,0:T(8,128)(2,1)} %collective-permute-done.3.refs_6_), channel_id=1, source_target_pairs={{0,16},{4,132},{8,56},{12,140},{16,32},{20,148},{24,8},{28,156},{3... | collective-permute-start | bytes 1572872 | tf_op jit(solution)/shard_map/gather_far/ppermute | solution.py:35
  52.5 18.5 %collective-permute-start.5 = (bf16[32,64,128]{2,1,0:T(8,128)(2,1)}, bf16[32,64,128]{2,1,0:T(8,128)(2,1)}, u32[]{:S(2)}, u32[]{:S(2)}) collective-permute-start(bf16[32,64,128]{2,1,0:T(8,128)(2,1)} %collective-permute-done.3.refs_6_), channel_id=1, source_target_pairs={{0,8},{4,68},{8,0},{12,76},{16,24},{20,84},{24,16},{28,92},{32,40}... | collective-permute-start | bytes 1572872 | tf_op jit(solution)/shard_map/gather_far/ppermute | solution.py:35
  57.7 13.4 %collective-permute-start.8 = (bf16[32,64,128]{2,1,0:T(8,128)(2,1)}, bf16[32,64,128]{2,1,0:T(8,128)(2,1)}, u32[]{:S(2)}, u32[]{:S(2)}) collective-permute-start(bf16[32,64,128]{2,1,0:T(8,128)(2,1)} %bitcast.5.refs_0_), channel_id=1, source_target_pairs={{0,56},{4,452},{8,16},{12,460},{16,8},{20,468},{24,32},{28,476},{3... | collective-permute-start | bytes 1572872 | tf_op jit(solution)/shard_map/gather_far/ppermute | solution.py:35
  81.0 19.3 %collective-permute-start.10 = (bf16[64,64,128]{2,1,0:T(8,128)(2,1)}, bf16[64,64,128]{2,1,0:T(8,128)(2,1)S(1)}, u32[]{:S(2)}, u32[]{:S(2)}) collective-permute-start(bf16[64,64,128]{2,1,0:T(8,128)(2,1)} %get-tuple-element.29), channel_id=1, source_target_pairs={{0,8},{4,68},{8,0},{12,76},{16,24},{20,84},{24,16},{28,92},{32,40}... | collective-permute-start | bytes 3145736 | tf_op jit(solution)/shard_map/reduce_far/ppermute | solution.py:35
  82.9 33.3 %collective-permute-start.11 = (bf16[64,64,128]{2,1,0:T(8,128)(2,1)}, bf16[64,64,128]{2,1,0:T(8,128)(2,1)}, u32[]{:S(2)}, u32[]{:S(2)}) collective-permute-start(bf16[64,64,128]{2,1,0:T(8,128)(2,1)} %get-tuple-element.31), channel_id=1, source_target_pairs={{0,56},{4,452},{8,16},{12,460},{16,8},{20,468},{24,32},{28,476},{3... | collective-permute-start | bytes 3145736 | tf_op jit(solution)/shard_map/reduce_far/ppermute | solution.py:35
  88.2 42.5 %all-to-all-start.1 = ((bf16[8,1088,128]{2,1,0:T(8,128)(2,1)}), bf16[8,1088,128]{2,1,0:T(8,128)(2,1)S(1)}, u32[]{:S(2)}, u32[]{:S(2)}) async-start(bf16[8,1088,128]{2,1,0:T(8,128)(2,1)} %get-tuple-element.34), calls=%async_computation.1 | async-start | bytes 4456448 | tf_op jit(solution)/shard_map/weight_grad/all_to_all | solution.py:351
  98.2 21.4 %copy-start.1 = (bf16[32,64,128]{2,1,0:T(8,128)(2,1)S(1)}, bf16[32,64,128]{2,1,0:T(8,128)(2,1)}, u32[]{:S(2)}) copy-start(bf16[32,64,128]{2,1,0:T(8,128)(2,1)} %get-tuple-element.33) | copy-start | bytes 1572868
  98.2 18.0 %collective-permute-start.12 = (bf16[32,64,128]{2,1,0:T(8,128)(2,1)}, bf16[32,64,128]{2,1,0:T(8,128)(2,1)S(1)}, u32[]{:S(2)}, u32[]{:S(2)}) collective-permute-start(bf16[32,64,128]{2,1,0:T(8,128)(2,1)} %get-tuple-element.32), channel_id=1, source_target_pairs={{0,16},{4,132},{8,56},{12,140},{16,32},{20,148},{24,8},{28,156},{3... | collective-permute-start | bytes 1572872 | tf_op jit(solution)/shard_map/reduce_far/ppermute | solution.py:35
  100.3 19.3 %copy-start = (bf16[64,64,128]{2,1,0:T(8,128)(2,1)}, bf16[64,64,128]{2,1,0:T(8,128)(2,1)S(1)}, u32[]{:S(2)}) copy-start(bf16[64,64,128]{2,1,0:T(8,128)(2,1)S(1)} %collective-permute-done.10) | copy-start | bytes 3145732
  101.9 19.2 %collective-permute-start.14 = (bf16[32,64,128]{2,1,0:T(8,128)(2,1)S(1)}, bf16[32,64,128]{2,1,0:T(8,128)(2,1)S(1)}, u32[]{:S(2)}, u32[]{:S(2)}) collective-permute-start(bf16[32,64,128]{2,1,0:T(8,128)(2,1)S(1)} %add_convert_fusion.2), channel_id=1, source_target_pairs={{0,48},{4,388},{8,24},{12,396},{16,0},{20,404},{24,40},{28,412},{3... | collective-permute-start | bytes 1572872 | tf_op jit(solution)/shard_map/reduce_far/ppermute | solution.py:35
  117.7 12.0 %collective-permute-start.13 = (bf16[32,64,128]{2,1,0:T(8,128)(2,1)S(1)}, bf16[32,64,128]{2,1,0:T(8,128)(2,1)S(1)}, u32[]{:S(2)}, u32[]{:S(2)}) collective-permute-start(bf16[32,64,128]{2,1,0:T(8,128)(2,1)S(1)} %add_convert_fusion.1), channel_id=1, source_target_pairs={{0,16},{4,132},{8,56},{12,140},{16,32},{20,148},{24,8},{28,156},{3... | collective-permute-start | bytes 1572872 | tf_op jit(solution)/shard_map/reduce_far/ppermute | solution.py:35
  130.8 15.9 %all-to-all-start.2 = ((bf16[8,256,128]{2,1,0:T(8,128)(2,1)}), bf16[8,256,128]{2,1,0:T(8,128)(2,1)S(1)}, u32[]{:S(2)}, u32[]{:S(2)}) async-start(bf16[8,256,128]{2,1,0:T(8,128)(2,1)} %bitcast.39), calls=%async_computation.2 | async-start | bytes 1048576 | tf_op jit(solution)/shard_map/reduce_near/all_to_all | solution.py:43
  134.5 3.1 %collective-permute-start.9 = (bf16[2,64,128]{2,1,0:T(8,128)(2,1)S(1)}, bf16[2,64,128]{2,1,0:T(8,128)(2,1)S(1)}, u32[]{:S(2)}, u32[]{:S(2)}) collective-permute-start(bf16[2,64,128]{2,1,0:T(8,128)(2,1)S(1)} %slice.53), channel_id=1, source_target_pairs={{0,4},{4,0},{8,12},{12,8},{16,20},{20,16},{24,28},{28,24},{32,36},... | collective-permute-start | bytes 98312 | tf_op jit(solution)/shard_map/swap_back/ppermute | solution.py:39
  146.7 3.1 %collective-permute-start.15 = (bf16[2,64,128]{2,1,0:T(8,128)(2,1)S(1)}, bf16[2,64,128]{2,1,0:T(8,128)(2,1)S(1)}, u32[]{:S(2)}, u32[]{:S(2)}) collective-permute-start(bf16[2,64,128]{2,1,0:T(8,128)(2,1)S(1)} %bitcast.49), channel_id=1, source_target_pairs={{0,4},{4,0},{8,12},{12,8},{16,20},{20,16},{24,28},{28,24},{32,36},... | collective-permute-start | bytes 98312 | tf_op jit(solution)/shard_map/swap_back/ppermute | solution.py:39

commit v6 on v5

--- a/solution.py
+++ b/solution.py
@@ -99,11 +99,13 @@
         pltpu.make_async_copy(weights_here.at[i], weights.at[i], weight_sems.at[i])
         for i in range(rows // 2)
     ]
-    for copy in loads + weight_loads:
+    for copy in loads:
         copy.start()
     dense[...] = jnp.zeros_like(dense)
     for copy in loads:
         copy.wait()
+    for copy in weight_loads:
+        copy.start()
     for row in range(rows):
         for k in range(blocks):
             kept[row, :, k * 128 : (k + 1) * 128] = gathered[idx[row * blocks + k]]
@@ -340,8 +342,7 @@
     def rejoin(keep, came):
         low = jnp.where(first, keep, came)
         high = jnp.where(first, came, keep)
-        whole = jnp.stack([low, high])
-        return jnp.transpose(whole, (0, 2, 1, 3)).reshape(tokens, owned * width)
+        return jnp.concatenate([jnp.concatenate(list(v), axis=1) for v in (low, high)])
 
     with jax.named_scope("reduce_far"):
         column = far_reduce(*terms)

time: 152 us -> 152 us (level)
  no operation moved by 1% of the time
where the time goes in v6:
time: 152 us; the launch traced here: 151 us
  starting transfers between devices  68.8 us (45%)
  waiting for transfers between devices  41.1 us (27%)
  blocking collectives  16.7 us (11%)
  Pallas kernels  12.7 us (8%)
  other arithmetic  9.26 us (6%)
  local copies, waits for them, and re-layouts  1.56 us (1%)
    ppermute x12, starting transfers between devices, far_shift(): return lax.ppermute(value, 'blk', pairs)  40.5 us
    ppermute x12, waiting for transfers between devices, far_shift(): return lax.ppermute(value, 'blk', pairs)  31.6 us
    all_to_all x1, blocking collectives, near_exchange(): lax.all_to_all(value, 'blk', 0, 0, axis_index_groups=GROUPS_NEAR, tiled=T...  16.7 us
    ppermute x4, starting transfers between devices, swap_cores(): return lax.ppermute(value, 'blk', SWAP)  14.5 us
    pallas_call x1, Pallas kernels, run_blocks(): pl.pallas_call(block_kernel, in_specs=[scalars] * 2 + [outside] * 9 + [wh...  10.7 us
    all_to_all x1, starting transfers between devices, local(): lax.all_to_all(packed, BOTH, 0, 0, axis_index_groups=groups, tiled=True)  10 us
    all_to_all x1, waiting for transfers between devices, near_exchange(): lax.all_to_all(value, 'blk', 0, 0, axis_index_groups=GROUPS_NEAR, tiled=T...  7 us
    convert_element_type x3, other arithmetic, add(): return sum((value.astype(F32) for value in values)).astype(BF)  4.08 us
  transfers between devices with their start and end apart: 18, of which 10 were waited for; matrix products, arithmetic and copies ran while one was open for 6% of the time, Pallas kernels for 1%

profile of v6, /device:TPU:1, one launch (start us, length us, event | category | flops | bytes accessed | tf_op | source)
XLA Modules:
  0.0 151.3 jit_solution(13041980632461412435)
XLA Ops:
  1.5 8.8 %collective-permute-start = (bf16[2,64,256]{2,1,0:T(8,128)(2,1)S(1)}, bf16[2,64,256]{2,1,0:T(8,128)(2,1)S(1)}, u32[]{:S(2)}, u32[]{:S(2)}) collective-permute-start(bf16[2,64,256]{2,1,0:T(8,128)(2,1)S(1)} %get-tuple-element.40), channel_id=1, source_target_pairs={{0,4},{4,0},{8,12},{12,8},{16,20},{20,16},{24,28},{28,24},{32,36},... | collective-permute-start | bytes 196616 | tf_op jit(solution)/shard_map/swap_tokens/ppermute | solution.py:39
  11.5 16.7 %all_to_all.15 = bf16[8,4,64,128]{3,2,1,0:T(8,128)(2,1)} all-to-all(bf16[8,4,64,128]{3,2,1,0:T(8,128)(2,1)S(1)} %broadcast_in_dim.23), channel_id=1, replica_groups={{0,64,128,192,256,320,384,448},{8,72,136,200,264,328,392,456},{16,80,14..., dimensions={0} | all-to-all | bytes 1048576 | tf_op jit(solution)/shard_map/gather_near/all_to_all | solution.py:43
  30.1 5.9 %collective-permute-start.2 = (bf16[32,64,128]{2,1,0:T(8,128)(2,1)}, bf16[32,64,128]{2,1,0:T(8,128)(2,1)}, u32[]{:S(2)}, u32[]{:S(2)}) collective-permute-start(bf16[32,64,128]{2,1,0:T(8,128)(2,1)} %bitcast.5.refs_0_), channel_id=1, source_target_pairs={{0,48},{4,388},{8,24},{12,396},{16,0},{20,404},{24,40},{28,412},{3... | collective-permute-start | bytes 1572872 | tf_op jit(solution)/shard_map/gather_far/ppermute | solution.py:35
  36.0 1.9 %collective-permute-start.3 = (bf16[32,64,128]{2,1,0:T(8,128)(2,1)}, bf16[32,64,128]{2,1,0:T(8,128)(2,1)}, u32[]{:S(2)}, u32[]{:S(2)}) collective-permute-start(bf16[32,64,128]{2,1,0:T(8,128)(2,1)} %bitcast.5.refs_0_), channel_id=1, source_target_pairs={{0,16},{4,132},{8,56},{12,140},{16,32},{20,148},{24,8},{28,156},{3... | collective-permute-start | bytes 1572872 | tf_op jit(solution)/shard_map/gather_far/ppermute | solution.py:35
  40.7 2.8 %collective-permute-start.1 = (bf16[32,64,128]{2,1,0:T(8,128)(2,1)}, bf16[32,64,128]{2,1,0:T(8,128)(2,1)}, u32[]{:S(2)}, u32[]{:S(2)}) collective-permute-start(bf16[32,64,128]{2,1,0:T(8,128)(2,1)} %bitcast.5.refs_0_), channel_id=1, source_target_pairs={{0,8},{4,68},{8,0},{12,76},{16,24},{20,84},{24,16},{28,92},{32,40}... | collective-permute-start | bytes 1572872 | tf_op jit(solution)/shard_map/gather_far/ppermute | solution.py:35
  43.5 4.6 %collective-permute-done.2.refs_2_ = bf16[32,64,128]{2,1,0:T(8,128)(2,1)} collective-permute-done((bf16[32,64,128]{2,1,0:T(8,128)(2,1)}, bf16[32,64,128]{2,1,0:T(8,128)(2,1)}, u32[]{:S(2)}, u32[]{:S(2)}) %collective-permute-start.2) | collective-permute-done | bytes 524320 | tf_op jit(solution)/shard_map/gather_far/ppermute | solution.py:35
  50.1 2.4 %collective-permute-start.6 = (bf16[32,64,128]{2,1,0:T(8,128)(2,1)}, bf16[32,64,128]{2,1,0:T(8,128)(2,1)}, u32[]{:S(2)}, u32[]{:S(2)}) collective-permute-start(bf16[32,64,128]{2,1,0:T(8,128)(2,1)} %collective-permute-done.3.refs_6_), channel_id=1, source_target_pairs={{0,16},{4,132},{8,56},{12,140},{16,32},{20,148},{24,8},{28,156},{3... | collective-permute-start | bytes 1572872 | tf_op jit(solution)/shard_map/gather_far/ppermute | solution.py:35
  52.5 5.2 %collective-permute-start.5 = (bf16[32,64,128]{2,1,0:T(8,128)(2,1)}, bf16[32,64,128]{2,1,0:T(8,128)(2,1)}, u32[]{:S(2)}, u32[]{:S(2)}) collective-permute-start(bf16[32,64,128]{2,1,0:T(8,128)(2,1)} %collective-permute-done.3.refs_6_), channel_id=1, source_target_pairs={{0,8},{4,68},{8,0},{12,76},{16,24},{20,84},{24,16},{28,92},{32,40}... | collective-permute-start | bytes 1572872 | tf_op jit(solution)/shard_map/gather_far/ppermute | solution.py:35
  57.7 3.8 %collective-permute-start.8 = (bf16[32,64,128]{2,1,0:T(8,128)(2,1)}, bf16[32,64,128]{2,1,0:T(8,128)(2,1)}, u32[]{:S(2)}, u32[]{:S(2)}) collective-permute-start(bf16[32,64,128]{2,1,0:T(8,128)(2,1)} %bitcast.5.refs_0_), channel_id=1, source_target_pairs={{0,56},{4,452},{8,16},{12,460},{16,8},{20,468},{24,32},{28,476},{3... | collective-permute-start | bytes 1572872 | tf_op jit(solution)/shard_map/gather_far/ppermute | solution.py:35
  61.6 3.8 %collective-permute-done.7.refs_5_ = bf16[32,64,128]{2,1,0:T(8,128)(2,1)} collective-permute-done((bf16[32,64,128]{2,1,0:T(8,128)(2,1)}, bf16[32,64,128]{2,1,0:T(8,128)(2,1)}, u32[]{:S(2)}, u32[]{:S(2)}) %collective-permute-start.7) | collective-permute-done | bytes 524320 | tf_op jit(solution)/shard_map/gather_far/ppermute | solution.py:35
  65.4 5.6 %collective-permute-done.8.refs_7_ = bf16[32,64,128]{2,1,0:T(8,128)(2,1)} collective-permute-done((bf16[32,64,128]{2,1,0:T(8,128)(2,1)}, bf16[32,64,128]{2,1,0:T(8,128)(2,1)}, u32[]{:S(2)}, u32[]{:S(2)}) %collective-permute-start.8) | collective-permute-done | bytes 524320 | tf_op jit(solution)/shard_map/gather_far/ppermute | solution.py:35
  71.0 10.7 %blocks.1 = (bf16[4,64,128]{2,1,0:T(8,128)(2,1)S(1)}, bf16[32,64,128]{2,1,0:T(8,128)(2,1)}, bf16[64,64,128]{2,1,0:T(8,128)(2,1)}, bf16[64,64,128]{2,1,0:T(8,128)...) custom-call(s32[1]{0:T(128)} %bitcast.core, ...), custom_call_target="tpu_custom_call" | custom-call | flops 872415232 | bytes 15204352 | tf_op jit(solution)/shard_map/blocks/pallas_call | solution.py:202
  83.7 5.3 %collective-permute-start.11 = (bf16[64,64,128]{2,1,0:T(8,128)(2,1)}, bf16[64,64,128]{2,1,0:T(8,128)(2,1)}, u32[]{:S(2)}, u32[]{:S(2)}) collective-permute-start(bf16[64,64,128]{2,1,0:T(8,128)(2,1)} %get-tuple-element.31), channel_id=1, source_target_pairs={{0,56},{4,452},{8,16},{12,460},{16,8},{20,468},{24,32},{28,476},{3... | collective-permute-start | bytes 3145736 | tf_op jit(solution)/shard_map/reduce_far/ppermute | solution.py:35
  89.0 10.0 %all-to-all-start.1 = ((bf16[8,1088,128]{2,1,0:T(8,128)(2,1)}), bf16[8,1088,128]{2,1,0:T(8,128)(2,1)S(1)}, u32[]{:S(2)}, u32[]{:S(2)}) async-start(bf16[8,1088,128]{2,1,0:T(8,128)(2,1)} %get-tuple-element.34), calls=%async_computation.1 | async-start | bytes 4456448 | tf_op jit(solution)/shard_map/weight_grad/all_to_all | solution.py:352
  99.0 2.0 %collective-permute-start.12 = (bf16[32,64,128]{2,1,0:T(8,128)(2,1)}, bf16[32,64,128]{2,1,0:T(8,128)(2,1)S(1)}, u32[]{:S(2)}, u32[]{:S(2)}) collective-permute-start(bf16[32,64,128]{2,1,0:T(8,128)(2,1)} %get-tuple-element.32), channel_id=1, source_target_pairs={{0,16},{4,132},{8,56},{12,140},{16,32},{20,148},{24,8},{28,156},{3... | collective-permute-start | bytes 1572872 | tf_op jit(solution)/shard_map/reduce_far/ppermute | solution.py:35
  102.7 5.5 %collective-permute-start.14 = (bf16[32,64,128]{2,1,0:T(8,128)(2,1)S(1)}, bf16[32,64,128]{2,1,0:T(8,128)(2,1)S(1)}, u32[]{:S(2)}, u32[]{:S(2)}) collective-permute-start(bf16[32,64,128]{2,1,0:T(8,128)(2,1)S(1)} %add_convert_fusion.2), channel_id=1, source_target_pairs={{0,48},{4,388},{8,24},{12,396},{16,0},{20,404},{24,40},{28,412},{3... | collective-permute-start | bytes 1572872 | tf_op jit(solution)/shard_map/reduce_far/ppermute | solution.py:35
  108.2 8.8 %collective-permute-done.12 = bf16[32,64,128]{2,1,0:T(8,128)(2,1)S(1)} collective-permute-done((bf16[32,64,128]{2,1,0:T(8,128)(2,1)}, bf16[32,64,128]{2,1,0:T(8,128)(2,1)S(1)}, u32[]{:S(2)}, u32[]{:S(2)}) %collective-permute-start.12) | collective-permute-done | bytes 524320 | tf_op jit(solution)/shard_map/reduce_far/ppermute | solution.py:35
  118.5 1.9 %collective-permute-start.13 = (bf16[32,64,128]{2,1,0:T(8,128)(2,1)S(1)}, bf16[32,64,128]{2,1,0:T(8,128)(2,1)S(1)}, u32[]{:S(2)}, u32[]{:S(2)}) collective-permute-start(bf16[32,64,128]{2,1,0:T(8,128)(2,1)S(1)} %add_convert_fusion.1), channel_id=1, source_target_pairs={{0,16},{4,132},{8,56},{12,140},{16,32},{20,148},{24,8},{28,156},{3... | collective-permute-start | bytes 1572872 | tf_op jit(solution)/shard_map/reduce_far/ppermute | solution.py:35
  121.9 8.6 %collective-permute-done.13 = bf16[32,64,128]{2,1,0:T(8,128)(2,1)S(1)} collective-permute-done((bf16[32,64,128]{2,1,0:T(8,128)(2,1)S(1)}, bf16[32,64,128]{2,1,0:T(8,128)(2,1)S(1)}, u32[]{:S(2)}, u32[]{:S(2)}) %collective-permute-start.13) | collective-permute-done | bytes 524320 | tf_op jit(solution)/shard_map/reduce_far/ppermute | solution.py:35
  131.5 3.7 %all-to-all-start.2 = ((bf16[8,256,128]{2,1,0:T(8,128)(2,1)}), bf16[8,256,128]{2,1,0:T(8,128)(2,1)S(1)}, u32[]{:S(2)}, u32[]{:S(2)}) async-start(bf16[8,256,128]{2,1,0:T(8,128)(2,1)} %bitcast.33), calls=%async_computation.2 | async-start | bytes 1048576 | tf_op jit(solution)/shard_map/reduce_near/all_to_all | solution.py:43
  135.3 1.9 %collective-permute-start.9 = (bf16[2,64,128]{2,1,0:T(8,128)(2,1)S(1)}, bf16[2,64,128]{2,1,0:T(8,128)(2,1)S(1)}, u32[]{:S(2)}, u32[]{:S(2)}) collective-permute-start(bf16[2,64,128]{2,1,0:T(8,128)(2,1)S(1)} %slice.53), channel_id=1, source_target_pairs={{0,4},{4,0},{8,12},{12,8},{16,20},{20,16},{24,28},{28,24},{32,36},... | collective-permute-start | bytes 98312 | tf_op jit(solution)/shard_map/swap_back/ppermute | solution.py:39
  138.4 2.0 %reduce_near.1 = bf16[2,26,32,256]{3,2,1,0:T(8,128)(2,1)} custom-call(bf16[8,1088,128]{2,1,0:T(8,128)(2,1)S(1)} %all-to-all-done.1.refs_0_), custom_call_target="tpu_custom_call" | custom-call | flops 872415232 | bytes 3080192 | tf_op jit(solution)/shard_map/reduce_near/pallas_call | solution.py:265
  140.4 7.0 %all-to-all-done.2 = bf16[8,256,128]{2,1,0:T(8,128)(2,1)S(1)} async-done(((bf16[8,256,128]{2,1,0:T(8,128)(2,1)}), bf16[8,256,128]{2,1,0:T(8,128)(2,1)S(1)}, u32[]{:S(2)}, u32[]{:S(2)}) %all-to-all-start.2) | async-done | bytes 524320 | tf_op jit(solution)/shard_map/reduce_near/all_to_all | solution.py:43
  147.5 1.9 %collective-permute-start.15 = (bf16[2,64,128]{2,1,0:T(8,128)(2,1)S(1)}, bf16[2,64,128]{2,1,0:T(8,128)(2,1)S(1)}, u32[]{:S(2)}, u32[]{:S(2)}) collective-permute-start(bf16[2,64,128]{2,1,0:T(8,128)(2,1)S(1)} %bitcast.39), channel_id=1, source_target_pairs={{0,4},{4,0},{8,12},{12,8},{16,20},{20,16},{24,28},{28,24},{32,36},... | collective-permute-start | bytes 98312 | tf_op jit(solution)/shard_map/swap_back/ppermute | solution.py:39
  (55 shorter events, 19.2 us)
Async XLA Ops:
  1.5 9.7 %collective-permute-start = (bf16[2,64,256]{2,1,0:T(8,128)(2,1)S(1)}, bf16[2,64,256]{2,1,0:T(8,128)(2,1)S(1)}, u32[]{:S(2)}, u32[]{:S(2)}) collective-permute-start(bf16[2,64,256]{2,1,0:T(8,128)(2,1)S(1)} %get-tuple-element.40), channel_id=1, source_target_pairs={{0,4},{4,0},{8,12},{12,8},{16,20},{20,16},{24,28},{28,24},{32,36},... | collective-permute-start | bytes 196616 | tf_op jit(solution)/shard_map/swap_tokens/ppermute | solution.py:39
  28.2 21.9 %collective-permute-start.4 = (bf16[2,26,128,256]{3,2,1,0:T(8,128)(2,1)}, bf16[2,26,128,256]{3,2,1,0:T(8,128)(2,1)S(1)}, u32[]{:S(2)}, u32[]{:S(2)}) collective-permute-start(bf16[2,26,128,256]{3,2,1,0:T(8,128)(2,1)} %param.6), channel_id=1, source_target_pairs={{0,4},{4,0},{8,12},{12,8},{16,20},{20,16},{24,28},{28,24},{32,36},... | collective-permute-start | bytes 10223624 | tf_op jit(solution)/shard_map/gather_far/ppermute | solution.py:39
  30.1 17.9 %collective-permute-start.2 = (bf16[32,64,128]{2,1,0:T(8,128)(2,1)}, bf16[32,64,128]{2,1,0:T(8,128)(2,1)}, u32[]{:S(2)}, u32[]{:S(2)}) collective-permute-start(bf16[32,64,128]{2,1,0:T(8,128)(2,1)} %bitcast.5.refs_0_), channel_id=1, source_target_pairs={{0,48},{4,388},{8,24},{12,396},{16,0},{20,404},{24,40},{28,412},{3... | collective-permute-start | bytes 1572872 | tf_op jit(solution)/shard_map/gather_far/ppermute | solution.py:35
  36.0 14.1 %collective-permute-start.3 = (bf16[32,64,128]{2,1,0:T(8,128)(2,1)}, bf16[32,64,128]{2,1,0:T(8,128)(2,1)}, u32[]{:S(2)}, u32[]{:S(2)}) collective-permute-start(bf16[32,64,128]{2,1,0:T(8,128)(2,1)} %bitcast.5.refs_0_), channel_id=1, source_target_pairs={{0,16},{4,132},{8,56},{12,140},{16,32},{20,148},{24,8},{28,156},{3... | collective-permute-start | bytes 1572872 | tf_op jit(solution)/shard_map/gather_far/ppermute | solution.py:35
  40.7 21.0 %collective-permute-start.1 = (bf16[32,64,128]{2,1,0:T(8,128)(2,1)}, bf16[32,64,128]{2,1,0:T(8,128)(2,1)}, u32[]{:S(2)}, u32[]{:S(2)}) collective-permute-start(bf16[32,64,128]{2,1,0:T(8,128)(2,1)} %bitcast.5.refs_0_), channel_id=1, source_target_pairs={{0,8},{4,68},{8,0},{12,76},{16,24},{20,84},{24,16},{28,92},{32,40}... | collective-permute-start | bytes 1572872 | tf_op jit(solution)/shard_map/gather_far/ppermute | solution.py:35
  48.1 17.4 %collective-permute-start.7 = (bf16[32,64,128]{2,1,0:T(8,128)(2,1)}, bf16[32,64,128]{2,1,0:T(8,128)(2,1)}, u32[]{:S(2)}, u32[]{:S(2)}) collective-permute-start(bf16[32,64,128]{2,1,0:T(8,128)(2,1)} %collective-permute-done.2.refs_2_), channel_id=1, source_target_pairs={{0,56},{4,452},{8,16},{12,460},{16,8},{20,468},{24,32},{28,476},{3... | collective-permute-start | bytes 1572872 | tf_op jit(solution)/shard_map/gather_far/ppermute | solution.py:35
  50.1 20.9 %collective-permute-start.6 = (bf16[32,64,128]{2,1,0:T(8,128)(2,1)}, bf16[32,64,128]{2,1,0:T(8,128)(2,1)}, u32[]{:S(2)}, u32[]{:S(2)}) collective-permute-start(bf16[32,64,128]{2,1,0:T(8,128)(2,1)} %collective-permute-done.3.refs_6_), channel_id=1, source_target_pairs={{0,16},{4,132},{8,56},{12,140},{16,32},{20,148},{24,8},{28,156},{3... | collective-permute-start | bytes 1572872 | tf_op jit(solution)/shard_map/gather_far/ppermute | solution.py:35
  52.5 18.5 %collective-permute-start.5 = (bf16[32,64,128]{2,1,0:T(8,128)(2,1)}, bf16[32,64,128]{2,1,0:T(8,128)(2,1)}, u32[]{:S(2)}, u32[]{:S(2)}) collective-permute-start(bf16[32,64,128]{2,1,0:T(8,128)(2,1)} %collective-permute-done.3.refs_6_), channel_id=1, source_target_pairs={{0,8},{4,68},{8,0},{12,76},{16,24},{20,84},{24,16},{28,92},{32,40}... | collective-permute-start | bytes 1572872 | tf_op jit(solution)/shard_map/gather_far/ppermute | solution.py:35
  57.7 13.4 %collective-permute-start.8 = (bf16[32,64,128]{2,1,0:T(8,128)(2,1)}, bf16[32,64,128]{2,1,0:T(8,128)(2,1)}, u32[]{:S(2)}, u32[]{:S(2)}) collective-permute-start(bf16[32,64,128]{2,1,0:T(8,128)(2,1)} %bitcast.5.refs_0_), channel_id=1, source_target_pairs={{0,56},{4,452},{8,16},{12,460},{16,8},{20,468},{24,32},{28,476},{3... | collective-permute-start | bytes 1572872 | tf_op jit(solution)/shard_map/gather_far/ppermute | solution.py:35
  81.8 19.3 %collective-permute-start.10 = (bf16[64,64,128]{2,1,0:T(8,128)(2,1)}, bf16[64,64,128]{2,1,0:T(8,128)(2,1)S(1)}, u32[]{:S(2)}, u32[]{:S(2)}) collective-permute-start(bf16[64,64,128]{2,1,0:T(8,128)(2,1)} %get-tuple-element.29), channel_id=1, source_target_pairs={{0,8},{4,68},{8,0},{12,76},{16,24},{20,84},{24,16},{28,92},{32,40}... | collective-permute-start | bytes 3145736 | tf_op jit(solution)/shard_map/reduce_far/ppermute | solution.py:35
  83.7 33.3 %collective-permute-start.11 = (bf16[64,64,128]{2,1,0:T(8,128)(2,1)}, bf16[64,64,128]{2,1,0:T(8,128)(2,1)}, u32[]{:S(2)}, u32[]{:S(2)}) collective-permute-start(bf16[64,64,128]{2,1,0:T(8,128)(2,1)} %get-tuple-element.31), channel_id=1, source_target_pairs={{0,56},{4,452},{8,16},{12,460},{16,8},{20,468},{24,32},{28,476},{3... | collective-permute-start | bytes 3145736 | tf_op jit(solution)/shard_map/reduce_far/ppermute | solution.py:35
  89.0 42.5 %all-to-all-start.1 = ((bf16[8,1088,128]{2,1,0:T(8,128)(2,1)}), bf16[8,1088,128]{2,1,0:T(8,128)(2,1)S(1)}, u32[]{:S(2)}, u32[]{:S(2)}) async-start(bf16[8,1088,128]{2,1,0:T(8,128)(2,1)} %get-tuple-element.34), calls=%async_computation.1 | async-start | bytes 4456448 | tf_op jit(solution)/shard_map/weight_grad/all_to_all | solution.py:352
  99.0 21.4 %copy-start.1 = (bf16[32,64,128]{2,1,0:T(8,128)(2,1)S(1)}, bf16[32,64,128]{2,1,0:T(8,128)(2,1)}, u32[]{:S(2)}) copy-start(bf16[32,64,128]{2,1,0:T(8,128)(2,1)} %get-tuple-element.33) | copy-start | bytes 1572868
  99.0 18.0 %collective-permute-start.12 = (bf16[32,64,128]{2,1,0:T(8,128)(2,1)}, bf16[32,64,128]{2,1,0:T(8,128)(2,1)S(1)}, u32[]{:S(2)}, u32[]{:S(2)}) collective-permute-start(bf16[32,64,128]{2,1,0:T(8,128)(2,1)} %get-tuple-element.32), channel_id=1, source_target_pairs={{0,16},{4,132},{8,56},{12,140},{16,32},{20,148},{24,8},{28,156},{3... | collective-permute-start | bytes 1572872 | tf_op jit(solution)/shard_map/reduce_far/ppermute | solution.py:35
  101.1 19.3 %copy-start = (bf16[64,64,128]{2,1,0:T(8,128)(2,1)}, bf16[64,64,128]{2,1,0:T(8,128)(2,1)S(1)}, u32[]{:S(2)}) copy-start(bf16[64,64,128]{2,1,0:T(8,128)(2,1)S(1)} %collective-permute-done.10) | copy-start | bytes 3145732
  102.7 19.2 %collective-permute-start.14 = (bf16[32,64,128]{2,1,0:T(8,128)(2,1)S(1)}, bf16[32,64,128]{2,1,0:T(8,128)(2,1)S(1)}, u32[]{:S(2)}, u32[]{:S(2)}) collective-permute-start(bf16[32,64,128]{2,1,0:T(8,128)(2,1)S(1)} %add_convert_fusion.2), channel_id=1, source_target_pairs={{0,48},{4,388},{8,24},{12,396},{16,0},{20,404},{24,40},{28,412},{3... | collective-permute-start | bytes 1572872 | tf_op jit(solution)/shard_map/reduce_far/ppermute | solution.py:35
  118.5 12.0 %collective-permute-start.13 = (bf16[32,64,128]{2,1,0:T(8,128)(2,1)S(1)}, bf16[32,64,128]{2,1,0:T(8,128)(2,1)S(1)}, u32[]{:S(2)}, u32[]{:S(2)}) collective-permute-start(bf16[32,64,128]{2,1,0:T(8,128)(2,1)S(1)} %add_convert_fusion.1), channel_id=1, source_target_pairs={{0,16},{4,132},{8,56},{12,140},{16,32},{20,148},{24,8},{28,156},{3... | collective-permute-start | bytes 1572872 | tf_op jit(solution)/shard_map/reduce_far/ppermute | solution.py:35
  131.5 15.9 %all-to-all-start.2 = ((bf16[8,256,128]{2,1,0:T(8,128)(2,1)}), bf16[8,256,128]{2,1,0:T(8,128)(2,1)S(1)}, u32[]{:S(2)}, u32[]{:S(2)}) async-start(bf16[8,256,128]{2,1,0:T(8,128)(2,1)} %bitcast.33), calls=%async_computation.2 | async-start | bytes 1048576 | tf_op jit(solution)/shard_map/reduce_near/all_to_all | solution.py:43
  135.3 3.1 %collective-permute-start.9 = (bf16[2,64,128]{2,1,0:T(8,128)(2,1)S(1)}, bf16[2,64,128]{2,1,0:T(8,128)(2,1)S(1)}, u32[]{:S(2)}, u32[]{:S(2)}) collective-permute-start(bf16[2,64,128]{2,1,0:T(8,128)(2,1)S(1)} %slice.53), channel_id=1, source_target_pairs={{0,4},{4,0},{8,12},{12,8},{16,20},{20,16},{24,28},{28,24},{32,36},... | collective-permute-start | bytes 98312 | tf_op jit(solution)/shard_map/swap_back/ppermute | solution.py:39
  147.5 3.1 %collective-permute-start.15 = (bf16[2,64,128]{2,1,0:T(8,128)(2,1)S(1)}, bf16[2,64,128]{2,1,0:T(8,128)(2,1)S(1)}, u32[]{:S(2)}, u32[]{:S(2)}) collective-permute-start(bf16[2,64,128]{2,1,0:T(8,128)(2,1)S(1)} %bitcast.39), channel_id=1, source_target_pairs={{0,4},{4,0},{8,12},{12,8},{16,20},{20,16},{24,28},{28,24},{32,36},... | collective-permute-start | bytes 98312 | tf_op jit(solution)/shard_map/swap_back/ppermute | solution.py:39

commit v7 on v5

--- a/solution.py
+++ b/solution.py
@@ -340,8 +340,7 @@
     def rejoin(keep, came):
         low = jnp.where(first, keep, came)
         high = jnp.where(first, came, keep)
-        whole = jnp.stack([low, high])
-        return jnp.transpose(whole, (0, 2, 1, 3)).reshape(tokens, owned * width)
+        return jnp.concatenate([jnp.concatenate(list(v), axis=1) for v in (low, high)])
 
     with jax.named_scope("reduce_far"):
         column = far_reduce(*terms)

time: 152 us -> 151 us (level)
  no operation moved by 1% of the time
where the time goes in v7:
time: 151 us; the launch traced here: 150 us
  starting transfers between devices  68.8 us (46%)
  waiting for transfers between devices  41.1 us (27%)
  blocking collectives  16.7 us (11%)
  Pallas kernels  11.9 us (8%)
  other arithmetic  9.26 us (6%)
  local copies, waits for them, and re-layouts  1.56 us (1%)
    ppermute x12, starting transfers between devices, far_shift(): return lax.ppermute(value, 'blk', pairs)  40.6 us
    ppermute x12, waiting for transfers between devices, far_shift(): return lax.ppermute(value, 'blk', pairs)  31.6 us
    all_to_all x1, blocking collectives, near_exchange(): lax.all_to_all(value, 'blk', 0, 0, axis_index_groups=GROUPS_NEAR, tiled=T...  16.7 us
    ppermute x4, starting transfers between devices, swap_cores(): return lax.ppermute(value, 'blk', SWAP)  14.5 us
    all_to_all x1, starting transfers between devices, local(): lax.all_to_all(packed, BOTH, 0, 0, axis_index_groups=groups, tiled=True)  10 us
    pallas_call x1, Pallas kernels, run_blocks(): pl.pallas_call(block_kernel, in_specs=[scalars] * 2 + [outside] * 9 + [wh...  9.96 us
    all_to_all x1, waiting for transfers between devices, near_exchange(): lax.all_to_all(value, 'blk', 0, 0, axis_index_groups=GROUPS_NEAR, tiled=T...  7 us
    convert_element_type x3, other arithmetic, add(): return sum((value.astype(F32) for value in values)).astype(BF)  4.08 us
  transfers between devices with their start and end apart: 18, of which 10 were waited for; matrix products, arithmetic and copies ran while one was open for 6% of the time, Pallas kernels for 1%

profile of v7, /device:TPU:1, one launch (start us, length us, event | category | flops | bytes accessed | tf_op | source)
XLA Modules:
  0.0 150.5 jit_solution(17085796912978863096)
XLA Ops:
  1.5 8.8 %collective-permute-start = (bf16[2,64,256]{2,1,0:T(8,128)(2,1)S(1)}, bf16[2,64,256]{2,1,0:T(8,128)(2,1)S(1)}, u32[]{:S(2)}, u32[]{:S(2)}) collective-permute-start(bf16[2,64,256]{2,1,0:T(8,128)(2,1)S(1)} %get-tuple-element.40), channel_id=1, source_target_pairs={{0,4},{4,0},{8,12},{12,8},{16,20},{20,16},{24,28},{28,24},{32,36},... | collective-permute-start | bytes 196616 | tf_op jit(solution)/shard_map/swap_tokens/ppermute | solution.py:39
  11.5 16.7 %all_to_all.15 = bf16[8,4,64,128]{3,2,1,0:T(8,128)(2,1)} all-to-all(bf16[8,4,64,128]{3,2,1,0:T(8,128)(2,1)S(1)} %broadcast_in_dim.23), channel_id=1, replica_groups={{0,64,128,192,256,320,384,448},{8,72,136,200,264,328,392,456},{16,80,14..., dimensions={0} | all-to-all | bytes 1048576 | tf_op jit(solution)/shard_map/gather_near/all_to_all | solution.py:43
  30.1 5.9 %collective-permute-start.2 = (bf16[32,64,128]{2,1,0:T(8,128)(2,1)}, bf16[32,64,128]{2,1,0:T(8,128)(2,1)}, u32[]{:S(2)}, u32[]{:S(2)}) collective-permute-start(bf16[32,64,128]{2,1,0:T(8,128)(2,1)} %bitcast.5.refs_0_), channel_id=1, source_target_pairs={{0,48},{4,388},{8,24},{12,396},{16,0},{20,404},{24,40},{28,412},{3... | collective-permute-start | bytes 1572872 | tf_op jit(solution)/shard_map/gather_far/ppermute | solution.py:35
  36.0 1.9 %collective-permute-start.3 = (bf16[32,64,128]{2,1,0:T(8,128)(2,1)}, bf16[32,64,128]{2,1,0:T(8,128)(2,1)}, u32[]{:S(2)}, u32[]{:S(2)}) collective-permute-start(bf16[32,64,128]{2,1,0:T(8,128)(2,1)} %bitcast.5.refs_0_), channel_id=1, source_target_pairs={{0,16},{4,132},{8,56},{12,140},{16,32},{20,148},{24,8},{28,156},{3... | collective-permute-start | bytes 1572872 | tf_op jit(solution)/shard_map/gather_far/ppermute | solution.py:35
  40.7 2.8 %collective-permute-start.1 = (bf16[32,64,128]{2,1,0:T(8,128)(2,1)}, bf16[32,64,128]{2,1,0:T(8,128)(2,1)}, u32[]{:S(2)}, u32[]{:S(2)}) collective-permute-start(bf16[32,64,128]{2,1,0:T(8,128)(2,1)} %bitcast.5.refs_0_), channel_id=1, source_target_pairs={{0,8},{4,68},{8,0},{12,76},{16,24},{20,84},{24,16},{28,92},{32,40}... | collective-permute-start | bytes 1572872 | tf_op jit(solution)/shard_map/gather_far/ppermute | solution.py:35
  43.5 4.6 %collective-permute-done.2.refs_2_ = bf16[32,64,128]{2,1,0:T(8,128)(2,1)} collective-permute-done((bf16[32,64,128]{2,1,0:T(8,128)(2,1)}, bf16[32,64,128]{2,1,0:T(8,128)(2,1)}, u32[]{:S(2)}, u32[]{:S(2)}) %collective-permute-start.2) | collective-permute-done | bytes 524320 | tf_op jit(solution)/shard_map/gather_far/ppermute | solution.py:35
  50.1 2.4 %collective-permute-start.6 = (bf16[32,64,128]{2,1,0:T(8,128)(2,1)}, bf16[32,64,128]{2,1,0:T(8,128)(2,1)}, u32[]{:S(2)}, u32[]{:S(2)}) collective-permute-start(bf16[32,64,128]{2,1,0:T(8,128)(2,1)} %collective-permute-done.3.refs_6_), channel_id=1, source_target_pairs={{0,16},{4,132},{8,56},{12,140},{16,32},{20,148},{24,8},{28,156},{3... | collective-permute-start | bytes 1572872 | tf_op jit(solution)/shard_map/gather_far/ppermute | solution.py:35
  52.5 5.2 %collective-permute-start.5 = (bf16[32,64,128]{2,1,0:T(8,128)(2,1)}, bf16[32,64,128]{2,1,0:T(8,128)(2,1)}, u32[]{:S(2)}, u32[]{:S(2)}) collective-permute-start(bf16[32,64,128]{2,1,0:T(8,128)(2,1)} %collective-permute-done.3.refs_6_), channel_id=1, source_target_pairs={{0,8},{4,68},{8,0},{12,76},{16,24},{20,84},{24,16},{28,92},{32,40}... | collective-permute-start | bytes 1572872 | tf_op jit(solution)/shard_map/gather_far/ppermute | solution.py:35
  57.7 3.8 %collective-permute-start.8 = (bf16[32,64,128]{2,1,0:T(8,128)(2,1)}, bf16[32,64,128]{2,1,0:T(8,128)(2,1)}, u32[]{:S(2)}, u32[]{:S(2)}) collective-permute-start(bf16[32,64,128]{2,1,0:T(8,128)(2,1)} %bitcast.5.refs_0_), channel_id=1, source_target_pairs={{0,56},{4,452},{8,16},{12,460},{16,8},{20,468},{24,32},{28,476},{3... | collective-permute-start | bytes 1572872 | tf_op jit(solution)/shard_map/gather_far/ppermute | solution.py:35
  61.6 3.8 %collective-permute-done.7.refs_5_ = bf16[32,64,128]{2,1,0:T(8,128)(2,1)} collective-permute-done((bf16[32,64,128]{2,1,0:T(8,128)(2,1)}, bf16[32,64,128]{2,1,0:T(8,128)(2,1)}, u32[]{:S(2)}, u32[]{:S(2)}) %collective-permute-start.7) | collective-permute-done | bytes 524320 | tf_op jit(solution)/shard_map/gather_far/ppermute | solution.py:35
  65.4 5.6 %collective-permute-done.8.refs_7_ = bf16[32,64,128]{2,1,0:T(8,128)(2,1)} collective-permute-done((bf16[32,64,128]{2,1,0:T(8,128)(2,1)}, bf16[32,64,128]{2,1,0:T(8,128)(2,1)}, u32[]{:S(2)}, u32[]{:S(2)}) %collective-permute-start.8) | collective-permute-done | bytes 524320 | tf_op jit(solution)/shard_map/gather_far/ppermute | solution.py:35
  71.0 10.0 %blocks.1 = (bf16[4,64,128]{2,1,0:T(8,128)(2,1)S(1)}, bf16[32,64,128]{2,1,0:T(8,128)(2,1)}, bf16[64,64,128]{2,1,0:T(8,128)(2,1)}, bf16[64,64,128]{2,1,0:T(8,128)...) custom-call(s32[1]{0:T(128)} %bitcast.core, ...), custom_call_target="tpu_custom_call" | custom-call | flops 872415232 | bytes 15204352 | tf_op jit(solution)/shard_map/blocks/pallas_call | solution.py:200
  82.9 5.3 %collective-permute-start.11 = (bf16[64,64,128]{2,1,0:T(8,128)(2,1)}, bf16[64,64,128]{2,1,0:T(8,128)(2,1)}, u32[]{:S(2)}, u32[]{:S(2)}) collective-permute-start(bf16[64,64,128]{2,1,0:T(8,128)(2,1)} %get-tuple-element.31), channel_id=1, source_target_pairs={{0,56},{4,452},{8,16},{12,460},{16,8},{20,468},{24,32},{28,476},{3... | collective-permute-start | bytes 3145736 | tf_op jit(solution)/shard_map/reduce_far/ppermute | solution.py:35
  88.2 10.0 %all-to-all-start.1 = ((bf16[8,1088,128]{2,1,0:T(8,128)(2,1)}), bf16[8,1088,128]{2,1,0:T(8,128)(2,1)S(1)}, u32[]{:S(2)}, u32[]{:S(2)}) async-start(bf16[8,1088,128]{2,1,0:T(8,128)(2,1)} %get-tuple-element.34), calls=%async_computation.1 | async-start | bytes 4456448 | tf_op jit(solution)/shard_map/weight_grad/all_to_all | solution.py:350
  98.2 2.0 %collective-permute-start.12 = (bf16[32,64,128]{2,1,0:T(8,128)(2,1)}, bf16[32,64,128]{2,1,0:T(8,128)(2,1)S(1)}, u32[]{:S(2)}, u32[]{:S(2)}) collective-permute-start(bf16[32,64,128]{2,1,0:T(8,128)(2,1)} %get-tuple-element.32), channel_id=1, source_target_pairs={{0,16},{4,132},{8,56},{12,140},{16,32},{20,148},{24,8},{28,156},{3... | collective-permute-start | bytes 1572872 | tf_op jit(solution)/shard_map/reduce_far/ppermute | solution.py:35
  101.9 5.5 %collective-permute-start.14 = (bf16[32,64,128]{2,1,0:T(8,128)(2,1)S(1)}, bf16[32,64,128]{2,1,0:T(8,128)(2,1)S(1)}, u32[]{:S(2)}, u32[]{:S(2)}) collective-permute-start(bf16[32,64,128]{2,1,0:T(8,128)(2,1)S(1)} %add_convert_fusion.2), channel_id=1, source_target_pairs={{0,48},{4,388},{8,24},{12,396},{16,0},{20,404},{24,40},{28,412},{3... | collective-permute-start | bytes 1572872 | tf_op jit(solution)/shard_map/reduce_far/ppermute | solution.py:35
  107.4 8.8 %collective-permute-done.12 = bf16[32,64,128]{2,1,0:T(8,128)(2,1)S(1)} collective-permute-done((bf16[32,64,128]{2,1,0:T(8,128)(2,1)}, bf16[32,64,128]{2,1,0:T(8,128)(2,1)S(1)}, u32[]{:S(2)}, u32[]{:S(2)}) %collective-permute-start.12) | collective-permute-done | bytes 524320 | tf_op jit(solution)/shard_map/reduce_far/ppermute | solution.py:35
  117.7 1.9 %collective-permute-start.13 = (bf16[32,64,128]{2,1,0:T(8,128)(2,1)S(1)}, bf16[32,64,128]{2,1,0:T(8,128)(2,1)S(1)}, u32[]{:S(2)}, u32[]{:S(2)}) collective-permute-start(bf16[32,64,128]{2,1,0:T(8,128)(2,1)S(1)} %add_convert_fusion.1), channel_id=1, source_target_pairs={{0,16},{4,132},{8,56},{12,140},{16,32},{20,148},{24,8},{28,156},{3... | collective-permute-start | bytes 1572872 | tf_op jit(solution)/shard_map/reduce_far/ppermute | solution.py:35
  121.1 8.6 %collective-permute-done.13 = bf16[32,64,128]{2,1,0:T(8,128)(2,1)S(1)} collective-permute-done((bf16[32,64,128]{2,1,0:T(8,128)(2,1)S(1)}, bf16[32,64,128]{2,1,0:T(8,128)(2,1)S(1)}, u32[]{:S(2)}, u32[]{:S(2)}) %collective-permute-start.13) | collective-permute-done | bytes 524320 | tf_op jit(solution)/shard_map/reduce_far/ppermute | solution.py:35
  130.8 3.7 %all-to-all-start.2 = ((bf16[8,256,128]{2,1,0:T(8,128)(2,1)}), bf16[8,256,128]{2,1,0:T(8,128)(2,1)S(1)}, u32[]{:S(2)}, u32[]{:S(2)}) async-start(bf16[8,256,128]{2,1,0:T(8,128)(2,1)} %bitcast.33), calls=%async_computation.2 | async-start | bytes 1048576 | tf_op jit(solution)/shard_map/reduce_near/all_to_all | solution.py:43
  134.5 1.9 %collective-permute-start.9 = (bf16[2,64,128]{2,1,0:T(8,128)(2,1)S(1)}, bf16[2,64,128]{2,1,0:T(8,128)(2,1)S(1)}, u32[]{:S(2)}, u32[]{:S(2)}) collective-permute-start(bf16[2,64,128]{2,1,0:T(8,128)(2,1)S(1)} %slice.53), channel_id=1, source_target_pairs={{0,4},{4,0},{8,12},{12,8},{16,20},{20,16},{24,28},{28,24},{32,36},... | collective-permute-start | bytes 98312 | tf_op jit(solution)/shard_map/swap_back/ppermute | solution.py:39
  137.6 2.0 %reduce_near.1 = bf16[2,26,32,256]{3,2,1,0:T(8,128)(2,1)} custom-call(bf16[8,1088,128]{2,1,0:T(8,128)(2,1)S(1)} %all-to-all-done.1.refs_0_), custom_call_target="tpu_custom_call" | custom-call | flops 872415232 | bytes 3080192 | tf_op jit(solution)/shard_map/reduce_near/pallas_call | solution.py:263
  139.6 7.0 %all-to-all-done.2 = bf16[8,256,128]{2,1,0:T(8,128)(2,1)S(1)} async-done(((bf16[8,256,128]{2,1,0:T(8,128)(2,1)}), bf16[8,256,128]{2,1,0:T(8,128)(2,1)S(1)}, u32[]{:S(2)}, u32[]{:S(2)}) %all-to-all-start.2) | async-done | bytes 524320 | tf_op jit(solution)/shard_map/reduce_near/all_to_all | solution.py:43
  146.7 1.9 %collective-permute-start.15 = (bf16[2,64,128]{2,1,0:T(8,128)(2,1)S(1)}, bf16[2,64,128]{2,1,0:T(8,128)(2,1)S(1)}, u32[]{:S(2)}, u32[]{:S(2)}) collective-permute-start(bf16[2,64,128]{2,1,0:T(8,128)(2,1)S(1)} %bitcast.39), channel_id=1, source_target_pairs={{0,4},{4,0},{8,12},{12,8},{16,20},{20,16},{24,28},{28,24},{32,36},... | collective-permute-start | bytes 98312 | tf_op jit(solution)/shard_map/swap_back/ppermute | solution.py:39
  (55 shorter events, 19.2 us)
Async XLA Ops:
  1.5 9.7 %collective-permute-start = (bf16[2,64,256]{2,1,0:T(8,128)(2,1)S(1)}, bf16[2,64,256]{2,1,0:T(8,128)(2,1)S(1)}, u32[]{:S(2)}, u32[]{:S(2)}) collective-permute-start(bf16[2,64,256]{2,1,0:T(8,128)(2,1)S(1)} %get-tuple-element.40), channel_id=1, source_target_pairs={{0,4},{4,0},{8,12},{12,8},{16,20},{20,16},{24,28},{28,24},{32,36},... | collective-permute-start | bytes 196616 | tf_op jit(solution)/shard_map/swap_tokens/ppermute | solution.py:39
  28.2 21.9 %collective-permute-start.4 = (bf16[2,26,128,256]{3,2,1,0:T(8,128)(2,1)}, bf16[2,26,128,256]{3,2,1,0:T(8,128)(2,1)S(1)}, u32[]{:S(2)}, u32[]{:S(2)}) collective-permute-start(bf16[2,26,128,256]{3,2,1,0:T(8,128)(2,1)} %param.6), channel_id=1, source_target_pairs={{0,4},{4,0},{8,12},{12,8},{16,20},{20,16},{24,28},{28,24},{32,36},... | collective-permute-start | bytes 10223624 | tf_op jit(solution)/shard_map/gather_far/ppermute | solution.py:39
  30.1 17.9 %collective-permute-start.2 = (bf16[32,64,128]{2,1,0:T(8,128)(2,1)}, bf16[32,64,128]{2,1,0:T(8,128)(2,1)}, u32[]{:S(2)}, u32[]{:S(2)}) collective-permute-start(bf16[32,64,128]{2,1,0:T(8,128)(2,1)} %bitcast.5.refs_0_), channel_id=1, source_target_pairs={{0,48},{4,388},{8,24},{12,396},{16,0},{20,404},{24,40},{28,412},{3... | collective-permute-start | bytes 1572872 | tf_op jit(solution)/shard_map/gather_far/ppermute | solution.py:35
  36.0 14.1 %collective-permute-start.3 = (bf16[32,64,128]{2,1,0:T(8,128)(2,1)}, bf16[32,64,128]{2,1,0:T(8,128)(2,1)}, u32[]{:S(2)}, u32[]{:S(2)}) collective-permute-start(bf16[32,64,128]{2,1,0:T(8,128)(2,1)} %bitcast.5.refs_0_), channel_id=1, source_target_pairs={{0,16},{4,132},{8,56},{12,140},{16,32},{20,148},{24,8},{28,156},{3... | collective-permute-start | bytes 1572872 | tf_op jit(solution)/shard_map/gather_far/ppermute | solution.py:35
  40.7 21.0 %collective-permute-start.1 = (bf16[32,64,128]{2,1,0:T(8,128)(2,1)}, bf16[32,64,128]{2,1,0:T(8,128)(2,1)}, u32[]{:S(2)}, u32[]{:S(2)}) collective-permute-start(bf16[32,64,128]{2,1,0:T(8,128)(2,1)} %bitcast.5.refs_0_), channel_id=1, source_target_pairs={{0,8},{4,68},{8,0},{12,76},{16,24},{20,84},{24,16},{28,92},{32,40}... | collective-permute-start | bytes 1572872 | tf_op jit(solution)/shard_map/gather_far/ppermute | solution.py:35
  48.1 17.4 %collective-permute-start.7 = (bf16[32,64,128]{2,1,0:T(8,128)(2,1)}, bf16[32,64,128]{2,1,0:T(8,128)(2,1)}, u32[]{:S(2)}, u32[]{:S(2)}) collective-permute-start(bf16[32,64,128]{2,1,0:T(8,128)(2,1)} %collective-permute-done.2.refs_2_), channel_id=1, source_target_pairs={{0,56},{4,452},{8,16},{12,460},{16,8},{20,468},{24,32},{28,476},{3... | collective-permute-start | bytes 1572872 | tf_op jit(solution)/shard_map/gather_far/ppermute | solution.py:35
  50.1 20.9 %collective-permute-start.6 = (bf16[32,64,128]{2,1,0:T(8,128)(2,1)}, bf16[32,64,128]{2,1,0:T(8,128)(2,1)}, u32[]{:S(2)}, u32[]{:S(2)}) collective-permute-start(bf16[32,64,128]{2,1,0:T(8,128)(2,1)} %collective-permute-done.3.refs_6_), channel_id=1, source_target_pairs={{0,16},{4,132},{8,56},{12,140},{16,32},{20,148},{24,8},{28,156},{3... | collective-permute-start | bytes 1572872 | tf_op jit(solution)/shard_map/gather_far/ppermute | solution.py:35
  52.5 18.5 %collective-permute-start.5 = (bf16[32,64,128]{2,1,0:T(8,128)(2,1)}, bf16[32,64,128]{2,1,0:T(8,128)(2,1)}, u32[]{:S(2)}, u32[]{:S(2)}) collective-permute-start(bf16[32,64,128]{2,1,0:T(8,128)(2,1)} %collective-permute-done.3.refs_6_), channel_id=1, source_target_pairs={{0,8},{4,68},{8,0},{12,76},{16,24},{20,84},{24,16},{28,92},{32,40}... | collective-permute-start | bytes 1572872 | tf_op jit(solution)/shard_map/gather_far/ppermute | solution.py:35
  57.7 13.4 %collective-permute-start.8 = (bf16[32,64,128]{2,1,0:T(8,128)(2,1)}, bf16[32,64,128]{2,1,0:T(8,128)(2,1)}, u32[]{:S(2)}, u32[]{:S(2)}) collective-permute-start(bf16[32,64,128]{2,1,0:T(8,128)(2,1)} %bitcast.5.refs_0_), channel_id=1, source_target_pairs={{0,56},{4,452},{8,16},{12,460},{16,8},{20,468},{24,32},{28,476},{3... | collective-permute-start | bytes 1572872 | tf_op jit(solution)/shard_map/gather_far/ppermute | solution.py:35
  81.0 19.3 %collective-permute-start.10 = (bf16[64,64,128]{2,1,0:T(8,128)(2,1)}, bf16[64,64,128]{2,1,0:T(8,128)(2,1)S(1)}, u32[]{:S(2)}, u32[]{:S(2)}) collective-permute-start(bf16[64,64,128]{2,1,0:T(8,128)(2,1)} %get-tuple-element.29), channel_id=1, source_target_pairs={{0,8},{4,68},{8,0},{12,76},{16,24},{20,84},{24,16},{28,92},{32,40}... | collective-permute-start | bytes 3145736 | tf_op jit(solution)/shard_map/reduce_far/ppermute | solution.py:35
  82.9 33.3 %collective-permute-start.11 = (bf16[64,64,128]{2,1,0:T(8,128)(2,1)}, bf16[64,64,128]{2,1,0:T(8,128)(2,1)}, u32[]{:S(2)}, u32[]{:S(2)}) collective-permute-start(bf16[64,64,128]{2,1,0:T(8,128)(2,1)} %get-tuple-element.31), channel_id=1, source_target_pairs={{0,56},{4,452},{8,16},{12,460},{16,8},{20,468},{24,32},{28,476},{3... | collective-permute-start | bytes 3145736 | tf_op jit(solution)/shard_map/reduce_far/ppermute | solution.py:35
  88.2 42.5 %all-to-all-start.1 = ((bf16[8,1088,128]{2,1,0:T(8,128)(2,1)}), bf16[8,1088,128]{2,1,0:T(8,128)(2,1)S(1)}, u32[]{:S(2)}, u32[]{:S(2)}) async-start(bf16[8,1088,128]{2,1,0:T(8,128)(2,1)} %get-tuple-element.34), calls=%async_computation.1 | async-start | bytes 4456448 | tf_op jit(solution)/shard_map/weight_grad/all_to_all | solution.py:350
  98.2 21.4 %copy-start.1 = (bf16[32,64,128]{2,1,0:T(8,128)(2,1)S(1)}, bf16[32,64,128]{2,1,0:T(8,128)(2,1)}, u32[]{:S(2)}) copy-start(bf16[32,64,128]{2,1,0:T(8,128)(2,1)} %get-tuple-element.33) | copy-start | bytes 1572868
  98.2 18.0 %collective-permute-start.12 = (bf16[32,64,128]{2,1,0:T(8,128)(2,1)}, bf16[32,64,128]{2,1,0:T(8,128)(2,1)S(1)}, u32[]{:S(2)}, u32[]{:S(2)}) collective-permute-start(bf16[32,64,128]{2,1,0:T(8,128)(2,1)} %get-tuple-element.32), channel_id=1, source_target_pairs={{0,16},{4,132},{8,56},{12,140},{16,32},{20,148},{24,8},{28,156},{3... | collective-permute-start | bytes 1572872 | tf_op jit(solution)/shard_map/reduce_far/ppermute | solution.py:35
  100.3 19.3 %copy-start = (bf16[64,64,128]{2,1,0:T(8,128)(2,1)}, bf16[64,64,128]{2,1,0:T(8,128)(2,1)S(1)}, u32[]{:S(2)}) copy-start(bf16[64,64,128]{2,1,0:T(8,128)(2,1)S(1)} %collective-permute-done.10) | copy-start | bytes 3145732
  101.9 19.2 %collective-permute-start.14 = (bf16[32,64,128]{2,1,0:T(8,128)(2,1)S(1)}, bf16[32,64,128]{2,1,0:T(8,128)(2,1)S(1)}, u32[]{:S(2)}, u32[]{:S(2)}) collective-permute-start(bf16[32,64,128]{2,1,0:T(8,128)(2,1)S(1)} %add_convert_fusion.2), channel_id=1, source_target_pairs={{0,48},{4,388},{8,24},{12,396},{16,0},{20,404},{24,40},{28,412},{3... | collective-permute-start | bytes 1572872 | tf_op jit(solution)/shard_map/reduce_far/ppermute | solution.py:35
  117.7 12.0 %collective-permute-start.13 = (bf16[32,64,128]{2,1,0:T(8,128)(2,1)S(1)}, bf16[32,64,128]{2,1,0:T(8,128)(2,1)S(1)}, u32[]{:S(2)}, u32[]{:S(2)}) collective-permute-start(bf16[32,64,128]{2,1,0:T(8,128)(2,1)S(1)} %add_convert_fusion.1), channel_id=1, source_target_pairs={{0,16},{4,132},{8,56},{12,140},{16,32},{20,148},{24,8},{28,156},{3... | collective-permute-start | bytes 1572872 | tf_op jit(solution)/shard_map/reduce_far/ppermute | solution.py:35
  130.8 15.9 %all-to-all-start.2 = ((bf16[8,256,128]{2,1,0:T(8,128)(2,1)}), bf16[8,256,128]{2,1,0:T(8,128)(2,1)S(1)}, u32[]{:S(2)}, u32[]{:S(2)}) async-start(bf16[8,256,128]{2,1,0:T(8,128)(2,1)} %bitcast.33), calls=%async_computation.2 | async-start | bytes 1048576 | tf_op jit(solution)/shard_map/reduce_near/all_to_all | solution.py:43
  134.5 3.1 %collective-permute-start.9 = (bf16[2,64,128]{2,1,0:T(8,128)(2,1)S(1)}, bf16[2,64,128]{2,1,0:T(8,128)(2,1)S(1)}, u32[]{:S(2)}, u32[]{:S(2)}) collective-permute-start(bf16[2,64,128]{2,1,0:T(8,128)(2,1)S(1)} %slice.53), channel_id=1, source_target_pairs={{0,4},{4,0},{8,12},{12,8},{16,20},{20,16},{24,28},{28,24},{32,36},... | collective-permute-start | bytes 98312 | tf_op jit(solution)/shard_map/swap_back/ppermute | solution.py:39
  146.7 3.1 %collective-permute-start.15 = (bf16[2,64,128]{2,1,0:T(8,128)(2,1)S(1)}, bf16[2,64,128]{2,1,0:T(8,128)(2,1)S(1)}, u32[]{:S(2)}, u32[]{:S(2)}) collective-permute-start(bf16[2,64,128]{2,1,0:T(8,128)(2,1)S(1)} %bitcast.39), channel_id=1, source_target_pairs={{0,4},{4,0},{8,12},{12,8},{16,20},{20,16},{24,28},{28,24},{32,36},... | collective-permute-start | bytes 98312 | tf_op jit(solution)/shard_map/swap_back/ppermute | solution.py:39

commit v8 on v5

--- a/solution.py
+++ b/solution.py
@@ -99,8 +99,10 @@
         pltpu.make_async_copy(weights_here.at[i], weights.at[i], weight_sems.at[i])
         for i in range(rows // 2)
     ]
-    for copy in loads + weight_loads:
+    for copy in loads:
         copy.start()
+    for copy in weight_loads:
+        copy.start(priority=1)
     dense[...] = jnp.zeros_like(dense)
     for copy in loads:
         copy.wait()

time: 152 us -> 151 us (level)
  no operation moved by 1% of the time
where the time goes in v8:
time: 151 us; the launch traced here: 150 us
  starting transfers between devices  68.8 us (46%)
  waiting for transfers between devices  41.1 us (27%)
  blocking collectives  16.7 us (11%)
  Pallas kernels  11.4 us (8%)
  other arithmetic  8 us (5%)
  local copies, waits for them, and re-layouts  2.96 us (2%)
    ppermute x12, starting transfers between devices, far_shift(): return lax.ppermute(value, 'blk', pairs)  40.6 us
    ppermute x12, waiting for transfers between devices, far_shift(): return lax.ppermute(value, 'blk', pairs)  31.6 us
    all_to_all x1, blocking collectives, near_exchange(): lax.all_to_all(value, 'blk', 0, 0, axis_index_groups=GROUPS_NEAR, tiled=T...  16.7 us
    ppermute x4, starting transfers between devices, swap_cores(): return lax.ppermute(value, 'blk', SWAP)  14.5 us
    all_to_all x1, starting transfers between devices, local(): lax.all_to_all(packed, BOTH, 0, 0, axis_index_groups=groups, tiled=True)  10 us
    pallas_call x1, Pallas kernels, run_blocks(): pl.pallas_call(block_kernel, in_specs=[scalars] * 2 + [outside] * 9 + [wh...  9.45 us
    all_to_all x1, waiting for transfers between devices, near_exchange(): lax.all_to_all(value, 'blk', 0, 0, axis_index_groups=GROUPS_NEAR, tiled=T...  7.03 us
    convert_element_type x3, other arithmetic, add(): return sum((value.astype(F32) for value in values)).astype(BF)  4.08 us
  transfers between devices with their start and end apart: 18, of which 10 were waited for; matrix products, arithmetic and copies ran while one was open for 6% of the time, Pallas kernels for 1%

profile of v8, /device:TPU:1, one launch (start us, length us, event | category | flops | bytes accessed | tf_op | source)
XLA Modules:
  0.0 150.1 jit_solution(1898688935029597011)
XLA Ops:
  1.5 8.8 %collective-permute-start = (bf16[2,64,256]{2,1,0:T(8,128)(2,1)S(1)}, bf16[2,64,256]{2,1,0:T(8,128)(2,1)S(1)}, u32[]{:S(2)}, u32[]{:S(2)}) collective-permute-start(bf16[2,64,256]{2,1,0:T(8,128)(2,1)S(1)} %get-tuple-element.40), channel_id=1, source_target_pairs={{0,4},{4,0},{8,12},{12,8},{16,20},{20,16},{24,28},{28,24},{32,36},... | collective-permute-start | bytes 196616 | tf_op jit(solution)/shard_map/swap_tokens/ppermute | solution.py:39
  11.5 16.7 %all_to_all.15 = bf16[8,4,64,128]{3,2,1,0:T(8,128)(2,1)} all-to-all(bf16[8,4,64,128]{3,2,1,0:T(8,128)(2,1)S(1)} %broadcast_in_dim.23), channel_id=1, replica_groups={{0,64,128,192,256,320,384,448},{8,72,136,200,264,328,392,456},{16,80,14..., dimensions={0} | all-to-all | bytes 1048576 | tf_op jit(solution)/shard_map/gather_near/all_to_all | solution.py:43
  30.1 5.9 %collective-permute-start.2 = (bf16[32,64,128]{2,1,0:T(8,128)(2,1)}, bf16[32,64,128]{2,1,0:T(8,128)(2,1)}, u32[]{:S(2)}, u32[]{:S(2)}) collective-permute-start(bf16[32,64,128]{2,1,0:T(8,128)(2,1)} %bitcast.5.refs_0_), channel_id=1, source_target_pairs={{0,48},{4,388},{8,24},{12,396},{16,0},{20,404},{24,40},{28,412},{3... | collective-permute-start | bytes 1572872 | tf_op jit(solution)/shard_map/gather_far/ppermute | solution.py:35
  36.0 1.9 %collective-permute-start.3 = (bf16[32,64,128]{2,1,0:T(8,128)(2,1)}, bf16[32,64,128]{2,1,0:T(8,128)(2,1)}, u32[]{:S(2)}, u32[]{:S(2)}) collective-permute-start(bf16[32,64,128]{2,1,0:T(8,128)(2,1)} %bitcast.5.refs_0_), channel_id=1, source_target_pairs={{0,16},{4,132},{8,56},{12,140},{16,32},{20,148},{24,8},{28,156},{3... | collective-permute-start | bytes 1572872 | tf_op jit(solution)/shard_map/gather_far/ppermute | solution.py:35
  40.7 2.8 %collective-permute-start.1 = (bf16[32,64,128]{2,1,0:T(8,128)(2,1)}, bf16[32,64,128]{2,1,0:T(8,128)(2,1)}, u32[]{:S(2)}, u32[]{:S(2)}) collective-permute-start(bf16[32,64,128]{2,1,0:T(8,128)(2,1)} %bitcast.5.refs_0_), channel_id=1, source_target_pairs={{0,8},{4,68},{8,0},{12,76},{16,24},{20,84},{24,16},{28,92},{32,40}... | collective-permute-start | bytes 1572872 | tf_op jit(solution)/shard_map/gather_far/ppermute | solution.py:35
  43.5 4.6 %collective-permute-done.2.refs_2_ = bf16[32,64,128]{2,1,0:T(8,128)(2,1)} collective-permute-done((bf16[32,64,128]{2,1,0:T(8,128)(2,1)}, bf16[32,64,128]{2,1,0:T(8,128)(2,1)}, u32[]{:S(2)}, u32[]{:S(2)}) %collective-permute-start.2) | collective-permute-done | bytes 524320 | tf_op jit(solution)/shard_map/gather_far/ppermute | solution.py:35
  50.1 2.4 %collective-permute-start.6 = (bf16[32,64,128]{2,1,0:T(8,128)(2,1)}, bf16[32,64,128]{2,1,0:T(8,128)(2,1)}, u32[]{:S(2)}, u32[]{:S(2)}) collective-permute-start(bf16[32,64,128]{2,1,0:T(8,128)(2,1)} %collective-permute-done.3.refs_6_), channel_id=1, source_target_pairs={{0,16},{4,132},{8,56},{12,140},{16,32},{20,148},{24,8},{28,156},{3... | collective-permute-start | bytes 1572872 | tf_op jit(solution)/shard_map/gather_far/ppermute | solution.py:35
  52.5 5.2 %collective-permute-start.5 = (bf16[32,64,128]{2,1,0:T(8,128)(2,1)}, bf16[32,64,128]{2,1,0:T(8,128)(2,1)}, u32[]{:S(2)}, u32[]{:S(2)}) collective-permute-start(bf16[32,64,128]{2,1,0:T(8,128)(2,1)} %collective-permute-done.3.refs_6_), channel_id=1, source_target_pairs={{0,8},{4,68},{8,0},{12,76},{16,24},{20,84},{24,16},{28,92},{32,40}... | collective-permute-start | bytes 1572872 | tf_op jit(solution)/shard_map/gather_far/ppermute | solution.py:35
  57.7 3.8 %collective-permute-start.8 = (bf16[32,64,128]{2,1,0:T(8,128)(2,1)}, bf16[32,64,128]{2,1,0:T(8,128)(2,1)}, u32[]{:S(2)}, u32[]{:S(2)}) collective-permute-start(bf16[32,64,128]{2,1,0:T(8,128)(2,1)} %bitcast.5.refs_0_), channel_id=1, source_target_pairs={{0,56},{4,452},{8,16},{12,460},{16,8},{20,468},{24,32},{28,476},{3... | collective-permute-start | bytes 1572872 | tf_op jit(solution)/shard_map/gather_far/ppermute | solution.py:35
  61.6 3.8 %collective-permute-done.7.refs_5_ = bf16[32,64,128]{2,1,0:T(8,128)(2,1)} collective-permute-done((bf16[32,64,128]{2,1,0:T(8,128)(2,1)}, bf16[32,64,128]{2,1,0:T(8,128)(2,1)}, u32[]{:S(2)}, u32[]{:S(2)}) %collective-permute-start.7) | collective-permute-done | bytes 524320 | tf_op jit(solution)/shard_map/gather_far/ppermute | solution.py:35
  65.4 5.6 %collective-permute-done.8.refs_7_ = bf16[32,64,128]{2,1,0:T(8,128)(2,1)} collective-permute-done((bf16[32,64,128]{2,1,0:T(8,128)(2,1)}, bf16[32,64,128]{2,1,0:T(8,128)(2,1)}, u32[]{:S(2)}, u32[]{:S(2)}) %collective-permute-start.8) | collective-permute-done | bytes 524320 | tf_op jit(solution)/shard_map/gather_far/ppermute | solution.py:35
  71.0 9.5 %blocks.1 = (bf16[4,64,128]{2,1,0:T(8,128)(2,1)S(1)}, bf16[32,64,128]{2,1,0:T(8,128)(2,1)}, bf16[64,64,128]{2,1,0:T(8,128)(2,1)}, bf16[64,64,128]{2,1,0:T(8,128)...) custom-call(s32[1]{0:T(128)} %bitcast.core, ...), custom_call_target="tpu_custom_call" | custom-call | flops 872415232 | bytes 15204352 | tf_op jit(solution)/shard_map/blocks/pallas_call | solution.py:202
  82.4 5.3 %collective-permute-start.11 = (bf16[64,64,128]{2,1,0:T(8,128)(2,1)}, bf16[64,64,128]{2,1,0:T(8,128)(2,1)}, u32[]{:S(2)}, u32[]{:S(2)}) collective-permute-start(bf16[64,64,128]{2,1,0:T(8,128)(2,1)} %get-tuple-element.31), channel_id=1, source_target_pairs={{0,56},{4,452},{8,16},{12,460},{16,8},{20,468},{24,32},{28,476},{3... | collective-permute-start | bytes 3145736 | tf_op jit(solution)/shard_map/reduce_far/ppermute | solution.py:35
  87.7 10.0 %all-to-all-start.1 = ((bf16[8,1088,128]{2,1,0:T(8,128)(2,1)}), bf16[8,1088,128]{2,1,0:T(8,128)(2,1)S(1)}, u32[]{:S(2)}, u32[]{:S(2)}) async-start(bf16[8,1088,128]{2,1,0:T(8,128)(2,1)} %get-tuple-element.34), calls=%async_computation.1 | async-start | bytes 4456448 | tf_op jit(solution)/shard_map/weight_grad/all_to_all | solution.py:353
  97.8 2.0 %collective-permute-start.12 = (bf16[32,64,128]{2,1,0:T(8,128)(2,1)}, bf16[32,64,128]{2,1,0:T(8,128)(2,1)S(1)}, u32[]{:S(2)}, u32[]{:S(2)}) collective-permute-start(bf16[32,64,128]{2,1,0:T(8,128)(2,1)} %get-tuple-element.32), channel_id=1, source_target_pairs={{0,16},{4,132},{8,56},{12,140},{16,32},{20,148},{24,8},{28,156},{3... | collective-permute-start | bytes 1572872 | tf_op jit(solution)/shard_map/reduce_far/ppermute | solution.py:35
  101.4 5.5 %collective-permute-start.14 = (bf16[32,64,128]{2,1,0:T(8,128)(2,1)S(1)}, bf16[32,64,128]{2,1,0:T(8,128)(2,1)S(1)}, u32[]{:S(2)}, u32[]{:S(2)}) collective-permute-start(bf16[32,64,128]{2,1,0:T(8,128)(2,1)S(1)} %add_convert_fusion.2), channel_id=1, source_target_pairs={{0,48},{4,388},{8,24},{12,396},{16,0},{20,404},{24,40},{28,412},{3... | collective-permute-start | bytes 1572872 | tf_op jit(solution)/shard_map/reduce_far/ppermute | solution.py:35
  106.9 8.8 %collective-permute-done.12 = bf16[32,64,128]{2,1,0:T(8,128)(2,1)S(1)} collective-permute-done((bf16[32,64,128]{2,1,0:T(8,128)(2,1)}, bf16[32,64,128]{2,1,0:T(8,128)(2,1)S(1)}, u32[]{:S(2)}, u32[]{:S(2)}) %collective-permute-start.12) | collective-permute-done | bytes 524320 | tf_op jit(solution)/shard_map/reduce_far/ppermute | solution.py:35
  117.2 1.9 %collective-permute-start.13 = (bf16[32,64,128]{2,1,0:T(8,128)(2,1)S(1)}, bf16[32,64,128]{2,1,0:T(8,128)(2,1)S(1)}, u32[]{:S(2)}, u32[]{:S(2)}) collective-permute-start(bf16[32,64,128]{2,1,0:T(8,128)(2,1)S(1)} %add_convert_fusion.1), channel_id=1, source_target_pairs={{0,16},{4,132},{8,56},{12,140},{16,32},{20,148},{24,8},{28,156},{3... | collective-permute-start | bytes 1572872 | tf_op jit(solution)/shard_map/reduce_far/ppermute | solution.py:35
  120.6 8.6 %collective-permute-done.13 = bf16[32,64,128]{2,1,0:T(8,128)(2,1)S(1)} collective-permute-done((bf16[32,64,128]{2,1,0:T(8,128)(2,1)S(1)}, bf16[32,64,128]{2,1,0:T(8,128)(2,1)S(1)}, u32[]{:S(2)}, u32[]{:S(2)}) %collective-permute-start.13) | collective-permute-done | bytes 524320 | tf_op jit(solution)/shard_map/reduce_far/ppermute | solution.py:35
  130.3 3.7 %all-to-all-start.2 = ((bf16[8,256,128]{2,1,0:T(8,128)(2,1)}), bf16[8,256,128]{2,1,0:T(8,128)(2,1)S(1)}, u32[]{:S(2)}, u32[]{:S(2)}) async-start(bf16[8,256,128]{2,1,0:T(8,128)(2,1)} %bitcast.39), calls=%async_computation.2 | async-start | bytes 1048576 | tf_op jit(solution)/shard_map/reduce_near/all_to_all | solution.py:43
  134.0 1.9 %collective-permute-start.9 = (bf16[2,64,128]{2,1,0:T(8,128)(2,1)S(1)}, bf16[2,64,128]{2,1,0:T(8,128)(2,1)S(1)}, u32[]{:S(2)}, u32[]{:S(2)}) collective-permute-start(bf16[2,64,128]{2,1,0:T(8,128)(2,1)S(1)} %slice.53), channel_id=1, source_target_pairs={{0,4},{4,0},{8,12},{12,8},{16,20},{20,16},{24,28},{28,24},{32,36},... | collective-permute-start | bytes 98312 | tf_op jit(solution)/shard_map/swap_back/ppermute | solution.py:39
  137.1 2.0 %reduce_near.1 = bf16[2,26,32,256]{3,2,1,0:T(8,128)(2,1)} custom-call(bf16[8,1088,128]{2,1,0:T(8,128)(2,1)S(1)} %all-to-all-done.1.refs_0_), custom_call_target="tpu_custom_call" | custom-call | flops 872415232 | bytes 3080192 | tf_op jit(solution)/shard_map/reduce_near/pallas_call | solution.py:265
  139.1 7.0 %all-to-all-done.2 = bf16[8,256,128]{2,1,0:T(8,128)(2,1)S(1)} async-done(((bf16[8,256,128]{2,1,0:T(8,128)(2,1)}), bf16[8,256,128]{2,1,0:T(8,128)(2,1)S(1)}, u32[]{:S(2)}, u32[]{:S(2)}) %all-to-all-start.2) | async-done | bytes 524320 | tf_op jit(solution)/shard_map/reduce_near/all_to_all | solution.py:43
  146.2 1.9 %collective-permute-start.15 = (bf16[2,64,128]{2,1,0:T(8,128)(2,1)S(1)}, bf16[2,64,128]{2,1,0:T(8,128)(2,1)S(1)}, u32[]{:S(2)}, u32[]{:S(2)}) collective-permute-start(bf16[2,64,128]{2,1,0:T(8,128)(2,1)S(1)} %bitcast.49), channel_id=1, source_target_pairs={{0,4},{4,0},{8,12},{12,8},{16,20},{20,16},{24,28},{28,24},{32,36},... | collective-permute-start | bytes 98312 | tf_op jit(solution)/shard_map/swap_back/ppermute | solution.py:39
  (55 shorter events, 19.3 us)
Async XLA Ops:
  1.5 9.7 %collective-permute-start = (bf16[2,64,256]{2,1,0:T(8,128)(2,1)S(1)}, bf16[2,64,256]{2,1,0:T(8,128)(2,1)S(1)}, u32[]{:S(2)}, u32[]{:S(2)}) collective-permute-start(bf16[2,64,256]{2,1,0:T(8,128)(2,1)S(1)} %get-tuple-element.40), channel_id=1, source_target_pairs={{0,4},{4,0},{8,12},{12,8},{16,20},{20,16},{24,28},{28,24},{32,36},... | collective-permute-start | bytes 196616 | tf_op jit(solution)/shard_map/swap_tokens/ppermute | solution.py:39
  28.2 21.9 %collective-permute-start.4 = (bf16[2,26,128,256]{3,2,1,0:T(8,128)(2,1)}, bf16[2,26,128,256]{3,2,1,0:T(8,128)(2,1)S(1)}, u32[]{:S(2)}, u32[]{:S(2)}) collective-permute-start(bf16[2,26,128,256]{3,2,1,0:T(8,128)(2,1)} %param.6), channel_id=1, source_target_pairs={{0,4},{4,0},{8,12},{12,8},{16,20},{20,16},{24,28},{28,24},{32,36},... | collective-permute-start | bytes 10223624 | tf_op jit(solution)/shard_map/gather_far/ppermute | solution.py:39
  30.1 17.9 %collective-permute-start.2 = (bf16[32,64,128]{2,1,0:T(8,128)(2,1)}, bf16[32,64,128]{2,1,0:T(8,128)(2,1)}, u32[]{:S(2)}, u32[]{:S(2)}) collective-permute-start(bf16[32,64,128]{2,1,0:T(8,128)(2,1)} %bitcast.5.refs_0_), channel_id=1, source_target_pairs={{0,48},{4,388},{8,24},{12,396},{16,0},{20,404},{24,40},{28,412},{3... | collective-permute-start | bytes 1572872 | tf_op jit(solution)/shard_map/gather_far/ppermute | solution.py:35
  36.0 14.1 %collective-permute-start.3 = (bf16[32,64,128]{2,1,0:T(8,128)(2,1)}, bf16[32,64,128]{2,1,0:T(8,128)(2,1)}, u32[]{:S(2)}, u32[]{:S(2)}) collective-permute-start(bf16[32,64,128]{2,1,0:T(8,128)(2,1)} %bitcast.5.refs_0_), channel_id=1, source_target_pairs={{0,16},{4,132},{8,56},{12,140},{16,32},{20,148},{24,8},{28,156},{3... | collective-permute-start | bytes 1572872 | tf_op jit(solution)/shard_map/gather_far/ppermute | solution.py:35
  40.7 21.0 %collective-permute-start.1 = (bf16[32,64,128]{2,1,0:T(8,128)(2,1)}, bf16[32,64,128]{2,1,0:T(8,128)(2,1)}, u32[]{:S(2)}, u32[]{:S(2)}) collective-permute-start(bf16[32,64,128]{2,1,0:T(8,128)(2,1)} %bitcast.5.refs_0_), channel_id=1, source_target_pairs={{0,8},{4,68},{8,0},{12,76},{16,24},{20,84},{24,16},{28,92},{32,40}... | collective-permute-start | bytes 1572872 | tf_op jit(solution)/shard_map/gather_far/ppermute | solution.py:35
  48.1 17.4 %collective-permute-start.7 = (bf16[32,64,128]{2,1,0:T(8,128)(2,1)}, bf16[32,64,128]{2,1,0:T(8,128)(2,1)}, u32[]{:S(2)}, u32[]{:S(2)}) collective-permute-start(bf16[32,64,128]{2,1,0:T(8,128)(2,1)} %collective-permute-done.2.refs_2_), channel_id=1, source_target_pairs={{0,56},{4,452},{8,16},{12,460},{16,8},{20,468},{24,32},{28,476},{3... | collective-permute-start | bytes 1572872 | tf_op jit(solution)/shard_map/gather_far/ppermute | solution.py:35
  50.1 20.9 %collective-permute-start.6 = (bf16[32,64,128]{2,1,0:T(8,128)(2,1)}, bf16[32,64,128]{2,1,0:T(8,128)(2,1)}, u32[]{:S(2)}, u32[]{:S(2)}) collective-permute-start(bf16[32,64,128]{2,1,0:T(8,128)(2,1)} %collective-permute-done.3.refs_6_), channel_id=1, source_target_pairs={{0,16},{4,132},{8,56},{12,140},{16,32},{20,148},{24,8},{28,156},{3... | collective-permute-start | bytes 1572872 | tf_op jit(solution)/shard_map/gather_far/ppermute | solution.py:35
  52.5 18.5 %collective-permute-start.5 = (bf16[32,64,128]{2,1,0:T(8,128)(2,1)}, bf16[32,64,128]{2,1,0:T(8,128)(2,1)}, u32[]{:S(2)}, u32[]{:S(2)}) collective-permute-start(bf16[32,64,128]{2,1,0:T(8,128)(2,1)} %collective-permute-done.3.refs_6_), channel_id=1, source_target_pairs={{0,8},{4,68},{8,0},{12,76},{16,24},{20,84},{24,16},{28,92},{32,40}... | collective-permute-start | bytes 1572872 | tf_op jit(solution)/shard_map/gather_far/ppermute | solution.py:35
  57.7 13.4 %collective-permute-start.8 = (bf16[32,64,128]{2,1,0:T(8,128)(2,1)}, bf16[32,64,128]{2,1,0:T(8,128)(2,1)}, u32[]{:S(2)}, u32[]{:S(2)}) collective-permute-start(bf16[32,64,128]{2,1,0:T(8,128)(2,1)} %bitcast.5.refs_0_), channel_id=1, source_target_pairs={{0,56},{4,452},{8,16},{12,460},{16,8},{20,468},{24,32},{28,476},{3... | collective-permute-start | bytes 1572872 | tf_op jit(solution)/shard_map/gather_far/ppermute | solution.py:35
  80.5 19.3 %collective-permute-start.10 = (bf16[64,64,128]{2,1,0:T(8,128)(2,1)}, bf16[64,64,128]{2,1,0:T(8,128)(2,1)S(1)}, u32[]{:S(2)}, u32[]{:S(2)}) collective-permute-start(bf16[64,64,128]{2,1,0:T(8,128)(2,1)} %get-tuple-element.29), channel_id=1, source_target_pairs={{0,8},{4,68},{8,0},{12,76},{16,24},{20,84},{24,16},{28,92},{32,40}... | collective-permute-start | bytes 3145736 | tf_op jit(solution)/shard_map/reduce_far/ppermute | solution.py:35
  82.4 33.3 %collective-permute-start.11 = (bf16[64,64,128]{2,1,0:T(8,128)(2,1)}, bf16[64,64,128]{2,1,0:T(8,128)(2,1)}, u32[]{:S(2)}, u32[]{:S(2)}) collective-permute-start(bf16[64,64,128]{2,1,0:T(8,128)(2,1)} %get-tuple-element.31), channel_id=1, source_target_pairs={{0,56},{4,452},{8,16},{12,460},{16,8},{20,468},{24,32},{28,476},{3... | collective-permute-start | bytes 3145736 | tf_op jit(solution)/shard_map/reduce_far/ppermute | solution.py:35
  87.7 42.5 %all-to-all-start.1 = ((bf16[8,1088,128]{2,1,0:T(8,128)(2,1)}), bf16[8,1088,128]{2,1,0:T(8,128)(2,1)S(1)}, u32[]{:S(2)}, u32[]{:S(2)}) async-start(bf16[8,1088,128]{2,1,0:T(8,128)(2,1)} %get-tuple-element.34), calls=%async_computation.1 | async-start | bytes 4456448 | tf_op jit(solution)/shard_map/weight_grad/all_to_all | solution.py:353
  97.8 21.4 %copy-start.1 = (bf16[32,64,128]{2,1,0:T(8,128)(2,1)S(1)}, bf16[32,64,128]{2,1,0:T(8,128)(2,1)}, u32[]{:S(2)}) copy-start(bf16[32,64,128]{2,1,0:T(8,128)(2,1)} %get-tuple-element.33) | copy-start | bytes 1572868
  97.8 18.0 %collective-permute-start.12 = (bf16[32,64,128]{2,1,0:T(8,128)(2,1)}, bf16[32,64,128]{2,1,0:T(8,128)(2,1)S(1)}, u32[]{:S(2)}, u32[]{:S(2)}) collective-permute-start(bf16[32,64,128]{2,1,0:T(8,128)(2,1)} %get-tuple-element.32), channel_id=1, source_target_pairs={{0,16},{4,132},{8,56},{12,140},{16,32},{20,148},{24,8},{28,156},{3... | collective-permute-start | bytes 1572872 | tf_op jit(solution)/shard_map/reduce_far/ppermute | solution.py:35
  99.8 19.3 %copy-start = (bf16[64,64,128]{2,1,0:T(8,128)(2,1)}, bf16[64,64,128]{2,1,0:T(8,128)(2,1)S(1)}, u32[]{:S(2)}) copy-start(bf16[64,64,128]{2,1,0:T(8,128)(2,1)S(1)} %collective-permute-done.10) | copy-start | bytes 3145732
  101.4 19.2 %collective-permute-start.14 = (bf16[32,64,128]{2,1,0:T(8,128)(2,1)S(1)}, bf16[32,64,128]{2,1,0:T(8,128)(2,1)S(1)}, u32[]{:S(2)}, u32[]{:S(2)}) collective-permute-start(bf16[32,64,128]{2,1,0:T(8,128)(2,1)S(1)} %add_convert_fusion.2), channel_id=1, source_target_pairs={{0,48},{4,388},{8,24},{12,396},{16,0},{20,404},{24,40},{28,412},{3... | collective-permute-start | bytes 1572872 | tf_op jit(solution)/shard_map/reduce_far/ppermute | solution.py:35
  117.2 12.0 %collective-permute-start.13 = (bf16[32,64,128]{2,1,0:T(8,128)(2,1)S(1)}, bf16[32,64,128]{2,1,0:T(8,128)(2,1)S(1)}, u32[]{:S(2)}, u32[]{:S(2)}) collective-permute-start(bf16[32,64,128]{2,1,0:T(8,128)(2,1)S(1)} %add_convert_fusion.1), channel_id=1, source_target_pairs={{0,16},{4,132},{8,56},{12,140},{16,32},{20,148},{24,8},{28,156},{3... | collective-permute-start | bytes 1572872 | tf_op jit(solution)/shard_map/reduce_far/ppermute | solution.py:35
  130.3 15.8 %all-to-all-start.2 = ((bf16[8,256,128]{2,1,0:T(8,128)(2,1)}), bf16[8,256,128]{2,1,0:T(8,128)(2,1)S(1)}, u32[]{:S(2)}, u32[]{:S(2)}) async-start(bf16[8,256,128]{2,1,0:T(8,128)(2,1)} %bitcast.39), calls=%async_computation.2 | async-start | bytes 1048576 | tf_op jit(solution)/shard_map/reduce_near/all_to_all | solution.py:43
  134.0 3.1 %collective-permute-start.9 = (bf16[2,64,128]{2,1,0:T(8,128)(2,1)S(1)}, bf16[2,64,128]{2,1,0:T(8,128)(2,1)S(1)}, u32[]{:S(2)}, u32[]{:S(2)}) collective-permute-start(bf16[2,64,128]{2,1,0:T(8,128)(2,1)S(1)} %slice.53), channel_id=1, source_target_pairs={{0,4},{4,0},{8,12},{12,8},{16,20},{20,16},{24,28},{28,24},{32,36},... | collective-permute-start | bytes 98312 | tf_op jit(solution)/shard_map/swap_back/ppermute | solution.py:39
  146.2 3.1 %collective-permute-start.15 = (bf16[2,64,128]{2,1,0:T(8,128)(2,1)S(1)}, bf16[2,64,128]{2,1,0:T(8,128)(2,1)S(1)}, u32[]{:S(2)}, u32[]{:S(2)}) collective-permute-start(bf16[2,64,128]{2,1,0:T(8,128)(2,1)S(1)} %bitcast.49), channel_id=1, source_target_pairs={{0,4},{4,0},{8,12},{12,8},{16,20},{20,16},{24,28},{28,24},{32,36},... | collective-permute-start | bytes 98312 | tf_op jit(solution)/shard_map/swap_back/ppermute | solution.py:39
